TPU v7x, 32 devices: a whole 2x2x4 slice. The times are simulated.
32 devices in a mesh: dp: 4 (over x, core), tensor: 8 (over z, y).
Axes of the slice: x: 2, y: 2, z: 4, core: 2. Of those that a mesh axis runs over, the one named last changes fastest.
Arguments:
- tokens: bfloat16 [2, 12288, 1024], P(None, ('dp', 'tensor')), may hold values from -6 to 6
- segment_ids: int32 [2, 4, 3072], P(None, 'dp'), may hold values from 0 to 3, never falling along the last dimension, each value on 1 to 1370 neighbouring positions
- out_grad: bfloat16 [2, 12288, 1024], P(None, ('dp', 'tensor')), may hold values from -6 to 6
- norm1_gain: bfloat16 [1024], P('dp'), may hold values from 0.25 to 1.75
- norm1_bias: bfloat16 [1024], P('dp'), may hold values from -3 to 3
- qkv_weight: bfloat16 [3, 1024, 1024], P(None, 'dp', 'tensor'), may hold values from -0.25 to 0.25
- qv_bias: bfloat16 [2, 1024], P(None, ('tensor', 'dp')), may hold values from -3 to 3
- proj_weight: bfloat16 [1024, 1024], P('tensor', 'dp'), may hold values from -1 to 1
- proj_bias: bfloat16 [1024], P('dp'), may hold values from -3 to 3
- scale1: bfloat16 [1024], P('dp'), may hold values from 0.25 to 1.75
- norm2_gain: bfloat16 [1024], P('dp'), may hold values from 0.25 to 1.75
- norm2_bias: bfloat16 [1024], P('dp'), may hold values from -3 to 3
- fc1_weight: bfloat16 [1024, 4096], P('dp', 'tensor'), may hold values from -0.1875 to 0.1875
- fc1_bias: bfloat16 [4096], P(('tensor', 'dp')), may hold values from -3 to 3
- fc2_weight: bfloat16 [4096, 1024], P('tensor', 'dp'), may hold values from -0.09375 to 0.09375
- fc2_bias: bfloat16 [1024], P('dp'), may hold values from -3 to 3
- scale2: bfloat16 [1024], P('dp'), may hold values from 0.25 to 1.75
Outputs:
- block_out: bfloat16 [2, 12288, 1024], P(None, ('dp', 'tensor'))
- tokens_grad: bfloat16 [2, 12288, 1024], P(None, ('dp', 'tensor'))
- grad_norm1_gain: float32 [1024], P('dp')
- grad_norm1_bias: float32 [1024], P('dp')
- grad_qkv_weight: float32 [3, 1024, 1024], P(None, 'dp', 'tensor')
- grad_qv_bias: float32 [2, 1024], P(None, ('tensor', 'dp'))
- grad_proj_weight: float32 [1024, 1024], P('tensor', 'dp')
- grad_proj_bias: float32 [1024], P('dp')
- grad_scale1: float32 [1024], P('dp')
- grad_norm2_gain: float32 [1024], P('dp')
- grad_norm2_bias: float32 [1024], P('dp')
- grad_fc1_weight: float32 [1024, 4096], P('dp', 'tensor')
- grad_fc1_bias: float32 [4096], P(('tensor', 'dp'))
- grad_fc2_weight: float32 [4096, 1024], P('tensor', 'dp')
- grad_fc2_bias: float32 [1024], P('dp')
- grad_scale2: float32 [1024], P('dp')
Inputs may be any that keep to these rules, and one draw needn't show every extreme that they name: `segment_ids`: along each run the image number never falls; each image is a run of 1 to 1370 tokens, and some image has exactly 1370.
All inputs are finite; a program needn't handle non-finite values.
Results may differ from a plain program's by a relative error of at most 0.023.
Values may be sent and summed in bfloat16 or wider, within the bound.
A program may use at most 192 MiB of HBM per device.

v0:
```python
import jax
import jax.numpy as jnp
from jax import lax
from jax.experimental import pallas as pl
from jax.experimental.pallas import tpu as pltpu
from jax.sharding import PartitionSpec as P

HEAD_DIM = 64

norm_eps = 1e-06
mask_fill = -1e30
query_rows = 512
key_rows = 512
contract_rows = (((0,), (0,)), ((), ()))
contract_cols = (((1,), (1,)), ((), ()))
everywhere = ("dp", "tensor")


def dot_f32(left, right, dims=(((1,), (0,)), ((), ()))):
    return lax.dot_general(left, right, dims, preferred_element_type=jnp.float32)


def norm_parts(values):
    center = values - jnp.mean(values, axis=-1, keepdims=True)
    rate = lax.rsqrt(jnp.mean(center * center, axis=-1, keepdims=True) + norm_eps)
    return center * rate, rate


def norm_back(normed, rate, gain, grad):
    scaled = gain * grad
    average = jnp.mean(scaled, axis=-1, keepdims=True)
    along = jnp.mean(scaled * normed, axis=-1, keepdims=True)
    return rate * (scaled - average - normed * along)


def head_part(rows, head):
    lane = lax.broadcasted_iota(jnp.int32, rows.shape, 1)
    return jnp.where(lane // HEAD_DIM == head, rows, jnp.zeros_like(rows))


def forward_kernel(low_ref, high_ref, q_ref, k_ref, v_ref, idq_ref, idk_ref, out_ref, lse_ref):
    batch, block = pl.program_id(0), pl.program_id(1)
    queries = q_ref[0]
    heads = queries.shape[1] // HEAD_DIM
    rows = queries.shape[0]
    parts = [head_part(queries, head) for head in range(heads)]
    ids_query = idq_ref[0]

    def step(index, carry):
        start = pl.multiple_of(index * key_rows, key_rows)
        keys = k_ref[0, pl.ds(start, key_rows), :]
        values = v_ref[0, pl.ds(start, key_rows), :].T
        same = idk_ref[0, pl.ds(start, key_rows), :] == ids_query
        result = []
        for head in range(heads):
            top, total, acc = carry[head]
            scores = jnp.where(same, dot_f32(keys, parts[head], contract_cols), mask_fill)
            new_top = jnp.maximum(top, jnp.max(scores, axis=0, keepdims=True))
            expon = jnp.exp(scores - new_top)
            shrink = jnp.exp(top - new_top)
            total = shrink * total + jnp.sum(expon, axis=0, keepdims=True)
            mine = values[head * HEAD_DIM : (head + 1) * HEAD_DIM]
            acc = shrink * acc + dot_f32(mine, expon.astype(jnp.bfloat16))
            result.append((new_top, total, acc))
        return tuple(result)

    start_carry = tuple(
        (
            jnp.full((1, rows), mask_fill, jnp.float32),
            jnp.zeros((1, rows), jnp.float32),
            jnp.zeros((HEAD_DIM, rows), jnp.float32),
        )
        for _ in range(heads)
    )
    final = lax.fori_loop(low_ref[batch, block], high_ref[batch, block], step, start_carry)
    merged = jnp.concatenate([acc / total for _, total, acc in final], axis=0)
    out_ref[0] = merged.T.astype(out_ref.dtype)
    lse_ref[0, 0] = jnp.concatenate([top + jnp.log(total) for top, total, _ in final], axis=0)


def backward_kernel(
    low_ref, high_ref, q_ref, k_ref, v_ref, idq_ref, idk_ref, att_ref, d_att_ref, lse_ref,
    dq_ref, dk_ref, dv_ref, dk_sum, dv_sum,
):
    batch, block = pl.program_id(0), pl.program_id(1)

    @pl.when(block == 0)
    def _():
        dk_sum[...] = jnp.zeros_like(dk_sum)
        dv_sum[...] = jnp.zeros_like(dv_sum)

    queries, d_att = q_ref[0], d_att_ref[0]
    heads = queries.shape[1] // HEAD_DIM
    rows = queries.shape[0]
    parts = [head_part(queries, head) for head in range(heads)]
    d_parts = [head_part(d_att, head) for head in range(heads)]
    ids_query = idq_ref[0]
    products = (att_ref[0].astype(jnp.float32) * d_att.astype(jnp.float32)).T
    inner = [
        jnp.sum(products[head * HEAD_DIM : (head + 1) * HEAD_DIM], axis=0, keepdims=True)
        for head in range(heads)
    ]
    lse = lse_ref[0, 0]

    def step(index, carry):
        start = pl.multiple_of(index * key_rows, key_rows)
        here = pl.ds(start, key_rows)
        keys, values = k_ref[0, here, :], v_ref[0, here, :]
        keys_turned = keys.T
        same = idk_ref[0, here, :] == ids_query
        result = []
        d_value, d_key = dv_sum[here, :], dk_sum[here, :]
        for head in range(heads):
            scores = jnp.where(same, dot_f32(keys, parts[head], contract_cols), mask_fill)
            probs = jnp.exp(scores - lse[head : head + 1])
            d_probs = dot_f32(values, d_parts[head], contract_cols)
            d_scores = (probs * (d_probs - inner[head])).astype(jnp.bfloat16)
            d_value = d_value + dot_f32(probs.astype(jnp.bfloat16), d_parts[head])
            d_key = d_key + dot_f32(d_scores, parts[head])
            mine = keys_turned[head * HEAD_DIM : (head + 1) * HEAD_DIM]
            result.append(carry[head] + dot_f32(mine, d_scores))
        dv_sum[here, :] = d_value
        dk_sum[here, :] = d_key
        return tuple(result)

    empty = tuple(jnp.zeros((HEAD_DIM, rows), jnp.float32) for _ in range(heads))
    final = lax.fori_loop(low_ref[batch, block], high_ref[batch, block], step, empty)
    dq_ref[0] = (jnp.concatenate(final, axis=0).T * 0.125).astype(dq_ref.dtype)

    @pl.when(block == pl.num_programs(1) - 1)
    def _():
        dk_ref[0] = dk_sum[...].astype(dk_ref.dtype)
        dv_ref[0] = dv_sum[...].astype(dv_ref.dtype)


def attention_inputs(qkv):
    cols = qkv.shape[2] // 3
    if cols % 128 == 0:
        return qkv, qkv, qkv
    return qkv[..., :cols], qkv[..., cols : 2 * cols], qkv[..., 2 * cols :]


def attention_specs(tok_count, cols):
    spot_k, spot_v = (1, 2) if cols % 128 == 0 else (0, 0)
    q_spec = pl.BlockSpec((1, query_rows, cols), lambda b, i, *_: (b, i, 0))
    k_spec = pl.BlockSpec((1, tok_count, cols), lambda b, i, *_: (b, 0, spot_k))
    v_spec = pl.BlockSpec((1, tok_count, cols), lambda b, i, *_: (b, 0, spot_v))
    whole = pl.BlockSpec((1, tok_count, cols), lambda b, i, *_: (b, 0, 0))
    idq_spec = pl.BlockSpec((1, 1, query_rows), lambda b, i, *_: (b, 0, i))
    idk_spec = pl.BlockSpec((1, tok_count, 1), lambda b, i, *_: (b, 0, 0))
    lse_spec = pl.BlockSpec(
        (1, 1, cols // HEAD_DIM, query_rows), lambda b, i, *_: (b, i, 0, 0)
    )
    return q_spec, k_spec, v_spec, whole, idq_spec, idk_spec, lse_spec


def attention(qkv, bounds, ids_row, ids_col):
    batches, tok_count, cols3 = qkv.shape
    cols = cols3 // 3
    blocks = tok_count // query_rows
    q_spec, k_spec, v_spec, _, idq_spec, idk_spec, lse_spec = attention_specs(
        tok_count, cols
    )
    pairs = batches * tok_count * tok_count // 2
    return pl.pallas_call(
        forward_kernel,
        grid_spec=pltpu.PrefetchScalarGridSpec(
            num_scalar_prefetch=2,
            grid=(batches, blocks),
            in_specs=[q_spec, k_spec, v_spec, idq_spec, idk_spec],
            out_specs=[q_spec, lse_spec],
        ),
        out_shape=[
            jax.ShapeDtypeStruct((batches, tok_count, cols), jnp.bfloat16),
            jax.ShapeDtypeStruct(
                (batches, blocks, cols // HEAD_DIM, query_rows), jnp.float32
            ),
        ],
        compiler_params=pltpu.CompilerParams(vmem_limit_bytes=40 * 1024 * 1024),
        cost_estimate=pl.CostEstimate(
            flops=pairs * 16 * cols, bytes_accessed=2 * qkv.size, transcendentals=2 * pairs
        ),
    )(*bounds, *attention_inputs(qkv), ids_row, ids_col)


def attention_back(qkv, bounds, ids_row, ids_col, att, d_att, lse):
    batches, tok_count, cols3 = qkv.shape
    cols = cols3 // 3
    blocks = tok_count // query_rows
    q_spec, k_spec, v_spec, whole, idq_spec, idk_spec, lse_spec = attention_specs(
        tok_count, cols
    )
    pairs = batches * tok_count * tok_count // 2
    one = jax.ShapeDtypeStruct((batches, tok_count, cols), jnp.bfloat16)
    return pl.pallas_call(
        backward_kernel,
        grid_spec=pltpu.PrefetchScalarGridSpec(
            num_scalar_prefetch=2,
            grid=(batches, blocks),
            in_specs=[q_spec, k_spec, v_spec, idq_spec, idk_spec, q_spec, q_spec, lse_spec],
            out_specs=[q_spec, whole, whole],
            scratch_shapes=[
                pltpu.VMEM((tok_count, cols), jnp.float32),
                pltpu.VMEM((tok_count, cols), jnp.float32),
            ],
        ),
        out_shape=[one, one, one],
        compiler_params=pltpu.CompilerParams(vmem_limit_bytes=48 * 1024 * 1024),
        cost_estimate=pl.CostEstimate(
            flops=pairs * 40 * cols, bytes_accessed=4 * qkv.size, transcendentals=2 * pairs
        ),
    )(*bounds, *attention_inputs(qkv), ids_row, ids_col, att, d_att, lse)


def gather_matrix(shard):
    parts = lax.all_gather(shard, everywhere, axis=0, tiled=False)
    parts = parts.reshape(lax.axis_size("dp"), -1, shard.shape[1])
    return jnp.moveaxis(parts, 0, 1).reshape(parts.shape[1], -1)


def scatter_matrix(grad):
    part = lax.psum_scatter(grad.astype(jnp.bfloat16), "dp", scatter_dimension=0, tiled=True)
    return lax.psum_scatter(part, "tensor", scatter_dimension=1, tiled=True).astype(jnp.float32)


def body(
    tokens,
    segment_ids,
    out_grad,
    norm1_gain,
    norm1_bias,
    qkv_weight,
    qv_bias,
    proj_weight,
    proj_bias,
    scale1,
    norm2_gain,
    norm2_bias,
    fc1_weight,
    fc1_bias,
    fc2_weight,
    fc2_bias,
    scale2,
):
    tensor_count = lax.axis_size("tensor")
    dp_count = lax.axis_size("dp")
    batches, rows_here, width = tokens.shape
    total_rows = batches * rows_here
    tok_count = rows_here * tensor_count
    cols_here = qkv_weight.shape[2]
    shard_rows = qkv_weight.shape[1]
    hidden = fc1_weight.shape[1] * tensor_count

    vectors = jnp.stack(
        [norm1_gain, norm1_bias, proj_bias, scale1, norm2_gain, norm2_bias, fc2_bias, scale2]
    )
    short = qv_bias.shape[1]
    small = jnp.concatenate([qv_bias.reshape(-1), fc1_bias])
    small = jnp.pad(small[None], ((0, 15), (0, shard_rows - small.shape[0])))
    vecs = lax.all_gather(vectors, "dp", axis=1, tiled=True).astype(jnp.float32)
    turned = jnp.swapaxes(qkv_weight, 1, 2).reshape(3 * cols_here, shard_rows)
    mixed = lax.all_gather(
        jnp.concatenate([turned, small], axis=0), everywhere, axis=0, tiled=False
    )
    w_qkv = mixed[:, : 3 * cols_here].reshape(dp_count, -1, shard_rows)
    w_qkv = jnp.moveaxis(w_qkv, 0, 1).reshape(-1, width)
    biases = mixed[:, 3 * cols_here].reshape(dp_count, tensor_count, shard_rows)
    biases = jnp.moveaxis(biases, 0, 1).reshape(-1, shard_rows).astype(jnp.float32)
    biases = biases[:, : 2 * short + fc1_bias.shape[0]]
    bias_q = biases[:, :short].reshape(tensor_count, 1, cols_here)
    bias_v = biases[:, short : 2 * short].reshape(tensor_count, 1, cols_here)
    bias_fc1 = biases[:, 2 * short :].reshape(hidden)
    bias_qkv = jnp.concatenate([bias_q, jnp.zeros_like(bias_q), bias_v], axis=1).reshape(-1)
    scale_qkv = jnp.concatenate(
        [jnp.full_like(bias_q, 0.125), jnp.ones_like(bias_q), jnp.ones_like(bias_q)], axis=1
    ).reshape(-1)

    w_qkv, proj_weight, fc1_weight, fc2_weight = lax.optimization_barrier(
        (w_qkv, proj_weight, fc1_weight, fc2_weight)
    )
    w_proj = gather_matrix(proj_weight)
    w_fc1 = gather_matrix(fc1_weight.T)
    w_fc2 = gather_matrix(fc2_weight)

    run_ids = segment_ids[:, 0]
    blocks = tok_count // query_rows
    first = run_ids.reshape(batches, blocks, query_rows)[:, :, :1]
    last = run_ids.reshape(batches, blocks, query_rows)[:, :, -1:]
    low = jnp.sum((run_ids[:, None, :] < first).astype(jnp.int32), axis=-1) // key_rows
    reach = jnp.sum((run_ids[:, None, :] <= last).astype(jnp.int32), axis=-1)
    bounds = (low, (reach + key_rows - 1) // key_rows)
    ids_row, ids_col = run_ids[:, None, :], run_ids[:, :, None]

    rows_in = tokens.reshape(total_rows, width).astype(jnp.float32)
    normed_one, rate_one = norm_parts(rows_in)
    normed_one_low = (normed_one * vecs[0] + vecs[1]).astype(jnp.bfloat16)
    projected = ((dot_f32(normed_one_low, w_qkv, contract_cols) + bias_qkv) * scale_qkv).astype(jnp.bfloat16)
    qkv = lax.all_to_all(
        projected.reshape(batches, rows_here, tensor_count * 3 * cols_here),
        "tensor", split_axis=2, concat_axis=1, tiled=True,
    )
    att_heads, lse = attention(qkv, bounds, ids_row, ids_col)
    attended = lax.all_to_all(
        att_heads, "tensor", split_axis=1, concat_axis=2, tiled=True
    ).reshape(total_rows, width)
    branch_one = dot_f32(attended, w_proj) + vecs[2]
    middle = rows_in + vecs[3] * branch_one
    normed_two, rate_two = norm_parts(middle)
    mlp_in = (normed_two * vecs[4] + vecs[5]).astype(jnp.bfloat16)
    pre_act = dot_f32(mlp_in, w_fc1, contract_cols) + bias_fc1
    spread = 0.5 * (1.0 + lax.erf(pre_act * 0.7071067811865476))
    activated = (pre_act * spread).astype(jnp.bfloat16)
    slope = spread + pre_act * jnp.exp(-0.5 * pre_act * pre_act) * 0.3989422804014327
    branch_two = dot_f32(activated, w_fc2) + vecs[6]
    block_out = (middle + vecs[7] * branch_two).astype(jnp.bfloat16)

    grad_top = out_grad.reshape(total_rows, width).astype(jnp.float32)
    d_scale2 = jnp.sum(grad_top * branch_two, axis=0)
    d_branch2 = (vecs[7] * grad_top).astype(jnp.bfloat16)
    d_fc2_bias = jnp.sum(d_branch2.astype(jnp.float32), axis=0)
    d_fc2 = dot_f32(d_branch2, activated, contract_rows)
    d_pre = (dot_f32(d_branch2, w_fc2, contract_cols) * slope).astype(jnp.bfloat16)
    d_fc1_bias = jnp.sum(d_pre.astype(jnp.float32), axis=0)
    d_fc1 = dot_f32(mlp_in, d_pre, contract_rows)
    d_normed_two = dot_f32(d_pre, w_fc1)
    d_gain2 = jnp.sum(d_normed_two * normed_two, axis=0)
    d_bias2 = jnp.sum(d_normed_two, axis=0)
    d_middle = grad_top + norm_back(normed_two, rate_two, vecs[4], d_normed_two)
    d_scale1 = jnp.sum(d_middle * branch_one, axis=0)
    d_branch1 = (vecs[3] * d_middle).astype(jnp.bfloat16)
    d_proj_bias = jnp.sum(d_branch1.astype(jnp.float32), axis=0)
    d_proj = dot_f32(d_branch1, attended, contract_rows)
    d_attended = dot_f32(d_branch1, w_proj, contract_cols).astype(jnp.bfloat16)
    d_att_heads = lax.all_to_all(
        d_attended.reshape(batches, rows_here, width),
        "tensor", split_axis=2, concat_axis=1, tiled=True,
    )
    shard_fc2 = scatter_matrix(d_fc2)
    shard_fc1 = scatter_matrix(d_fc1)
    shard_proj = scatter_matrix(d_proj)
    d_heads = jnp.concatenate(
        attention_back(qkv, bounds, ids_row, ids_col, att_heads, d_att_heads, lse), axis=2
    )
    d_qkv = lax.all_to_all(d_heads, "tensor", split_axis=1, concat_axis=2, tiled=True)
    d_qkv = d_qkv.reshape(total_rows, tensor_count * 3 * cols_here)
    shard_qkv = scatter_matrix(dot_f32(normed_one_low, d_qkv, contract_rows))
    d_bias_qkv = jnp.sum(d_qkv.astype(jnp.float32), axis=0)
    d_normed_one = dot_f32(d_qkv, w_qkv)
    d_gain1 = jnp.sum(d_normed_one * normed_one, axis=0)
    d_bias1 = jnp.sum(d_normed_one, axis=0)
    input_grad = d_middle + norm_back(normed_one, rate_one, vecs[0], d_normed_one)

    early = [d_proj_bias, d_scale1, d_gain2, d_bias2, d_fc2_bias, d_scale2]
    summed = lax.psum(
        jnp.concatenate([d_gain1, d_bias1] + early + [d_fc1_bias, d_bias_qkv]), everywhere
    )
    place_dp = lax.axis_index("dp")
    place = lax.axis_index("tensor") * dp_count + place_dp
    vec_sums = summed[: 8 * width].reshape(8, width)
    vec_sums = lax.dynamic_slice_in_dim(vec_sums, place_dp * shard_rows, shard_rows, 1)
    fc1_sums = summed[8 * width : 8 * width + hidden]
    grad_fc1_bias = lax.dynamic_slice_in_dim(
        fc1_sums, place * fc1_bias.shape[0], fc1_bias.shape[0], 0
    )
    qkv_sums = summed[8 * width + hidden :].reshape(tensor_count, 3, cols_here)
    qv_sums = jnp.stack([qkv_sums[:, 0].reshape(-1), qkv_sums[:, 2].reshape(-1)])
    grad_qv_bias = lax.dynamic_slice_in_dim(qv_sums, place * short, short, 1)
    shape = tokens.shape
    return (
        block_out.reshape(shape),
        input_grad.astype(jnp.bfloat16).reshape(shape),
        vec_sums[0],
        vec_sums[1],
        jnp.moveaxis(shard_qkv.reshape(shard_rows, 3, cols_here), 1, 0),
        grad_qv_bias,
        shard_proj.T,
        vec_sums[2],
        vec_sums[3],
        vec_sums[4],
        vec_sums[5],
        shard_fc1,
        grad_fc1_bias,
        shard_fc2.T,
        vec_sums[6],
        vec_sums[7],
    )


def solution(mesh):
    in_specs = (
        P(None, ("dp", "tensor"), None),
        P(None, "dp", None),
        P(None, ("dp", "tensor"), None),
        P("dp"),
        P("dp"),
        P(None, "dp", "tensor"),
        P(None, ("tensor", "dp")),
        P("tensor", "dp"),
        P("dp"),
        P("dp"),
        P("dp"),
        P("dp"),
        P("dp", "tensor"),
        P(("tensor", "dp")),
        P("tensor", "dp"),
        P("dp"),
        P("dp"),
    )
    out_specs = (
        P(None, ("dp", "tensor"), None),
        P(None, ("dp", "tensor"), None),
        P("dp"),
        P("dp"),
        P(None, "dp", "tensor"),
        P(None, ("tensor", "dp")),
        P("tensor", "dp"),
        P("dp"),
        P("dp"),
        P("dp"),
        P("dp"),
        P("dp", "tensor"),
        P(("tensor", "dp")),
        P("tensor", "dp"),
        P("dp"),
        P("dp"),
    )
    return jax.shard_map(body, mesh=mesh, in_specs=in_specs, out_specs=out_specs, check_vma=False)
```

profile of v0, /device:TPU:0, one launch (start us, length us, event | category | flops | bytes accessed | tf_op | source)
XLA Modules:
  0.0 1100.7 jit_solution(7053402708441256474)
XLA Ops:
  10.5 74.4 %all-gather.9.cloned.1.call-done = bf16[12800,256]{1,0:T(8,128)(2,1)} async-done(((bf16[400,256]{1,0:T(8,128)(2,1)}), bf16[12800,256]{1,0:T(8,128)(2,1)}) %all-gather.9.cloned.1.call-update) | async-done | bytes 6553616 | tf_op jit(solution)/shard_map/all_gather | solution.py:262
  84.9 6.1 slice.147
  91.1 8.8 copy.107
  101.9 5.2 all_gather.27
  110.0 9.5 multiply_convert_fusion.1
  119.5 12.6 %copy.111 = bf16[2,384,3072]{1,0,2:T(2,128)(2,1)} copy(bf16[2,384,3072]{2,1,0:T(8,128)(2,1)} %bitcast.185) | data formatting | bytes 9437184 | tf_op jit(solution)/shard_map/reshape | solution.py:299
  132.1 4.9 all-to-all-start
  139.0 114.7 %all-to-all-done = bf16[2,384,3072]{1,0,2:T(2,128)(2,1)} async-done(((bf16[2,384,3072]{1,0,2:T(2,128)(2,1)}), bf16[2,384,3072]{1,0,2:T(2,128)(2,1)}, u32[]{:S(2)}, u32[]{:S(2)}) %all-to-all-start) | async-done | bytes 4718624 | tf_op jit(solution)/shard_map/all_to_all | solution.py:298
  253.7 5.1 copy.112
  258.8 6.7 copy.113
  265.5 2.4 copy-done
  267.9 55.4 %shard_map.288 = (bf16[2,3072,128]{2,1,0:T(8,128)(2,1)S(1)}, f32[2,6,2,512]{3,2,1,0:T(2,128)S(1)}) custom-call(s32[2,6]{1,0:T(2,128)S(1)} %get-tuple-element.167.low_ref, s32[2,6]{1,0:T(2,128)S(1)} %get-tuple-element.166.high_ref, bf16[2,3072,384]{2,1,0:T(8,128)(2,1)S(1)} %bitcast.162, bf16[2,3072,384]{2,1,0:T(8,128)(2,1)S(1)} %bitcast.163, ...), custom_call_target="tpu_custom_call" | custom-call | flops 19327352832 | bytes 4718592 | tf_op jit(solution)/shard_map/pallas_call | solution.py:165
  324.5 13.8 %copy.115 = bf16[2,3072,128]{2,0,1:T(2,128)(2,1)} copy(bf16[2,3072,128]{2,1,0:T(8,128)(2,1)S(1)} %get-tuple-element.26.att_ref) | data formatting | bytes 3145728 | tf_op jit(solution)/shard_map/pallas_call | solution.py:165
  338.2 3.7 all-to-all-start.1
  342.2 2.2 convert_reduce_fusion.3
  344.5 4.1 copy.117
  348.7 55.1 %all-to-all-done.1 = bf16[2,3072,128]{2,0,1:T(2,128)(2,1)S(1)} async-done(((bf16[2,3072,128]{2,0,1:T(2,128)(2,1)}), bf16[2,3072,128]{2,0,1:T(2,128)(2,1)S(1)}, u32[]{:S(2)}, u32[]{:S(2)}) %all-to-all-start.1) | async-done | bytes 1572896 | tf_op jit(solution)/shard_map/all_to_all | solution.py:303
  405.3 3.6 fusion.40
  411.1 11.5 %copy.120 = bf16[4096,4,256]{0,2,1:T(8,128)(2,1)} copy(bf16[4096,4,256]{2,0,1:T(8,128)(2,1)} %bitcast.168) | data formatting | bytes 16777216 | tf_op jit(solution)/shard_map/transpose | solution.py:218
  422.6 11.4 %copy.119 = bf16[4096,4,256]{0,2,1:T(8,128)(2,1)} copy(bf16[4096,4,256]{2,0,1:T(8,128)(2,1)} %bitcast.169) | data formatting | bytes 16777216 | tf_op jit(solution)/shard_map/transpose | solution.py:218
  434.0 13.9 %multiply_convert_fusion = (bf16[768,4096]{1,0:T(8,128)(2,1)}, f32[768,4096]{1,0:T(8,128)}) fusion(f32[4096]{0:T(1024)S(1)} %slice_bitcast_fusion, bf16[4096,1024]{0,1:T(8,128)(2,1)} %bitcast.172, f32[768,1024]{1,0:T(8,128)S(1)} %copy-done.11, f32[1024]{0:T(1024)S(1)} %bitcast.221, f32[1024]{0:T(1024)S(1)} %bitcast.217, f32[768]{0:T(1024)S(1)} %add_rsqrt_fusion, ...), kind=kOutput, calls=%fused_computation.8 | convolution fusion | flops 6465257472 | bytes 30439424 | tf_op jit(solution)/shard_map/dot_general | solution.py:20
  448.0 14.8 %convert_reduce_fusion = (f32[4096]{0:T(1024)}, bf16[768,4096]{1,0:T(8,128)(2,1)}) fusion(f32[768,4096]{1,0:T(8,128)} %get-tuple-element.161, f32[4096]{0:T(1024)S(1)} %slice_bitcast_fusion, bf16[768,1024]{1,0:T(8,128)(2,1)S(1)} %bitcast.192, bf16[4096,1024]{0,1:T(8,128)(2,1)S(1)} %bitcast.171), kind=kOutput, calls=%fused_computation.7 | convolution fusion | flops 6483341312 | bytes 28868608 | tf_op jit(solution)/shard_map/dot_general | solution.py:20
  462.7 11.0 %multiply_reduce_fusion = (f32[1024]{0:T(1024)S(1)}, f32[768]{0:T(1024)S(1)}, f32[768]{0:T(1024)S(1)}, f32[1024]{0:T(1024)S(1)}, f32[768,1024]{1,0:T(8,128)}) fusion(f32[768,1024]{1,0:T(8,128)S(1)} %copy-done.11, f32[768]{0:T(1024)S(1)} %add_rsqrt_fusion, f32[768]{0:T(1024)S(1)} %broadcast_multiply_fusion.4, f32[1024]{0:T(1024)S(1)} %bitcast.218, ...), kind=kOutput, calls=%fused_computation.47 | convolution fusion | flops 6449524736 | bytes 20996096 | tf_op jit(solution)/shard_map/dot_general | solution.py:20
  473.7 15.0 %fusion.7 = (f32[1024]{0:T(1024)S(1)}, bf16[768,1024]{1,0:T(8,128)(2,1)}, f32[1024]{0:T(1024)S(1)}, f32[768,1024]{1,0:T(8,128)S(1)}, bf16[768,1024]{1,0:T(8,128)(2,1)}) fusion(bf16[2,384,1024]{2,1,0:T(8,128)(2,1)} %param.19, f32[1024]{0:T(1024)S(1)} %bitcast.223, f32[768,1024]{1,0:T(8,128)S(1)} %copy-done.11, f32[1024]{0:T(1024)S(1)} %bitcast.212, ...), kind=kOutput, calls=%fused_computation.21 | convolution fusion | flops 6458177536 | bytes 32018432 | tf_op jit(solution)/shard_map/dot_general | solution.py:20
  492.1 3.2 convolution_convert_fusion.3
  495.4 11.6 %convolution_convert_fusion = bf16[1024,4096]{1,0:T(8,128)(2,1)} fusion(bf16[768,1024]{1,0:T(8,128)(2,1)} %get-tuple-element.136, bf16[768,4096]{1,0:T(8,128)(2,1)} %get-tuple-element.160), kind=kOutput, calls=%fused_computation.12 | convolution fusion | flops 6446645248 | bytes 16252928 | tf_op jit(solution)/shard_map/dot_general | solution.py:20
  507.1 12.1 %convolution_convert_fusion.1 = bf16[1024,4096]{1,0:T(8,128)(2,1)} fusion(bf16[768,4096]{1,0:T(8,128)(2,1)} %get-tuple-element.165, f32[768,1024]{1,0:T(8,128)S(1)} %copy-done.11, f32[1024]{0:T(1024)S(1)} %bitcast.222, f32[1024]{0:T(1024)S(1)} %bitcast.220, f32[768]{0:T(1024)S(1)} %add_rsqrt_fusion, f32[768]{0:T(1024)S(1)} %broadcast_multiply_fusion.4), kind=kOutput, calls=%fused_computation.13 | convolution fusion | flops 6450577408 | bytes 17840128 | tf_op jit(solution)/shard_map/dot_general | solution.py:20
  520.7 4.4 convolution_convert_fusion.4
  525.1 4.3 copy.121
  529.4 42.8 %all_to_all.66 = bf16[2,384,1024]{1,0,2:T(2,128)(2,1)S(1)} all-to-all(bf16[2,384,1024]{1,0,2:T(2,128)(2,1)S(1)} %copy.121), channel_id=1, replica_groups=mesh['dp'=4,'tensor'=8] {'tensor'}, dimensions={2} | all-to-all | bytes 3145728 | tf_op jit(solution)/shard_map/all_to_all | solution.py:334
  574.0 69.6 %shard_map.289 = (bf16[2,3072,128]{2,1,0:T(8,128)(2,1)S(1)}, bf16[2,3072,128]{2,1,0:T(8,128)(2,1)S(1)}, bf16[2,3072,128]{2,1,0:T(8,128)(2,1)S(1)}) custom-call(s32[2,6]{1,0:T(2,128)S(1)} %get-tuple-element.167.low_ref, s32[2,6]{1,0:T(2,128)S(1)} %get-tuple-element.166.high_ref, bf16[2,3072,384]{2,1,0:T(8,128)(2,1)} %bitcast.159, ...), custom_call_target="tpu_custom_call" | custom-call | flops 48318382080 | bytes 9437184 | tf_op jit(solution)/shard_map/pallas_call | solution.py:195
  644.3 44.7 %copy.125 = bf16[2,3072,384]{2,0,1:T(2,128)(2,1)} copy(bf16[2,3072,384]{2,1,0:T(8,128)(2,1)S(1)} %pad_maximum_fusion) | data formatting | bytes 9437184 | tf_op jit(solution)/shard_map/concatenate | solution.py:341
  689.0 4.7 all-to-all-start.3
  694.6 2.0 copy.135
  696.9 105.8 %all-to-all-done.3 = bf16[2,3072,384]{2,0,1:T(2,128)(2,1)} async-done(((bf16[2,3072,384]{2,0,1:T(2,128)(2,1)}), bf16[2,3072,384]{2,0,1:T(2,128)(2,1)}, u32[]{:S(2)}, u32[]{:S(2)}) %all-to-all-start.3) | async-done | bytes 4718624 | tf_op jit(solution)/shard_map/all_to_all | solution.py:344
  802.8 5.1 copy.126
  809.1 2.2 copy-done.9
  811.3 7.3 convolution_convert_fusion.2
  822.2 10.4 fusion.27
  832.6 47.8 %reduce-scatter.13.cloned.1.call-done = bf16[256,3072]{1,0:T(8,128)(2,1)} async-done(((bf16[1024,3072]{1,0:T(8,128)(2,1)}), bf16[256,3072]{1,0:T(8,128)(2,1)}) %reduce-scatter.13.cloned.1.call-update) | async-done | bytes 1572880 | tf_op jit(solution)/shard_map/reduce_scatter | solution.py:222
  880.4 2.6 copy.133
  883.0 4.8 convert_reduce_fusion.1
  888.0 40.5 %psum.7 = f32[15360]{0:T(1024)S(1)} all-reduce(f32[15360]{0:T(1024)S(1)} %constant_dynamic-update-slice_fusion), channel_id=1, replica_groups=mesh['dp'=4,'tensor'=8] {'dp','tensor'}, use_global_device_ids=true, to_apply=%region_20.21 | all-reduce | flops 15360 | bytes 122880 | tf_op jit(solution)/shard_map/psum | solution.py:354
  930.4 4.4 fusion.26
  934.8 17.9 %reduce-scatter.23.cloned.1.call-done = bf16[256,512]{1,0:T(8,128)(2,1)} async-done(((bf16[256,4096]{1,0:T(8,128)(2,1)}), bf16[256,512]{1,0:T(8,128)(2,1)}) %reduce-scatter.23.cloned.1.call-update) | async-done | bytes 262160 | tf_op jit(solution)/shard_map/reduce_scatter | solution.py:223
  954.8 69.1 %reduce-scatter.19.cloned.1.call-done = bf16[256,512]{1,0:T(8,128)(2,1)} async-done(((bf16[256,4096]{1,0:T(8,128)(2,1)}), bf16[256,512]{1,0:T(8,128)(2,1)}) %reduce-scatter.19.cloned.1.call-update) | async-done | bytes 262160 | tf_op jit(solution)/shard_map/reduce_scatter | solution.py:223
  1023.8 1.8 convert_element_type.150
  1025.6 65.8 %reduce-scatter.25.cloned.1.call-done = bf16[384,256]{1,0:T(8,128)(2,1)} async-done(((bf16[3072,256]{1,0:T(8,128)(2,1)}), bf16[384,256]{1,0:T(8,128)(2,1)}) %reduce-scatter.25.cloned.1.call-update) | async-done | bytes 196624
  (206 shorter events, 34.4 us)
Async XLA Ops:
  7.2 77.8 %all-gather.9.cloned.1.call-start = ((), (), s32[]{:S(2)}) async-start(), calls=%async_computation.18 | async-start | bytes 6758400 | tf_op jit(solution)/shard_map/all_gather | solution.py:262
  10.5 334.0 %all-gather.11.cloned.1.call-start = ((), (), s32[]{:S(2)}) async-start(), calls=%async_computation.19 | async-start | bytes 2162688 | tf_op jit(solution)/shard_map/all_gather | solution.py:216
  91.0 9.7 copy-start.34
  91.0 9.7 copy-start.35
  91.0 9.7 copy-start.36
  91.0 9.7 copy-start.37
  91.0 9.7 copy-start.38
  91.0 9.8 copy-start.39
  91.1 9.8 copy-start.40
  91.1 9.8 copy-start.41
  91.1 9.8 copy-start.4
  99.9 7.2 copy-start.19
  99.9 311.2 %all-gather.15.cloned.1.call-start = ((), (), s32[]{:S(2)}) async-start(), calls=%async_computation.21 | async-start | bytes 8650752 | tf_op jit(solution)/shard_map/all_gather | solution.py:216
  100.6 321.9 %all-gather.13.cloned.1.call-start = ((), (), s32[]{:S(2)}) async-start(), calls=%async_computation.20 | async-start | bytes 8650752 | tf_op jit(solution)/shard_map/all_gather | solution.py:216
  101.2 8.9 copy-start.42
  101.2 6.9 copy-start.22
  101.2 8.4 copy-start.24
  101.8 6.3 copy-start.30
  101.8 7.8 copy-start.26
  132.1 5.0 copy-start.3
  132.1 121.6 %all-to-all-start = ((bf16[2,384,3072]{1,0,2:T(2,128)(2,1)}), bf16[2,384,3072]{1,0,2:T(2,128)(2,1)}, u32[]{:S(2)}, u32[]{:S(2)}) async-start(bf16[2,384,3072]{1,0,2:T(2,128)(2,1)} %copy.111), calls=%async_computation | async-start | bytes 9437184 | tf_op jit(solution)/shard_map/all_to_all | solution.py:298
  138.1 127.4 %copy-start.1 = (s32[2,3072,1]{2,1,0:T(8,128)}, s32[2,3072,1]{2,1,0:T(8,128)S(1)}, u32[]{:S(2)}) copy-start(s32[2,3072,1]{2,1,0:T(8,128)S(1)} %broadcast_in_dim_squeeze.4.idk_ref) | copy-start | bytes 73732
  324.5 17.8 %copy-start.14 = (bf16[2,384,1024]{2,1,0:T(8,128)(2,1)S(1)}, bf16[2,384,1024]{2,1,0:T(8,128)(2,1)}, u32[]{:S(2)}) copy-start(bf16[2,384,1024]{2,1,0:T(8,128)(2,1)} %param.19) | copy-start | bytes 4718596
  338.2 65.5 %all-to-all-start.1 = ((bf16[2,3072,128]{2,0,1:T(2,128)(2,1)}), bf16[2,3072,128]{2,0,1:T(2,128)(2,1)S(1)}, u32[]{:S(2)}, u32[]{:S(2)}) async-start(bf16[2,3072,128]{2,0,1:T(2,128)(2,1)} %copy.115), calls=%async_computation.1 | async-start | bytes 3145728 | tf_op jit(solution)/shard_map/all_to_all | solution.py:303
  341.9 352.6 %reduce-scatter.15.cloned.1.call-start = ((), (), s32[]{:S(2)}) async-start(), calls=%async_computation.13 | async-start | bytes 2621440 | tf_op jit(solution)/shard_map/reduce_scatter | solution.py:222
  344.5 60.2 %copy-start.5 = (bf16[2,384,1024]{2,1,0:T(8,128)(2,1)S(1)}, bf16[2,384,1024]{2,1,0:T(8,128)(2,1)}, u32[]{:S(2)}) copy-start(bf16[2,384,1024]{2,1,0:T(8,128)(2,1)} %param.17) | copy-start | bytes 4718596
  404.8 4.2 copy-start.15
  422.6 11.4 %copy-start.11 = (f32[768,1024]{1,0:T(8,128)S(1)}, f32[768,1024]{1,0:T(8,128)}, u32[]{:S(2)}) copy-start(f32[768,1024]{1,0:T(8,128)} %copy-done.10) | copy-start | bytes 9437188
  434.0 13.9 %copy-start.8 = (bf16[4096,4,256]{0,2,1:T(8,128)(2,1)S(1)}, bf16[4096,4,256]{0,2,1:T(8,128)(2,1)}, u32[]{:S(2)}) copy-start(bf16[4096,4,256]{0,2,1:T(8,128)(2,1)} %copy.120) | copy-start | bytes 25165828
  434.0 13.9 %copy-start.17 = (bf16[2,384,1024]{2,1,0:T(8,128)(2,1)S(1)}, bf16[2,384,1024]{2,1,0:T(8,128)(2,1)}, u32[]{:S(2)}) copy-start(bf16[2,384,1024]{2,1,0:T(8,128)(2,1)} %get-tuple-element.125) | copy-start | bytes 4718596
  434.0 28.7 %slice-start = ((s8[8388608]{0:T(1024)(128)(4,1)}), s8[4194304]{0:T(1024)(128)(4,1)S(1)}, s32[]{:S(2)}) async-start(s8[8388608]{0:T(1024)(128)(4,1)} %bitcast.173), calls=%async_computation.24 | async-start | bytes 8388608
  448.0 14.8 %slice-start.1 = ((s8[8388608]{0:T(1024)(128)(4,1)}), s8[4194304]{0:T(1024)(128)(4,1)S(1)}, s32[]{:S(2)}) async-start(s8[8388608]{0:T(1024)(128)(4,1)} %bitcast.173), calls=%async_computation.25 | async-start | bytes 8388608
  495.3 323.3 %reduce-scatter.21.cloned.1.call-start = ((), (), s32[]{:S(2)}) async-start(), calls=%async_computation.16 | async-start | bytes 10485760 | tf_op jit(solution)/shard_map/reduce_scatter | solution.py:222
  507.0 312.2 %reduce-scatter.17.cloned.1.call-start = ((), (), s32[]{:S(2)}) async-start(), calls=%async_computation.14 | async-start | bytes 10485760 | tf_op jit(solution)/shard_map/reduce_scatter | solution.py:222
  689.0 4.8 copy-start.6
  689.0 4.8 copy-start.21
  689.0 4.8 copy-start.23
  689.0 4.8 copy-start.29
  689.0 4.8 copy-start.31
  689.0 113.7 %all-to-all-start.3 = ((bf16[2,3072,384]{2,0,1:T(2,128)(2,1)}), bf16[2,3072,384]{2,0,1:T(2,128)(2,1)}, u32[]{:S(2)}, u32[]{:S(2)}) async-start(bf16[2,3072,384]{2,0,1:T(2,128)(2,1)} %copy.125), calls=%async_computation.3 | async-start | bytes 9437184 | tf_op jit(solution)/shard_map/all_to_all | solution.py:344
  693.8 126.7 %reduce-scatter.27.cloned.1.call-start = ((), (), s32[]{:S(2)}) async-start(), calls=%async_computation.23 | async-start | bytes 589824
  696.6 183.8 %reduce-scatter.13.cloned.1.call-start = ((), (), s32[]{:S(2)}) async-start(), calls=%async_computation.12 | async-start | bytes 7864320 | tf_op jit(solution)/shard_map/reduce_scatter | solution.py:222
  818.6 3.6 copy-start.25
  818.6 134.2 %reduce-scatter.23.cloned.1.call-start = ((), (), s32[]{:S(2)}) async-start(), calls=%async_computation.17 | async-start | bytes 2359296 | tf_op jit(solution)/shard_map/reduce_scatter | solution.py:223
  819.2 204.6 %reduce-scatter.19.cloned.1.call-start = ((), (), s32[]{:S(2)}) async-start(), calls=%async_computation.15 | async-start | bytes 2359296 | tf_op jit(solution)/shard_map/reduce_scatter | solution.py:223
  819.9 271.6 %reduce-scatter.25.cloned.1.call-start = ((), (), s32[]{:S(2)}) async-start(), calls=%async_computation.22 | async-start | bytes 1769472
  883.0 4.9 copy-start.32
  883.0 4.9 copy-start.33
  (12 other events, 25.4 us)
Sparse Core Ops, SparseCore 0:
  11.5 73.3 all-gather.8
  100.0 77.7 all-gather.10
  180.8 127.5 all-gather.14
  311.7 98.8 all-gather.12
  495.5 31.2 reduce-scatter.14
  529.4 71.7 reduce-scatter.20
  603.7 71.7 reduce-scatter.16
  698.9 121.5 reduce-scatter.26
  823.0 57.3 reduce-scatter.12
  884.2 68.4 reduce-scatter.22
  956.7 67.0 reduce-scatter.18
  1027.5 63.9 reduce-scatter.24
where the time goes:
time: 1110 us; the launch traced here: 1100 us
  waiting for transfers between devices  553 us (50%)
  local copies, waits for them, and re-layouts  165 us (15%)
  Pallas kernels  125 us (11%)
  matrix products  117 us (11%)
  blocking collectives  88.5 us (8%)
  other arithmetic  22.5 us (2%)
  between operations  15.6 us (1%)
  starting transfers between devices  14.7 us (1%)
    dot_general x12, matrix products, dot_f32(): lax.dot_general(left, right, dims, preferred_element_type=jnp.float32)  117 us
    all_to_all x1, waiting for transfers between devices, body(): lax.all_to_all(projected.reshape(batches, rows_here, tensor_count * 3 * c...  115 us
    all_to_all x1, waiting for transfers between devices, body(): lax.all_to_all(d_heads, 'tensor', split_axis=1, concat_axis=2, tiled=True)  106 us
    reduce_scatter x2, waiting for transfers between devices, scatter_matrix(): lax.psum_scatter(part, 'tensor', scatter_dimension=1, tiled=True)  87 us
    all_gather x1, waiting for transfers between devices, body(): lax.all_gather(jnp.concatenate([turned, small], axis=0), everywhere, axis...  74.4 us
    pallas_call x1, Pallas kernels, attention_back(): pl.pallas_call(backward_kernel, grid_spec=pltpu.PrefetchScalarGridSpec(nu...  69.6 us
    unnamed x14, waiting for transfers between devices  68.1 us
    pallas_call x1, Pallas kernels, attention(): pl.pallas_call(forward_kernel, grid_spec=pltpu.PrefetchScalarGridSpec(num...  55.4 us
  transfers between devices with their start and end apart: 15, of which 9 were waited for; matrix products, arithmetic and copies ran while one was open for 18% of the time, Pallas kernels for 11%

commit v1 on v0

v1 whole, which is shorter than its diff:
```python
import jax
import jax.numpy as jnp
from jax import lax
from jax.experimental import pallas as pl
from jax.experimental.pallas import tpu as pltpu
from jax.sharding import Mesh, PartitionSpec as P

HEAD_DIM = 64

norm_eps = 1e-06
mask_fill = -1e30
query_rows = 512
key_rows = 512
contract_rows = (((0,), (0,)), ((), ()))
contract_cols = (((1,), (1,)), ((), ()))
everywhere = ("o", "c", "a", "r")


def dot_f32(left, right, dims=(((1,), (0,)), ((), ()))):
    return lax.dot_general(left, right, dims, preferred_element_type=jnp.float32)


def norm_parts(values):
    center = values - jnp.mean(values, axis=-1, keepdims=True)
    rate = lax.rsqrt(jnp.mean(center * center, axis=-1, keepdims=True) + norm_eps)
    return center * rate, rate


def norm_back(normed, rate, gain, grad):
    scaled = gain * grad
    average = jnp.mean(scaled, axis=-1, keepdims=True)
    along = jnp.mean(scaled * normed, axis=-1, keepdims=True)
    return rate * (scaled - average - normed * along)


def head_part(rows, head):
    lane = lax.broadcasted_iota(jnp.int32, rows.shape, 1)
    return jnp.where(lane // HEAD_DIM == head, rows, jnp.zeros_like(rows))


def forward_kernel(low_ref, high_ref, q_ref, k_ref, v_ref, idq_ref, idk_ref, out_ref, lse_ref):
    block = pl.program_id(1)
    queries = q_ref[...]
    heads = queries.shape[1] // HEAD_DIM
    rows = queries.shape[0]
    parts = [head_part(queries, head) for head in range(heads)]
    ids_query = idq_ref[...]

    def step(index, carry):
        start = pl.multiple_of(index * key_rows, key_rows)
        keys = k_ref[pl.ds(start, key_rows), :]
        values = v_ref[pl.ds(start, key_rows), :].T
        same = idk_ref[pl.ds(start, key_rows), :] == ids_query
        result = []
        for head in range(heads):
            top, total, acc = carry[head]
            scores = jnp.where(same, dot_f32(keys, parts[head], contract_cols), mask_fill)
            new_top = jnp.maximum(top, jnp.max(scores, axis=0, keepdims=True))
            expon = jnp.exp(scores - new_top)
            shrink = jnp.exp(top - new_top)
            total = shrink * total + jnp.sum(expon, axis=0, keepdims=True)
            mine = values[head * HEAD_DIM : (head + 1) * HEAD_DIM]
            acc = shrink * acc + dot_f32(mine, expon.astype(jnp.bfloat16))
            result.append((new_top, total, acc))
        return tuple(result)

    start_carry = tuple(
        (
            jnp.full((1, rows), mask_fill, jnp.float32),
            jnp.zeros((1, rows), jnp.float32),
            jnp.zeros((HEAD_DIM, rows), jnp.float32),
        )
        for _ in range(heads)
    )
    final = lax.fori_loop(low_ref[block], high_ref[block], step, start_carry)
    merged = jnp.concatenate([acc / total for _, total, acc in final], axis=0)
    out_ref[...] = merged.T.astype(out_ref.dtype)
    lse_ref[0, 0] = jnp.concatenate([top + jnp.log(total) for top, total, _ in final], axis=0)


def backward_kernel(
    low_ref, high_ref, q_ref, k_ref, v_ref, idq_ref, idk_ref, att_ref, d_att_ref, lse_ref,
    dq_ref, dk_ref, dv_ref, dk_sum, dv_sum,
):
    block = pl.program_id(1)

    @pl.when(block == 0)
    def _():
        dk_sum[...] = jnp.zeros_like(dk_sum)
        dv_sum[...] = jnp.zeros_like(dv_sum)

    queries, d_att = q_ref[...], d_att_ref[...]
    heads = queries.shape[1] // HEAD_DIM
    rows = queries.shape[0]
    parts = [head_part(queries, head) for head in range(heads)]
    d_parts = [head_part(d_att, head) for head in range(heads)]
    ids_query = idq_ref[...]
    products = (att_ref[...].astype(jnp.float32) * d_att.astype(jnp.float32)).T
    inner = [
        jnp.sum(products[head * HEAD_DIM : (head + 1) * HEAD_DIM], axis=0, keepdims=True)
        for head in range(heads)
    ]
    lse = lse_ref[0, 0]

    def step(index, carry):
        start = pl.multiple_of(index * key_rows, key_rows)
        here = pl.ds(start, key_rows)
        keys, values = k_ref[here, :], v_ref[here, :]
        keys_turned = keys.T
        same = idk_ref[here, :] == ids_query
        result = []
        d_value, d_key = dv_sum[here, :], dk_sum[here, :]
        for head in range(heads):
            scores = jnp.where(same, dot_f32(keys, parts[head], contract_cols), mask_fill)
            probs = jnp.exp(scores - lse[head : head + 1])
            d_probs = dot_f32(values, d_parts[head], contract_cols)
            d_scores = (probs * (d_probs - inner[head])).astype(jnp.bfloat16)
            d_value = d_value + dot_f32(probs.astype(jnp.bfloat16), d_parts[head])
            d_key = d_key + dot_f32(d_scores, parts[head])
            mine = keys_turned[head * HEAD_DIM : (head + 1) * HEAD_DIM]
            result.append(carry[head] + dot_f32(mine, d_scores))
        dv_sum[here, :] = d_value
        dk_sum[here, :] = d_key
        return tuple(result)

    empty = tuple(jnp.zeros((HEAD_DIM, rows), jnp.float32) for _ in range(heads))
    final = lax.fori_loop(low_ref[block], high_ref[block], step, empty)
    dq_ref[...] = (jnp.concatenate(final, axis=0).T * 0.125).astype(dq_ref.dtype)

    @pl.when(block == pl.num_programs(1) - 1)
    def _():
        dk_ref[...] = dk_sum[...].astype(dk_ref.dtype)
        dv_ref[...] = dv_sum[...].astype(dv_ref.dtype)


def column_specs(tok_count, col_blocks, group=0):
    q_spec = pl.BlockSpec((query_rows, 128), lambda g, i, *_: (i, group + g))
    k_spec = pl.BlockSpec((tok_count, 128), lambda g, i, *_: (0, col_blocks + group + g))
    v_spec = pl.BlockSpec((tok_count, 128), lambda g, i, *_: (0, 2 * col_blocks + group + g))
    idq_spec = pl.BlockSpec((1, query_rows), lambda g, i, *_: (0, i))
    idk_spec = pl.BlockSpec((tok_count, 1), lambda g, i, *_: (0, 0))
    lse_spec = pl.BlockSpec(
        (1, 1, 128 // HEAD_DIM, query_rows), lambda g, i, *_: (group + g, i, 0, 0)
    )
    return q_spec, k_spec, v_spec, idq_spec, idk_spec, lse_spec


def attention(qkv, bounds, ids_row, ids_col):
    tok_count, cols3 = qkv.shape
    cols = cols3 // 3
    blocks, groups = tok_count // query_rows, cols // 128
    q_spec, k_spec, v_spec, idq_spec, idk_spec, lse_spec = column_specs(tok_count, groups)
    pairs = tok_count * tok_count // 2
    return pl.pallas_call(
        forward_kernel,
        grid_spec=pltpu.PrefetchScalarGridSpec(
            num_scalar_prefetch=2,
            grid=(groups, blocks),
            in_specs=[q_spec, k_spec, v_spec, idq_spec, idk_spec],
            out_specs=[q_spec, lse_spec],
        ),
        out_shape=[
            jax.ShapeDtypeStruct((tok_count, cols), jnp.bfloat16),
            jax.ShapeDtypeStruct((groups, blocks, 128 // HEAD_DIM, query_rows), jnp.float32),
        ],
        compiler_params=pltpu.CompilerParams(vmem_limit_bytes=40 * 1024 * 1024),
        cost_estimate=pl.CostEstimate(
            flops=pairs * 32 * cols, bytes_accessed=2 * qkv.size, transcendentals=2 * pairs
        ),
    )(*bounds, qkv, qkv, qkv, ids_row, ids_col)


def attention_back(qkv, bounds, ids_row, ids_col, att, d_att, lse, group):
    tok_count, cols3 = qkv.shape
    cols = cols3 // 3
    blocks, groups = tok_count // query_rows, cols // 128
    q_spec, k_spec, v_spec, idq_spec, idk_spec, lse_spec = column_specs(tok_count, groups, group)
    pairs = tok_count * tok_count // 2
    out_spec = pl.BlockSpec((query_rows, 128), lambda g, i, *_: (i, 0))
    out_whole = pl.BlockSpec((tok_count, 128), lambda g, i, *_: (0, 0))
    one = jax.ShapeDtypeStruct((tok_count, 128), jnp.bfloat16)
    return pl.pallas_call(
        backward_kernel,
        grid_spec=pltpu.PrefetchScalarGridSpec(
            num_scalar_prefetch=2,
            grid=(1, blocks),
            in_specs=[q_spec, k_spec, v_spec, idq_spec, idk_spec, q_spec, q_spec, lse_spec],
            out_specs=[out_spec, out_whole, out_whole],
            scratch_shapes=[
                pltpu.VMEM((tok_count, 128), jnp.float32),
                pltpu.VMEM((tok_count, 128), jnp.float32),
            ],
        ),
        out_shape=[one, one, one],
        compiler_params=pltpu.CompilerParams(vmem_limit_bytes=48 * 1024 * 1024),
        cost_estimate=pl.CostEstimate(
            flops=pairs * 40 * 128, bytes_accessed=4 * qkv.size, transcendentals=2 * pairs
        ),
    )(*bounds, qkv, qkv, qkv, ids_row, ids_col, att, d_att, lse)


pieces = 2


def entry_kernel(
    outer_count, rest_count, tok_ref, w_in_ref, pack_ref, ids_ref, x_ref, w_ref, packs_ref, ids_out_ref,
    ids_send, ids_recv, ids_sem,
    pack_sem, pack_send, pack_recv, packs_send, packs_recv, move_send, move_recv, rest_send, rest_recv, core_send, core_recv,
    w_send, w_recv, outer_send, outer_recv, own_sem,
):
    o, c, a, r = (lax.axis_index(name) for name in everywhere)
    rows = tok_ref.shape[1]
    part = rows // pieces
    w_rows = w_in_ref.shape[1]
    half, low = a // 2, a % 2
    counts = (outer_count, 2, 4, rest_count)
    here_spot = (o, c, a, r)
    dp_shifts = [(i, j, 0, 0) for i in range(outer_count) for j in range(2)][1:]
    tensor_shifts = [(0, 0, i, j) for i in range(4) for j in range(rest_count)][1:]
    core_shifts = [(0, i, j, 0) for i in range(2) for j in range(4)][1:]

    def away(shift):
        return tuple((spot + s) % n for spot, s, n in zip(here_spot, shift, counts))

    def back(shift):
        return tuple((spot - s + n) % n for spot, s, n in zip(here_spot, shift, counts))

    partners = [away(shift) for shift in sorted({*dp_shifts, *tensor_shifts, *core_shifts})]
    barrier = pltpu.get_barrier_semaphore()
    for partner in partners:
        pl.semaphore_signal(barrier, inc=1, device_id=partner, device_id_type=pl.DeviceIdType.MESH)
    pl.semaphore_wait(barrier, len(partners))
    peer = (o, 1 - c, a, r)

    def remote(src, dst, send, recv, target):
        return pltpu.make_async_remote_copy(
            src_ref=src, dst_ref=dst, send_sem=send, recv_sem=recv,
            device_id=target, device_id_type=pl.DeviceIdType.MESH,
        )

    def pack_spot(spot):
        return packs_ref.at[spot[2] * rest_count + spot[3], spot[0] * 2 + spot[1]]

    def pack_group(spot):
        return packs_ref.at[spot[2] * rest_count + spot[3]]

    def pack_copy(i):
        return remote(
            pack_ref, pack_spot(here_spot), pack_send.at[i], pack_recv.at[i], away(dp_shifts[i])
        )

    def packs_copy(i):
        mine = pack_group(here_spot)
        return remote(mine, mine, packs_send.at[i], packs_recv.at[i], away(tensor_shifts[i]))

    pack_own = pltpu.make_async_copy(pack_ref, pack_spot(here_spot), pack_sem)
    pack_own.start()
    ids_own = pltpu.make_async_copy(ids_ref, ids_out_ref.at[c], ids_sem)
    ids_own.start()
    ids_copy = remote(ids_ref, ids_out_ref.at[c], ids_send, ids_recv, peer)
    ids_copy.start()
    for i in range(len(dp_shifts)):
        pack_copy(i).start()

    def x_rows(seq_spot, rest_spot, piece):
        start = (seq_spot * rest_count + rest_spot) * rows + piece * part
        return x_ref.at[pl.ds(pl.multiple_of(start, part), part), :]

    def tok_rows(batch, piece):
        return tok_ref.at[batch, pl.ds(piece * part, part), :]

    def own_copy(batch, piece):
        return pltpu.make_async_copy(
            tok_rows(batch, piece), x_rows(a, r, piece), own_sem.at[piece]
        )

    def move_copy(batch, piece):
        return remote(
            tok_rows(batch, piece), x_rows(a, r, piece),
            move_send.at[batch, piece], move_recv.at[low, piece], (o, half, 2 * batch + c, r),
        )

    def stays(batch):
        return jnp.logical_and(half == c, 2 * batch + c == a)

    for piece in range(pieces):
        for batch in range(2):
            @pl.when(stays(batch))
            def _():
                own_copy(batch, piece).start()

            @pl.when(jnp.logical_not(stays(batch)))
            def _():
                move_copy(batch, piece).start()

    def w_spot(outer_spot, core_spot, turn):
        start = pl.multiple_of((outer_spot * 2 + core_spot) * w_rows, w_rows)
        return w_ref.at[turn, :, pl.ds(start, w_rows), :]

    w_own = pltpu.make_async_copy(w_in_ref, w_spot(o, c, low), own_sem.at[pieces])

    def w_copy(target):
        return remote(
            w_in_ref, w_spot(o, c, low), w_send.at[target], w_recv.at[c, low], (o, half, target, r)
        )

    for target in range(4):
        same = jnp.logical_and(half == c, a == target)

        @pl.when(same)
        def _():
            w_own.start()

        @pl.when(jnp.logical_not(same))
        def _():
            w_copy(target).start()

    pack_own.wait()
    for i, shift in enumerate(dp_shifts):
        spot = pack_spot(back(shift))
        remote(spot, spot, pack_send.at[i], pack_recv.at[i], peer).wait_recv()
    for i in range(len(tensor_shifts)):
        packs_copy(i).start()

    def rest_copy(turn, piece, shift):
        here = x_rows(2 * c + turn, r, piece)
        return remote(
            here, here, rest_send.at[turn, piece, shift - 1], rest_recv.at[turn, piece, shift - 1],
            (o, c, a, (r + shift) % rest_count),
        )

    def rest_landed(turn, piece, shift):
        here = x_rows(2 * c + turn, (r - shift + rest_count) % rest_count, piece)
        return remote(
            here, here, rest_send.at[turn, piece, shift - 1], rest_recv.at[turn, piece, shift - 1],
            peer,
        )

    def core_copy(turn, piece, shift, core):
        here = x_rows(2 * core + turn, (r - shift + rest_count) % rest_count, piece)
        return remote(
            here, here, core_send.at[turn, piece, shift], core_recv.at[turn, piece, shift], peer
        )

    for piece in range(pieces):
        for turn in range(2):
            same = jnp.logical_and(low == c, 2 * c + turn == a)

            @pl.when(same)
            def _():
                own_copy(0, piece).wait()

            @pl.when(jnp.logical_not(same))
            def _():
                here = x_rows(2 * c + turn, r, piece)
                remote(
                    here, here, move_send.at[0, piece], move_recv.at[turn, piece], peer
                ).wait_recv()

            for shift in range(1, rest_count):
                rest_copy(turn, piece, shift).start()
            core_copy(turn, piece, 0, c).start()

    def outer_copy(core, shift, outer_spot):
        start = pl.multiple_of((outer_spot * 2 + core) * w_rows, w_rows)
        here = w_ref.at[:, :, pl.ds(start, w_rows), :]
        return remote(
            here, here, outer_send.at[core, shift - 1], outer_recv.at[core, shift - 1],
            ((o + shift) % outer_count, c, a, r),
        )

    for core in range(2):
        for turn in range(2):
            same = jnp.logical_and(
                half == c, jnp.logical_and(c == core, low == turn)
            )

            @pl.when(same)
            def _():
                w_own.wait()

            @pl.when(jnp.logical_not(same))
            def _():
                here = w_spot(o, core, turn)
                remote(here, here, w_send.at[0], w_recv.at[core, turn], peer).wait_recv()
        for shift in range(1, outer_count):
            outer_copy(core, shift, o).start()

    for piece in range(pieces):
        for turn in range(2):
            for shift in range(1, rest_count):
                rest_landed(turn, piece, shift).wait_recv()
                core_copy(turn, piece, shift, c).start()

    for core in range(2):
        for shift in range(1, outer_count):
            outer_copy(core, shift, (o - shift + outer_count) % outer_count).wait_recv()
    for piece in range(pieces):
        for turn in range(2):
            for shift in range(rest_count):
                core_copy(turn, piece, shift, 1 - c).wait_recv()

    for piece in range(pieces):
        for batch in range(2):
            @pl.when(jnp.logical_not(stays(batch)))
            def _():
                move_copy(batch, piece).wait_send()
        for turn in range(2):
            for shift in range(1, rest_count):
                rest_copy(turn, piece, shift).wait_send()
            for shift in range(rest_count):
                core_copy(turn, piece, shift, c).wait_send()
    for target in range(4):
        @pl.when(jnp.logical_not(jnp.logical_and(half == c, a == target)))
        def _():
            w_copy(target).wait_send()
    for core in range(2):
        for shift in range(1, outer_count):
            outer_copy(core, shift, o).wait_send()
    for i in range(len(dp_shifts)):
        pack_copy(i).wait_send()
    ids_own.wait()
    ids_copy.wait_send()
    remote(ids_ref, ids_out_ref.at[1 - c], ids_send, ids_recv, peer).wait_recv()
    for i, shift in enumerate(tensor_shifts):
        spot = pack_group(back(shift))
        remote(spot, spot, packs_send.at[i], packs_recv.at[i], peer).wait_recv()
        packs_copy(i).wait_send()


def entry(tokens, qkv_weight, pack, ids):
    outer_count, rest_count = lax.axis_size("o"), lax.axis_size("r")
    batches, rows, width = tokens.shape
    dma = pltpu.SemaphoreType.DMA
    wide, narrow = max(rest_count - 1, 1), max(outer_count - 1, 1)
    return pl.pallas_call(
        lambda *refs: entry_kernel(outer_count, rest_count, *refs),
        in_specs=[pl.BlockSpec(memory_space=pl.ANY)] * 4,
        out_specs=[pl.BlockSpec(memory_space=pl.ANY)] * 4,
        out_shape=[
            jax.ShapeDtypeStruct((4 * rest_count * rows, width), tokens.dtype),
            jax.ShapeDtypeStruct(
                (2, qkv_weight.shape[0], width, qkv_weight.shape[2]), qkv_weight.dtype
            ),
            jax.ShapeDtypeStruct((4 * rest_count, 2 * outer_count, *pack.shape), pack.dtype),
            jax.ShapeDtypeStruct((2, *ids.shape), ids.dtype),
        ],
        scratch_shapes=[
            dma(()), dma(()), dma(()),
            dma(()), dma((2 * outer_count - 1,)), dma((2 * outer_count - 1,)),
            dma((4 * rest_count - 1,)), dma((4 * rest_count - 1,)),
            dma((2, pieces)), dma((2, pieces)),
            dma((2, pieces, wide)), dma((2, pieces, wide)),
            dma((2, pieces, rest_count)), dma((2, pieces, rest_count)),
            dma((4,)), dma((2, 2)), dma((2, narrow)), dma((2, narrow)), dma((pieces + 1,)),
        ],
        compiler_params=pltpu.CompilerParams(collective_id=0, has_side_effects=True),
        cost_estimate=pl.CostEstimate(
            flops=0, bytes_accessed=200 * 1024 * 1024, transcendentals=0
        ),
    )(tokens, qkv_weight, pack, ids)


def exit_kernel(
    outer_count, rest_count, sums_ref, own_ref, total_ref, out_ref,
    dp_got, part, tensor_got, dp_send, dp_recv, tensor_send, tensor_recv,
    move_send, move_recv, own_sem,
):
    o, c, a, r = (lax.axis_index(name) for name in everywhere)
    half, low = a // 2, a % 2
    counts = (outer_count, 2, 4, rest_count)
    here_spot = (o, c, a, r)
    dp_shifts = [(i, j, 0, 0) for i in range(outer_count) for j in range(2)][1:]
    tensor_shifts = [(0, 0, i, j) for i in range(4) for j in range(rest_count)][1:]
    core_shifts = [(0, i, j, 0) for i in range(2) for j in range(4)][1:]

    def away(shift):
        return tuple((spot + s) % n for spot, s, n in zip(here_spot, shift, counts))

    partners = [away(shift) for shift in sorted({*dp_shifts, *tensor_shifts, *core_shifts})]
    barrier = pltpu.get_barrier_semaphore()
    for partner in partners:
        pl.semaphore_signal(barrier, inc=1, device_id=partner, device_id_type=pl.DeviceIdType.MESH)
    pl.semaphore_wait(barrier, len(partners))
    peer = (o, 1 - c, a, r)

    def remote(src, dst, send, recv, target):
        return pltpu.make_async_remote_copy(
            src_ref=src, dst_ref=dst, send_sem=send, recv_sem=recv,
            device_id=target, device_id_type=pl.DeviceIdType.MESH,
        )

    def stays(turn):
        return jnp.logical_and(low == c, 2 * c + turn == a)

    def move_copy(turn):
        return remote(
            own_ref.at[turn], out_ref.at[half], move_send.at[turn], move_recv.at[half],
            (o, low, 2 * c + turn, r),
        )

    stay_copy = pltpu.make_async_copy(own_ref.at[low], out_ref.at[half], own_sem)
    for turn in range(2):
        @pl.when(stays(turn))
        def _():
            stay_copy.start()

        @pl.when(jnp.logical_not(stays(turn)))
        def _():
            move_copy(turn).start()

    def dp_copy(i):
        target = away(dp_shifts[i])
        return remote(
            sums_ref.at[target[0] * 2 + target[1]], dp_got.at[i], dp_send.at[i], dp_recv.at[i],
            target,
        )

    for i in range(len(dp_shifts)):
        dp_copy(i).start()
    total = sums_ref[o * 2 + c]
    for i in range(len(dp_shifts)):
        dp_copy(i).wait_recv()
        total = total + dp_got[i]
    part[...] = total

    def tensor_copy(i):
        return remote(
            part, tensor_got.at[i], tensor_send.at[i], tensor_recv.at[i], away(tensor_shifts[i])
        )

    for i in range(len(tensor_shifts)):
        tensor_copy(i).start()
    for i in range(len(tensor_shifts)):
        tensor_copy(i).wait_recv()
        total = total + tensor_got[i]
    total_ref[...] = total

    for batch in range(2):
        same = jnp.logical_and(half == c, 2 * batch + c == a)

        @pl.when(same)
        def _():
            stay_copy.wait()

        @pl.when(jnp.logical_not(same))
        def _():
            spot = out_ref.at[batch]
            remote(spot, spot, move_send.at[0], move_recv.at[batch], peer).wait_recv()
    for turn in range(2):
        @pl.when(jnp.logical_not(stays(turn)))
        def _():
            move_copy(turn).wait_send()
    for i in range(len(dp_shifts)):
        dp_copy(i).wait_send()
    for i in range(len(tensor_shifts)):
        tensor_copy(i).wait_send()


def leave(sums, own):
    outer_count, rest_count = lax.axis_size("o"), lax.axis_size("r")
    dma = pltpu.SemaphoreType.DMA
    few, many = 2 * outer_count - 1, 4 * rest_count - 1
    shape = sums.shape[1:]
    return pl.pallas_call(
        lambda *refs: exit_kernel(outer_count, rest_count, *refs),
        in_specs=[pl.BlockSpec(memory_space=pltpu.VMEM), pl.BlockSpec(memory_space=pl.ANY)],
        out_specs=[pl.BlockSpec(memory_space=pltpu.VMEM), pl.BlockSpec(memory_space=pl.ANY)],
        out_shape=[
            jax.ShapeDtypeStruct(shape, jnp.float32),
            jax.ShapeDtypeStruct(own.shape, own.dtype),
        ],
        scratch_shapes=[
            pltpu.VMEM((few, *shape), jnp.float32), pltpu.VMEM(shape, jnp.float32),
            pltpu.VMEM((many, *shape), jnp.float32),
            dma((few,)), dma((few,)), dma((many,)), dma((many,)), dma((2,)), dma((2,)), dma(()),
        ],
        compiler_params=pltpu.CompilerParams(collective_id=1, has_side_effects=True),
        cost_estimate=pl.CostEstimate(
            flops=0, bytes_accessed=120 * 1024 * 1024, transcendentals=0
        ),
    )(sums, own)


def mlp_kernel(
    h_ref, dm_ref, w1_ref, w2_ref, bias_ref, m_ref, dh_ref, grad1_ref, grad2_ref, dbias_ref,
    h_turned, dm_turned, kept, sent, got, send_sem, got_sem,
):
    o, core, a, r = (lax.axis_index(name) for name in everywhere)
    block = pl.program_id(0)
    count = pl.num_programs(0) - 1
    slot, other = block % 2, (block + 1) % 2
    peer = (o, 1 - core, a, r)

    def to_peer(index, turn):
        return pltpu.make_async_remote_copy(
            src_ref=sent.at[turn], dst_ref=got.at[index],
            send_sem=send_sem.at[turn], recv_sem=got_sem.at[index],
            device_id=peer, device_id_type=pl.DeviceIdType.MESH,
        )

    @pl.when(block == 0)
    def _():
        barrier = pltpu.get_barrier_semaphore()
        pl.semaphore_signal(barrier, inc=1, device_id=peer, device_id_type=pl.DeviceIdType.MESH)
        pl.semaphore_wait(barrier, 1)
        h_turned[...] = h_ref[...].T
        dm_turned[...] = dm_ref[...].T
        m_ref[...] = jnp.zeros_like(m_ref)
        dh_ref[...] = jnp.zeros_like(dh_ref)

    @pl.when(block >= 2)
    def _():
        to_peer(block - 2, slot).wait_send()

    @pl.when(block < count)
    def _():
        dp_count, _, _, rows = w1_ref.shape
        pre, d_act = bias_ref[...], 0.0
        for d in range(dp_count):
            spot = slice(d * rows, (d + 1) * rows)
            pre = pre + dot_f32(h_ref[:, spot], w1_ref[d, 0], contract_cols)
        for d in range(dp_count):
            spot = slice(d * rows, (d + 1) * rows)
            d_act = d_act + dot_f32(dm_ref[:, spot], w2_ref[d, 0], contract_cols)
        spread = 0.5 * (1.0 + lax.erf(pre * 0.7071067811865476))
        act = (pre * spread).astype(jnp.bfloat16)
        slope = spread + pre * jnp.exp(-0.5 * pre * pre) * 0.3989422804014327
        d_pre = (d_act * slope).astype(jnp.bfloat16)
        dbias_ref[...] = jnp.sum(d_pre.astype(jnp.float32), axis=0, keepdims=True)
        for d in range(dp_count):
            spot = slice(d * rows, (d + 1) * rows)
            m_ref[:, spot] += dot_f32(act, w2_ref[d, 0])
            dh_ref[:, spot] += dot_f32(d_pre, w1_ref[d, 0])
        for d in range(dp_count):
            spot = slice(d * rows, (d + 1) * rows)
            grad1 = dot_f32(h_turned[spot, :], d_pre).astype(jnp.bfloat16)
            grad2 = dot_f32(dm_turned[spot, :], act).astype(jnp.bfloat16)

            @pl.when(core == d % 2)
            def _():
                kept[slot, 0, d // 2] = grad1
                kept[slot, 1, d // 2] = grad2

            @pl.when(core != d % 2)
            def _():
                sent[slot, 0, d // 2] = grad1
                sent[slot, 1, d // 2] = grad2

        to_peer(block, slot).start()

    @pl.when(block >= 1)
    def _():
        to_peer(block - 1, other).wait_recv()
        for turn, out_ref in enumerate((grad1_ref, grad2_ref)):
            mine = kept[other, turn].astype(jnp.float32)
            out_ref[0] = (mine + got[block - 1, turn].astype(jnp.float32)).astype(jnp.bfloat16)

    @pl.when(block == count)
    def _():
        to_peer(block - 1, other).wait_send()


def mlp(rows_low, d_branch, weights, hid, bias):
    tokens_here, width = rows_low.shape
    dp_count, tensor_count, _, rows = weights.shape
    outer = dp_count // 2
    whole = pl.BlockSpec((tokens_here, width), lambda t: (0, 0))
    grad_spec = pl.BlockSpec((1, outer, rows, hid), lambda t: (jnp.maximum(t - 1, 0), 0, 0, 0))
    grad = jax.ShapeDtypeStruct((tensor_count, outer, rows, hid), jnp.bfloat16)
    out = jax.ShapeDtypeStruct((tokens_here, width), jnp.float32)
    last = tensor_count - 1
    line = pl.BlockSpec((1, hid), lambda t: (0, jnp.minimum(t, last)))
    w1_spec = pl.BlockSpec((dp_count, 1, hid, rows), lambda t: (0, jnp.minimum(t, last), 0, 0))
    w2_spec = pl.BlockSpec((dp_count, 1, hid, rows), lambda t: (0, jnp.minimum(t, last), 1, 0))
    return pl.pallas_call(
        mlp_kernel,
        grid=(tensor_count + 1,),
        in_specs=[whole, whole, w1_spec, w2_spec, line],
        out_specs=[whole, whole, grad_spec, grad_spec, line],
        out_shape=[
            out, out, grad, grad,
            jax.ShapeDtypeStruct((1, tensor_count * hid), jnp.float32),
        ],
        scratch_shapes=[
            pltpu.VMEM((width, tokens_here), jnp.bfloat16),
            pltpu.VMEM((width, tokens_here), jnp.bfloat16),
            pltpu.VMEM((2, 2, outer, rows, hid), jnp.bfloat16),
            pltpu.VMEM((2, 2, outer, rows, hid), jnp.bfloat16),
            pltpu.VMEM((tensor_count, 2, outer, rows, hid), jnp.bfloat16),
            pltpu.SemaphoreType.DMA((2,)),
            pltpu.SemaphoreType.DMA((tensor_count,)),
        ],
        compiler_params=pltpu.CompilerParams(
            vmem_limit_bytes=60 * 1024 * 1024, collective_id=2, has_side_effects=True
        ),
        cost_estimate=pl.CostEstimate(
            flops=12 * tokens_here * width * tensor_count * hid,
            bytes_accessed=64 * 1024 * 1024,
            transcendentals=2 * tokens_here * tensor_count * hid,
        ),
    )(rows_low, d_branch, weights, weights, bias)


def gather_parts(shard):
    parts = lax.all_gather(shard, everywhere, axis=0, tiled=False)
    return parts.reshape(lax.axis_size("o") * 2, -1, *shard.shape)


def pick(blocks, index):
    return lax.dynamic_index_in_dim(blocks, index, 0, keepdims=False)


def place_shift(step, count):
    return [(spot, (spot + step) % count) for spot in range(count)]


def move_pairs(step):
    pairs = []
    for core in range(2):
        for seq in range(4):
            batch = (seq % 2) ^ step
            pairs.append((core * 4 + seq, (seq // 2) * 4 + 2 * batch + core))
    return pairs


def move_in(both):
    low = lax.axis_index("a") % 2
    batch = lax.axis_index("a") // 2
    got = [
        lax.ppermute(pick(both, low ^ step), ("c", "a"), move_pairs(step)) for step in range(2)
    ]
    return jnp.stack([jnp.where(batch == 0, got[j], got[1 - j]) for j in range(2)])


def move_out(own):
    low = lax.axis_index("a") % 2
    batch = lax.axis_index("a") // 2
    got = [
        lax.ppermute(
            pick(own, batch ^ step), ("c", "a"), [(t, s) for s, t in move_pairs(step)]
        )
        for step in range(2)
    ]
    return jnp.stack([jnp.where(low == 0, got[b], got[1 - b]) for b in range(2)])


def sum_shards(blocks, axis, dim, dtype):
    count, me = blocks.shape[dim], lax.axis_index(axis)

    def block(spot):
        return lax.dynamic_index_in_dim(blocks, spot, dim, keepdims=False)

    got = [
        lax.ppermute(block((me + step) % count), axis, place_shift(step, count))
        for step in range(1, count)
    ]
    total = block(me).astype(jnp.float32)
    for values in got:
        total = total + values.astype(jnp.float32)
    return total.astype(dtype)


def core_sum(own, sent):
    got = lax.ppermute(sent, "c", [(0, 1), (1, 0)])
    total = (own.astype(jnp.float32) + got.astype(jnp.float32)).astype(jnp.bfloat16)
    return total.reshape(4, lax.axis_size("r"), *total.shape[1:])


def body(
    tokens, segment_ids, out_grad, norm1_gain, norm1_bias, qkv_weight, qv_bias, proj_weight,
    proj_bias, scale1, norm2_gain, norm2_bias, fc1_weight, fc1_bias, fc2_weight, fc2_bias, scale2,
):
    o, c, a, r = (lax.axis_index(name) for name in everywhere)
    outer, rest = lax.axis_size("o"), lax.axis_size("r")
    dp_count, tensor_count = outer * 2, 4 * rest
    batches, rows_here, width = tokens.shape
    own_rows = 2 * rows_here
    tok_count = rows_here * tensor_count
    cols_here, shard_rows = qkv_weight.shape[2], qkv_weight.shape[1]
    own_cols = 2 * cols_here
    hidden = fc1_weight.shape[1] * tensor_count
    short, fc1_short = qv_bias.shape[1], fc1_bias.shape[0]

    vectors = jnp.stack(
        [norm1_gain, norm1_bias, proj_bias, scale1, norm2_gain, norm2_bias, fc2_bias, scale2]
    )
    small = jnp.concatenate([qv_bias.reshape(-1), fc1_bias])
    small = jnp.pad(small[None], ((0, 7), (0, shard_rows - small.shape[0])))
    seq_rows, w_parts, packs, ids = entry(
        tokens, qkv_weight, jnp.concatenate([vectors, small]), segment_ids
    )
    seq_rows, out_grad = lax.optimization_barrier((seq_rows, out_grad))
    vecs = jnp.moveaxis(packs[0, :, :8], 0, 1).reshape(8, width).astype(jnp.float32)
    biases = packs[:, :, 8].astype(jnp.float32)
    bias_fc1 = biases[:, :, 2 * short : 2 * short + fc1_short].reshape(hidden)
    bias_qv = biases[:, :, : 2 * short].reshape(2, 2, rest, dp_count, 2, short)
    bias_qv = lax.dynamic_index_in_dim(bias_qv, c, 0, keepdims=False)
    bias_qv = lax.dynamic_index_in_dim(bias_qv, r, 1, keepdims=False)
    bias_qv = jnp.moveaxis(bias_qv, 2, 0).reshape(2, own_cols)
    bias_qkv = jnp.concatenate([bias_qv[0], jnp.zeros_like(bias_qv[0]), bias_qv[1]])
    scale_qkv = jnp.concatenate([jnp.full((own_cols,), 0.125), jnp.ones((2 * own_cols,))])

    run_ids = pick(pick(ids, a % 2), a // 2)[0]
    blocks = tok_count // query_rows
    first = run_ids.reshape(blocks, query_rows)[:, :1]
    last = run_ids.reshape(blocks, query_rows)[:, -1:]
    low = jnp.sum((run_ids[None] < first).astype(jnp.int32), axis=-1) // key_rows
    reach = jnp.sum((run_ids[None] <= last).astype(jnp.int32), axis=-1)
    bounds = (low, (reach + key_rows - 1) // key_rows)
    ids_row, ids_col = run_ids[None, :], run_ids[:, None]

    weights = gather_parts(jnp.concatenate([fc1_weight.T, fc2_weight, proj_weight]))
    w_proj = weights[:, :, 2 * fc2_weight.shape[0] :]
    w_proj = jnp.transpose(w_proj, (1, 2, 0, 3)).reshape(width, width)
    w_qkv = jnp.moveaxis(w_parts, 0, 2).swapaxes(0, 1).reshape(width, 3 * own_cols)

    def own_of(values):
        split = values.reshape(2, 2, rest, rows_here, values.shape[1])
        split = lax.dynamic_index_in_dim(split, c, 0, keepdims=False)
        split = lax.dynamic_index_in_dim(split, r, 1, keepdims=False)
        return split.reshape(own_rows, values.shape[1])

    normed_all, _ = norm_parts(seq_rows.astype(jnp.float32))
    normed_all_low = (normed_all * vecs[0] + vecs[1]).astype(jnp.bfloat16)
    qkv = ((dot_f32(normed_all_low, w_qkv) + bias_qkv) * scale_qkv).astype(jnp.bfloat16)
    grad_moved = move_in(out_grad)
    att_heads, lse = attention(qkv, bounds, ids_row, ids_col)

    rows_in = own_of(seq_rows).astype(jnp.float32)
    normed_one, rate_one = norm_parts(rows_in)
    sent = att_heads.reshape(2, 2, rest, rows_here, own_cols)
    sent = jnp.swapaxes(sent, 1, 2).reshape(2 * rest, own_rows, own_cols)
    attended = lax.all_to_all(sent, ("c", "r"), split_axis=0, concat_axis=0, tiled=True)
    attended = attended.reshape(2, rest, own_rows, 2, cols_here)
    attended = jnp.transpose(attended, (2, 0, 3, 1, 4)).reshape(own_rows, width)
    branch_one = dot_f32(attended, w_proj) + vecs[2]
    middle = rows_in + vecs[3] * branch_one
    normed_two, rate_two = norm_parts(middle)
    mlp_in = (normed_two * vecs[4] + vecs[5]).astype(jnp.bfloat16)
    grad_top = grad_moved.reshape(own_rows, width).astype(jnp.float32)
    d_branch2 = (vecs[7] * grad_top).astype(jnp.bfloat16)
    d_fc2_bias = jnp.sum(d_branch2.astype(jnp.float32), axis=0)
    branch_two, d_normed_two, grad_fc1, grad_fc2, d_fc1_bias = mlp(
        mlp_in, d_branch2, weights, fc2_weight.shape[0], bias_fc1[None]
    )
    branch_two = branch_two + vecs[6]
    block_out = (middle + vecs[7] * branch_two).astype(jnp.bfloat16)
    d_scale2 = jnp.sum(grad_top * branch_two, axis=0)
    d_gain2 = jnp.sum(d_normed_two * normed_two, axis=0)
    d_bias2 = jnp.sum(d_normed_two, axis=0)
    d_middle = grad_top + norm_back(normed_two, rate_two, vecs[4], d_normed_two)
    d_scale1 = jnp.sum(d_middle * branch_one, axis=0)
    d_branch1 = (vecs[3] * d_middle).astype(jnp.bfloat16)
    d_proj_bias = jnp.sum(d_branch1.astype(jnp.float32), axis=0)
    grad_fc1 = sum_shards(grad_fc1.reshape(4, rest, *grad_fc1.shape[1:]), "r", 1, jnp.bfloat16)
    grad_fc2 = sum_shards(grad_fc2.reshape(4, rest, *grad_fc2.shape[1:]), "o", 2, jnp.bfloat16)
    block_out = move_out(block_out.reshape(2, rows_here, width))
    d_attended = dot_f32(d_branch1, w_proj, contract_cols).astype(jnp.bfloat16)
    sent = d_attended.reshape(own_rows, 2, 2, rest, cols_here)
    sent = jnp.transpose(sent, (1, 3, 0, 2, 4)).reshape(2 * rest, own_rows, own_cols)
    d_heads = lax.all_to_all(sent, ("c", "r"), split_axis=0, concat_axis=0, tiled=True)
    d_heads = jnp.swapaxes(d_heads.reshape(2, rest, 2, rows_here, own_cols), 1, 2)
    d_heads = d_heads.reshape(tok_count, own_cols)

    split = d_branch1.reshape(own_rows, outer, 2, shard_rows)

    def proj_grad(which):
        mine = lax.dynamic_index_in_dim(split, which, 2, keepdims=False)
        grad = dot_f32(mine.reshape(own_rows, width // 2), attended, contract_rows)
        grad = grad.astype(jnp.bfloat16).reshape(outer, shard_rows, tensor_count, cols_here)
        return jnp.transpose(grad, (2, 0, 1, 3))

    grad_proj = core_sum(proj_grad(c), proj_grad(1 - c))
    d_heads, grad_fc1, grad_fc2, grad_proj = lax.optimization_barrier(
        (d_heads, grad_fc1, grad_fc2, grad_proj)
    )

    grad_fc1 = sum_shards(grad_fc1, "o", 1, jnp.bfloat16)
    grad_fc2 = sum_shards(grad_fc2, "r", 1, jnp.bfloat16)
    grad_proj = sum_shards(grad_proj, "o", 2, jnp.bfloat16)
    groups = own_cols // 128
    d_parts = []
    for group in range(groups):
        d_parts.append(
            attention_back(qkv, bounds, ids_row, ids_col, att_heads, d_heads, lse, group)
        )
        if group == 0:
            d_parts, d_heads, grad_fc1, grad_fc2, grad_proj = lax.optimization_barrier(
                (d_parts, d_heads, grad_fc1, grad_fc2, grad_proj)
            )
            shard_fc1 = sum_shards(grad_fc1, "a", 0, jnp.float32)
            shard_fc2 = sum_shards(grad_fc2, "a", 0, jnp.float32)
            grad_proj = sum_shards(grad_proj, "r", 1, jnp.bfloat16)
    d_parts, grad_proj = lax.optimization_barrier((d_parts, grad_proj))

    shard_proj = sum_shards(grad_proj, "a", 0, jnp.float32)
    d_qkv = jnp.concatenate([part[i] for i in range(3) for part in d_parts], axis=1)
    d_rows = dot_f32(d_qkv, w_qkv, contract_cols).astype(jnp.bfloat16)
    d_rows = sum_shards(d_rows.reshape(2, 2, rest, rows_here, width), "c", 0, jnp.bfloat16)
    d_w_qkv = dot_f32(normed_all_low, d_qkv, contract_rows).astype(jnp.bfloat16)
    d_bias_qkv = jnp.sum(d_qkv.astype(jnp.float32), axis=0).reshape(3, 2, cols_here)
    d_bias_qv = jnp.stack([d_bias_qkv[0], d_bias_qkv[2]])
    d_rows, d_w_qkv, d_bias_qv = lax.optimization_barrier((d_rows, d_w_qkv, d_bias_qv))

    d_w_qkv = sum_shards(
        d_w_qkv.reshape(outer, 2, shard_rows, 3, 2, cols_here), "o", 0, jnp.bfloat16
    )
    d_normed_one = sum_shards(d_rows, "r", 1, jnp.float32).reshape(own_rows, width)
    d_w_qkv = jnp.transpose(d_w_qkv, (0, 3, 2, 1, 4)).reshape(4, 3, shard_rows, cols_here)
    shard_qkv = 0.0
    for step in range(4):
        pairs = []
        for core in range(2):
            for seq in range(4):
                k = (seq + step) % 4
                pairs.append((core * 4 + seq, (k // 2) * 4 + 2 * core + k % 2))
        got = lax.ppermute(pick(d_w_qkv, (a + step) % 4), ("c", "a"), pairs)
        shard_qkv = shard_qkv + got.astype(jnp.float32)
    d_gain1 = jnp.sum(d_normed_one * normed_one, axis=0)
    d_bias1 = jnp.sum(d_normed_one, axis=0)
    input_grad = d_middle + norm_back(normed_one, rate_one, vecs[0], d_normed_one)
    spread_qv = jnp.zeros((2, 2, 2, rest, cols_here), jnp.float32)
    spread_qv = lax.dynamic_update_slice(
        spread_qv, d_bias_qv[:, None, :, None], (0, c, 0, r, 0)
    )
    lines = [d_gain1, d_bias1, d_proj_bias, d_scale1, d_gain2, d_bias2, d_fc2_bias, d_scale2]
    lines = jnp.stack(lines).reshape(8, dp_count, shard_rows)
    fc1_lines = d_fc1_bias.reshape(tensor_count, dp_count, fc1_short)
    fc1_lines = jnp.swapaxes(fc1_lines, 0, 1).reshape(dp_count, -1, shard_rows)
    qv_lines = spread_qv.reshape(2, tensor_count, dp_count, short)
    qv_lines = jnp.moveaxis(qv_lines, 2, 0).reshape(dp_count, -1, shard_rows)
    sums = jnp.concatenate([jnp.swapaxes(lines, 0, 1), fc1_lines, qv_lines], axis=1)
    sums = jnp.pad(sums, ((0, 0), (0, -sums.shape[1] % 8), (0, 0)))
    vec_sums, input_grad = leave(
        sums, input_grad.astype(jnp.bfloat16).reshape(2, rows_here, width)
    )
    place = a * rest + r
    fc1_rows = fc1_lines.shape[1]
    grad_fc1_bias = vec_sums[8 : 8 + fc1_rows].reshape(tensor_count, fc1_short)
    grad_fc1_bias = pick(grad_fc1_bias, place)
    grad_qv_bias = vec_sums[8 + fc1_rows : 8 + fc1_rows + qv_lines.shape[1]]
    grad_qv_bias = lax.dynamic_index_in_dim(
        grad_qv_bias.reshape(2, tensor_count, short), place, 1, keepdims=False
    )
    return (
        block_out,
        input_grad,
        vec_sums[0],
        vec_sums[1],
        shard_qkv,
        grad_qv_bias,
        shard_proj.T,
        vec_sums[2],
        vec_sums[3],
        vec_sums[4],
        vec_sums[5],
        shard_fc1,
        grad_fc1_bias,
        shard_fc2.T,
        vec_sums[6],
        vec_sums[7],
    )


def solution(mesh):
    dp, tensor = ("o", "c"), ("a", "r")
    dp_count, tensor_count = mesh.devices.shape
    finer = Mesh(mesh.devices.reshape(dp_count // 2, 2, 4, tensor_count // 4), everywhere)
    rows = P(None, everywhere, None)
    vec = P(dp)
    in_specs = (
        rows, P(None, dp, None), rows, vec, vec, P(None, dp, tensor), P(None, tensor + dp),
        P(tensor, dp), vec, vec, vec, vec, P(dp, tensor), P(tensor + dp), P(tensor, dp), vec, vec,
    )
    out_specs = (
        rows, rows, vec, vec, P(None, dp, tensor), P(None, tensor + dp), P(tensor, dp), vec, vec,
        vec, vec, P(dp, tensor), P(tensor + dp), P(tensor, dp), vec, vec,
    )
    return jax.shard_map(body, mesh=finer, in_specs=in_specs, out_specs=out_specs, check_vma=False)
```

time: 1110 us -> 704 us (0.63)
  waiting for transfers between devices: 553 us -> 53.5 us
  Pallas kernels: 125 us -> 350 us
  blocking collectives: 88.5 us -> 0 us
  matrix products: 117 us -> 31.2 us
  starting transfers between devices: 14.7 us -> 71.3 us
  local copies, waits for them, and re-layouts: 165 us -> 112 us
  other arithmetic: 22.5 us -> 63.3 us
    all_to_all x3 -> x2, waiting for transfers between devices: 276 us -> 27.5 us  [body(): lax.all_to_all(sent, ('c', 'r'), split_axis=0, concat_axis=0, tiled=True)]
    pallas_call x0 -> x3, Pallas kernels: none -> 206 us  [the longest x1 102 us: entry(): pl.pallas_call(lambda *refs: entry_kernel(outer_count, rest_count, *refs)...]
    reduce_scatter x6 -> x0, waiting for transfers between devices: 135 us -> none  [the longest x2 87 us: scatter_matrix(): lax.psum_scatter(part, 'tensor', scatter_dimension=1, tiled=True)]
    dot_general x12 -> x7, matrix products: 117 us -> 31.2 us  [dot_f32(): lax.dot_general(left, right, dims, preferred_element_type=jnp.float32)]
    all_gather x4 -> x1, waiting for transfers between devices: 74.4 us -> 0.01 us  [gather_parts(): parts = lax.all_gather(shard, everywhere, axis=0, tiled=False)]
    unnamed x14 -> x1, waiting for transfers between devices: 68.1 us -> 0.02 us
    ppermute x0 -> x27, starting transfers between devices: none -> 50 us  [the longest x18 27.9 us: sum_shards(): lax.ppermute(block((me + step) % count), axis, place_shift(step, count))]
    concatenate x3 -> x2, local copies, waits for them, and re-layouts: 44.8 us -> 1.4 us  [the longest x1 1.21 us: body(): jnp.concatenate([vectors, small])]
  transfers between devices with their start and end apart: 15 -> 30, of which waited for: 9 -> 7; matrix products, arithmetic and copies ran while one was open for 18% -> 19% of each run, Pallas kernels for 11% -> 35%
where the time goes in v1:
time: 704 us; the launch traced here: 696 us
  Pallas kernels  350 us (50%)
  local copies, waits for them, and re-layouts  112 us (16%)
  starting transfers between devices  71.3 us (10%)
  other arithmetic  63.3 us (9%)
  waiting for transfers between devices  53.5 us (8%)
  matrix products  31.2 us (4%)
  between operations  15.4 us (2%)
    pallas_call x1, Pallas kernels, entry(): pl.pallas_call(lambda *refs: entry_kernel(outer_count, rest_count, *refs)...  102 us
    pallas_call x2, Pallas kernels, attention_back(): pl.pallas_call(backward_kernel, grid_spec=pltpu.PrefetchScalarGridSpec(nu...  80.6 us
    pallas_call x1, Pallas kernels, attention(): pl.pallas_call(forward_kernel, grid_spec=pltpu.PrefetchScalarGridSpec(num...  63.1 us
    pallas_call x1, Pallas kernels, mlp(): pl.pallas_call(mlp_kernel, grid=(tensor_count + 1,), in_specs=[whole, who...  59.7 us
    pallas_call x1, Pallas kernels, leave(): pl.pallas_call(lambda *refs: exit_kernel(outer_count, rest_count, *refs),...  44.7 us
    dot_general x7, matrix products, dot_f32(): lax.dot_general(left, right, dims, preferred_element_type=jnp.float32)  31.2 us
    ppermute x18, starting transfers between devices, sum_shards(): lax.ppermute(block((me + step) % count), axis, place_shift(step, count))  27.9 us
    all_to_all x2, waiting for transfers between devices, body(): lax.all_to_all(sent, ('c', 'r'), split_axis=0, concat_axis=0, tiled=True)  27.5 us
  transfers between devices with their start and end apart: 30, of which 7 were waited for; matrix products, arithmetic and copies ran while one was open for 19% of the time, Pallas kernels for 35%

profile of v1, /device:TPU:0, one launch (start us, length us, event | category | flops | bytes accessed | tf_op | source)
XLA Modules:
  0.0 696.4 jit_solution(7039818006454877641)
XLA Ops:
  18.3 101.8 %shard_map.288 = (bf16[3072,1024]{1,0:T(8,128)(2,1)}, bf16[2,3,1024,128]{3,2,1,0:T(8,128)(2,1)}, bf16[8,4,16,256]{3,2,1,0:T(8,128)(2,1)}, s32[2,2,1,3072]{3,2,1,0:T(1,128)}) custom-call(bf16[2,384,1024]{2,1,0:T(8,128)(2,1)} %refs_0_.1, bf16[3,256,128]{2,1,0:T(8,128)(2,1)} %refs_1_.1, bf16[16,256]{1,0:T(8,128)(2,1)} %concatenate.20.refs_2_, s32[2,1,3072]{2,1,0:T(1,128)} %refs_3_.1), custom_call_target="tpu_custom_call" | custom-call | bytes 209715200 | tf_op jit(solution)/shard_map/pallas_call | solution.py:436
  121.5 7.5 %collective-permute-start = (bf16[384,1024]{1,0:T(8,128)(2,1)}, bf16[384,1024]{1,0:T(8,128)(2,1)}, u32[]{:S(2)}, u32[]{:S(2)}) collective-permute-start(bf16[384,1024]{1,0:T(8,128)(2,1)} %get-tuple-element.191), channel_id=1, source_target_pairs={{0,0},{2,4},{4,8},{6,12},{8,2},{10,6},{12,10},{14,14},{1,1},{3,5},... | collective-permute-start | bytes 2359304 | tf_op jit(solution)/shard_map/ppermute | solution.py:731
  134.9 3.9 convert_reduce_fusion
  142.5 7.1 %multiply_convert_fusion.q_ref.k_ref.v_ref = bf16[3072,768]{1,0:T(8,128)(2,1)S(1)} fusion(bf16[1024,768]{0,1:T(8,128)(2,1)S(1)} %bitcast.318, f32[768]{0:T(1024)S(1)} %copy-done.35, f32[768]{0:T(1024)S(1)} %pad_maximum_fusion.3, bf16[3072,1024]{1,0:T(8,128)(2,1)S(1)} %copy-done.1, f32[1024]{0:T(1024)S(1)} %bitcast.365, f32[1024]{0:T(1024)S(1)} %bitcast.344, ...), kind=kOutput, calls=%fused_computation.9 | convolution fusion | flops 4857790464 | bytes 12621824 | tf_op jit(solution)/shard_map/dot_general | solution.py:20
  149.7 63.1 %shard_map.289 = (bf16[3072,256]{1,0:T(8,128)(2,1)S(1)}, f32[2,6,2,512]{3,2,1,0:T(2,128)S(1)}) custom-call(s32[6]{0:T(128)S(1)} %get-tuple-element.226.low_ref, s32[6]{0:T(128)S(1)} %get-tuple-element.225.high_ref, bf16[3072,768]{1,0:T(8,128)(2,1)S(1)} %multiply_convert_fusion.q_ref.k_ref.v_ref, ...), custom_call_target="tpu_custom_call" | custom-call | flops 38654705664 | bytes 4718592 | tf_op jit(solution)/shard_map/pallas_call | solution.py:154
  214.1 16.9 %all-to-all-start = ((bf16[4,768,256]{2,1,0:T(8,128)(2,1)}), bf16[4,768,256]{2,1,0:T(8,128)(2,1)}, u32[]{:S(2)}, u32[]{:S(2)}) async-start(bf16[4,768,256]{2,1,0:T(8,128)(2,1)} %bitcast.303), calls=%async_computation | async-start | bytes 3145728 | tf_op jit(solution)/shard_map/all_to_all | solution.py:834
  240.3 10.7 %all-to-all-done = bf16[4,768,256]{2,1,0:T(8,128)(2,1)} async-done(((bf16[4,768,256]{2,1,0:T(8,128)(2,1)}), bf16[4,768,256]{2,1,0:T(8,128)(2,1)}, u32[]{:S(2)}, u32[]{:S(2)}) %all-to-all-start) | async-done | bytes 1572896 | tf_op jit(solution)/shard_map/all_to_all | solution.py:834
  251.0 3.5 reshape.375
  254.5 4.9 copy.103
  259.4 3.1 slice_bitcast_fusion
  262.5 4.3 copy.105
  266.8 6.1 fusion.54
  275.1 59.7 %shard_map.290 = (f32[768,1024]{1,0:T(8,128)}, f32[768,1024]{1,0:T(8,128)}, bf16[8,2,256,512]{3,2,1,0:T(8,128)(2,1)}, bf16[8,2,256,512]{3,2,1,0:T(8,128)(2,1)}, f32[1,4096]{1,0:T(1,128)}) custom-call(bf16[768,1024]{1,0:T(8,128)(2,1)} %add_convert_fusion.1.h_ref, bf16[768,1024]{1,0:T(8,128)(2,1)} %fusion.16.dm_ref, bf16[4,8,1152,256]{3,2,1,0:T(8,128)(2,1)} %bitcast.331, ...), custom_call_target="tpu_custom_call" | custom-call | flops 38654705664 | bytes 67108864 | tf_op jit(solution)/shard_map/pallas_call | solution.py:676
  334.8 4.2 multiply_reduce_fusion
  339.1 6.1 fusion.17
  348.5 3.9 reshape.386
  352.3 6.8 constant_dynamic-slice_fusion.6
  359.1 4.7 copy.132
  363.8 4.6 constant_dynamic-slice_fusion.9
  368.4 4.2 copy.112
  372.6 3.9 constant_dynamic-slice_fusion.11
  382.3 2.9 fusion.35
  385.2 3.8 reshape.380
  389.0 5.0 copy.106
  393.9 4.3 all-to-all-start.1
  400.1 4.7 copy.131
  409.2 4.2 copy.130
  413.4 2.8 dynamic-slice_bitcast_fusion.4
  416.2 7.4 %collective-permute-start.2 = (bf16[384,1024]{1,0:T(8,128)(2,1)}, bf16[384,1024]{1,0:T(8,128)(2,1)}, u32[]{:S(2)}, u32[]{:S(2)}) collective-permute-start(bf16[384,1024]{1,0:T(8,128)(2,1)} %get-tuple-element.187), channel_id=1, source_target_pairs={{0,0},{4,2},{8,4},{12,6},{2,8},{6,10},{10,12},{14,14},{1,1},{5,3},... | collective-permute-start | bytes 2359304 | tf_op jit(solution)/shard_map/ppermute | solution.py:740
  426.3 16.8 %all-to-all-done.1 = bf16[4,768,256]{1,2,0:T(8,128)(2,1)} async-done(((bf16[4,768,256]{1,2,0:T(8,128)(2,1)}), bf16[4,768,256]{1,2,0:T(8,128)(2,1)}, u32[]{:S(2)}, u32[]{:S(2)}) %all-to-all-start.1) | async-done | bytes 1572896 | tf_op jit(solution)/shard_map/all_to_all | solution.py:862
  443.1 2.7 copy.107
  445.9 2.8 copy.108
  455.8 40.3 %shard_map.291 = (bf16[3072,128]{1,0:T(8,128)(2,1)S(1)}, bf16[3072,128]{1,0:T(8,128)(2,1)S(1)}, bf16[3072,128]{1,0:T(8,128)(2,1)S(1)}) custom-call(s32[6]{0:T(128)S(1)} %get-tuple-element.226.low_ref, s32[6]{0:T(128)S(1)} %get-tuple-element.225.high_ref, bf16[3072,768]{1,0:T(8,128)(2,1)} %copy-done, bf16[3072,768]{1,0:T(8,128)(2,1)} %copy-done, ...), custom_call_target="tpu_custom_call" | custom-call | flops 24159191040 | bytes 9437184 | tf_op jit(solution)/shard_map/pallas_call | solution.py:182
  500.1 40.3 %shard_map.292 = (bf16[3072,128]{1,0:T(8,128)(2,1)S(1)}, bf16[3072,128]{1,0:T(8,128)(2,1)S(1)}, bf16[3072,128]{1,0:T(8,128)(2,1)S(1)}) custom-call(s32[6]{0:T(128)S(1)} %get-tuple-element.226.low_ref, s32[6]{0:T(128)S(1)} %get-tuple-element.225.high_ref, bf16[3072,768]{1,0:T(8,128)(2,1)} %copy-done, bf16[3072,768]{1,0:T(8,128)(2,1)} %copy-done, ...), custom_call_target="tpu_custom_call" | custom-call | flops 24159191040 | bytes 9437184 | tf_op jit(solution)/shard_map/pallas_call | solution.py:182
  542.2 5.3 convolution_convert_fusion
  553.1 3.5 collective-permute-start.26
  557.4 6.0 convolution_convert_fusion.1
  563.5 3.3 fusion.6
  571.8 2.8 collective-permute-done.25
  574.6 5.8 collective-permute-start.23
  582.5 11.6 %collective-permute-start.18 = (bf16[256,128]{1,0:T(8,128)(2,1)S(1)}, bf16[256,128]{1,0:T(8,128)(2,1)S(1)}, u32[]{:S(2)}, u32[]{:S(2)}) collective-permute-start(bf16[256,128]{1,0:T(8,128)(2,1)S(1)} %get-tuple-element.203), channel_id=1, source_target_pairs={{0,2},{2,4},{4,6},{6,0},{1,3},{3,5},{5,7},{7,1},{8,10},{10,12},{12... | collective-permute-start | bytes 196616 | tf_op jit(solution)/shard_map/ppermute | solution.py:755
  594.1 3.6 collective-permute-done.22
  597.7 5.9 collective-permute-done.23
  613.5 7.5 %collective-permute-done.15 = bf16[3,256,128]{2,1,0:T(8,128)(2,1)S(1)} collective-permute-done((bf16[3,256,128]{2,1,0:T(8,128)(2,1)S(1)}, bf16[3,256,128]{2,1,0:T(8,128)(2,1)S(1)}, u32[]{:S(2)}, u32[]{:S(2)}) %collective-permute-start.15) | collective-permute-done | bytes 196640 | tf_op jit(solution)/shard_map/ppermute | solution.py:918
  621.0 6.1 collective-permute-done.16
  628.0 4.4 fusion.21
  633.1 4.7 fusion.13
  637.8 44.7 %shard_map.293 = (f32[16,256]{1,0:T(8,128)}, bf16[2,384,1024]{2,1,0:T(8,128)(2,1)}) custom-call(f32[4,16,256]{2,1,0:T(8,128)} %select_maximum_fusion.refs_0_, bf16[2,384,1024]{2,1,0:T(8,128)(2,1)} %bitcast.306), custom_call_target="tpu_custom_call" | custom-call | bytes 125829120 | tf_op jit(solution)/shard_map/pallas_call | solution.py:565
  (246 shorter events, 96.9 us)
Async XLA Ops:
  7.2 113.0 %copy-start.18 = (bf16[2,384,1024]{2,1,0:T(8,128)(2,1)S(1)}, bf16[2,384,1024]{2,1,0:T(8,128)(2,1)}, u32[]{:S(2)}) copy-start(bf16[2,384,1024]{2,1,0:T(8,128)(2,1)} %param.19) | copy-start | bytes 4718596
  7.2 252.2 %all-gather.3.cloned.1.call-start = ((), (), s32[]{:S(2)}) async-start(), calls=%async_computation.2 | async-start | bytes 19464192 | tf_op jit(solution)/shard_map/all_gather | solution.py:706
  121.5 114.5 %collective-permute-start = (bf16[384,1024]{1,0:T(8,128)(2,1)}, bf16[384,1024]{1,0:T(8,128)(2,1)}, u32[]{:S(2)}, u32[]{:S(2)}) collective-permute-start(bf16[384,1024]{1,0:T(8,128)(2,1)} %get-tuple-element.191), channel_id=1, source_target_pairs={{0,0},{2,4},{4,8},{6,12},{8,2},{10,6},{12,10},{14,14},{1,1},{3,5},... | collective-permute-start | bytes 2359304 | tf_op jit(solution)/shard_map/ppermute | solution.py:731
  129.0 107.0 %collective-permute-start.1 = (bf16[384,1024]{1,0:T(8,128)(2,1)}, bf16[384,1024]{1,0:T(8,128)(2,1)}, u32[]{:S(2)}, u32[]{:S(2)}) collective-permute-start(bf16[384,1024]{1,0:T(8,128)(2,1)} %get-tuple-element.192), channel_id=1, source_target_pairs={{0,4},{2,0},{4,12},{6,8},{8,6},{10,2},{12,14},{14,10},{1,5},{3,1},... | collective-permute-start | bytes 2359304 | tf_op jit(solution)/shard_map/ppermute | solution.py:731
  134.4 8.1 %copy-start.19 = (bf16[1024,3,2,128]{0,3,2,1:T(8,128)(2,1)}, bf16[1024,3,2,128]{0,3,2,1:T(8,128)(2,1)S(1)}, u32[]{:S(2)}) copy-start(bf16[1024,3,2,128]{0,3,2,1:T(8,128)(2,1)S(1)} %copy.100) | copy-start | bytes 4718596
  134.9 4.7 copy-start.1
  141.7 8.0 %copy-start.31 = (f32[3072]{0:T(1024)}, f32[3072]{0:T(1024)S(1)}, u32[]{:S(2)}) copy-start(f32[3072]{0:T(1024)S(1)} %add_rsqrt_fusion) | copy-start | bytes 36868
  142.5 7.2 %copy-start.27 = (f32[1,4,256]{2,0,1:T(1,128)}, f32[1,4,256]{2,0,1:T(1,128)S(1)}, u32[]{:S(2)}) copy-start(f32[1,4,256]{2,0,1:T(1,128)S(1)} %get-tuple-element.212) | copy-start | bytes 12292
  142.5 7.2 %copy-start.33 = (f32[1,4,256]{2,0,1:T(1,128)}, f32[1,4,256]{2,0,1:T(1,128)S(1)}, u32[]{:S(2)}) copy-start(f32[1,4,256]{2,0,1:T(1,128)S(1)} %get-tuple-element.211) | copy-start | bytes 12292
  149.7 63.1 %copy-start = (bf16[3072,768]{1,0:T(8,128)(2,1)}, bf16[3072,768]{1,0:T(8,128)(2,1)S(1)}, u32[]{:S(2)}) copy-start(bf16[3072,768]{1,0:T(8,128)(2,1)S(1)} %multiply_convert_fusion.q_ref.k_ref.v_ref) | copy-start | bytes 14155780
  214.1 36.9 %all-to-all-start = ((bf16[4,768,256]{2,1,0:T(8,128)(2,1)}), bf16[4,768,256]{2,1,0:T(8,128)(2,1)}, u32[]{:S(2)}, u32[]{:S(2)}) async-start(bf16[4,768,256]{2,1,0:T(8,128)(2,1)} %bitcast.303), calls=%async_computation | async-start | bytes 3145728 | tf_op jit(solution)/shard_map/all_to_all | solution.py:834
  233.4 6.9 copy-start.23
  372.6 76.1 %collective-permute-start.5 = (bf16[4,2,256,512]{2,3,0,1:T(8,128)(2,1)}, bf16[4,2,256,512]{2,3,0,1:T(8,128)(2,1)}, u32[]{:S(2)}, u32[]{:S(2)}) collective-permute-start(bf16[4,2,256,512]{2,3,0,1:T(8,128)(2,1)} %bitcast.315), channel_id=1, source_target_pairs={{0,16},{16,0},{1,17},{17,1},{2,18},{18,2},{3,19},{19,3},{4,20},{20... | collective-permute-start | bytes 6291464 | tf_op jit(solution)/shard_map/ppermute | solution.py:755
  378.0 73.0 %collective-permute-start.4 = (bf16[4,2,256,512]{3,2,0,1:T(8,128)(2,1)}, bf16[4,2,256,512]{3,2,0,1:T(8,128)(2,1)}, u32[]{:S(2)}, u32[]{:S(2)}) collective-permute-start(bf16[4,2,256,512]{3,2,0,1:T(8,128)(2,1)} %bitcast.283), channel_id=1, source_target_pairs={{0,1},{1,0},{2,3},{3,2},{4,5},{5,4},{6,7},{7,6},{8,9},{9,8},{10,11... | collective-permute-start | bytes 6291464 | tf_op jit(solution)/shard_map/ppermute | solution.py:755
  381.3 42.3 %collective-permute-start.6 = (bf16[8,2,256,128]{3,2,1,0:T(8,128)(2,1)}, bf16[8,2,256,128]{3,2,1,0:T(8,128)(2,1)}, u32[]{:S(2)}, u32[]{:S(2)}) collective-permute-start(bf16[8,2,256,128]{3,2,1,0:T(8,128)(2,1)} %bitcast.284), channel_id=1, source_target_pairs={{0,8},{8,0},{1,9},{9,1},{2,10},{10,2},{3,11},{11,3},{4,12},{12,4},... | collective-permute-start | bytes 3145736 | tf_op jit(solution)/shard_map/ppermute | solution.py:765
  393.9 49.2 %all-to-all-start.1 = ((bf16[4,768,256]{1,2,0:T(8,128)(2,1)}), bf16[4,768,256]{1,2,0:T(8,128)(2,1)}, u32[]{:S(2)}, u32[]{:S(2)}) async-start(bf16[4,768,256]{1,2,0:T(8,128)(2,1)} %bitcast.305), calls=%async_computation.1 | async-start | bytes 3145728 | tf_op jit(solution)/shard_map/all_to_all | solution.py:862
  413.4 10.2 %copy-start.12 = (f32[64,8,8,128]{3,2,1,0:T(8,128)S(1)}, f32[64,8,8,128]{3,2,1,0:T(8,128)}, u32[]{:S(2)}) copy-start(f32[64,8,8,128]{3,2,1,0:T(8,128)} %copy.137) | copy-start | bytes 6291460
  416.2 132.5 %collective-permute-start.2 = (bf16[384,1024]{1,0:T(8,128)(2,1)}, bf16[384,1024]{1,0:T(8,128)(2,1)}, u32[]{:S(2)}, u32[]{:S(2)}) collective-permute-start(bf16[384,1024]{1,0:T(8,128)(2,1)} %get-tuple-element.187), channel_id=1, source_target_pairs={{0,0},{4,2},{8,4},{12,6},{2,8},{6,10},{10,12},{14,14},{1,1},{5,3},... | collective-permute-start | bytes 2359304 | tf_op jit(solution)/shard_map/ppermute | solution.py:740
  423.6 125.1 %collective-permute-start.3 = (bf16[384,1024]{1,0:T(8,128)(2,1)}, bf16[384,1024]{1,0:T(8,128)(2,1)}, u32[]{:S(2)}, u32[]{:S(2)}) collective-permute-start(bf16[384,1024]{1,0:T(8,128)(2,1)} %get-tuple-element.188), channel_id=1, source_target_pairs={{4,0},{0,2},{12,4},{8,6},{6,8},{2,10},{14,12},{10,14},{5,1},{1,3},... | collective-permute-start | bytes 2359304 | tf_op jit(solution)/shard_map/ppermute | solution.py:740
  453.4 42.7 %collective-permute-start.9 = (bf16[4,2,256,128]{3,2,1,0:T(8,128)(2,1)S(1)}, bf16[4,2,256,128]{3,2,1,0:T(8,128)(2,1)S(1)}, u32[]{:S(2)}, u32[]{:S(2)}) collective-permute-start(bf16[4,2,256,128]{3,2,1,0:T(8,128)(2,1)S(1)} %dynamic-slice_bitcast_fusion.7), channel_id=1, source_target_pairs={{0,16},{16,0},{1,17},{17,1},{2,18},{18,2},{3,19},{19,3},{4,20},{20... | collective-permute-start | bytes 1572872 | tf_op jit(solution)/shard_map/ppermute | solution.py:755
  455.3 41.0 %collective-permute-start.8 = (bf16[4,256,512]{1,2,0:T(8,128)(2,1)S(1)}, bf16[4,256,512]{1,2,0:T(8,128)(2,1)S(1)}, u32[]{:S(2)}, u32[]{:S(2)}) collective-permute-start(bf16[4,256,512]{1,2,0:T(8,128)(2,1)S(1)} %dynamic-slice_bitcast_fusion.1), channel_id=1, source_target_pairs={{0,1},{1,0},{2,3},{3,2},{4,5},{5,4},{6,7},{7,6},{8,9},{9,8},{10,11... | collective-permute-start | bytes 3145736 | tf_op jit(solution)/shard_map/ppermute | solution.py:755
  455.5 41.1 %collective-permute-start.7 = (bf16[4,256,512]{2,1,0:T(8,128)(2,1)S(1)}, bf16[4,256,512]{2,1,0:T(8,128)(2,1)S(1)}, u32[]{:S(2)}, u32[]{:S(2)}) collective-permute-start(bf16[4,256,512]{2,1,0:T(8,128)(2,1)S(1)} %dynamic-slice_bitcast_fusion.2), channel_id=1, source_target_pairs={{0,16},{16,0},{1,17},{17,1},{2,18},{18,2},{3,19},{19,3},{4,20},{20... | collective-permute-start | bytes 3145736 | tf_op jit(solution)/shard_map/ppermute | solution.py:755
  496.6 55.1 %copy-start.15 = (bf16[4,256,512]{1,2,0:T(8,128)(2,1)}, bf16[4,256,512]{1,2,0:T(8,128)(2,1)S(1)}, u32[]{:S(2)}) copy-start(bf16[4,256,512]{1,2,0:T(8,128)(2,1)S(1)} %fusion.30) | copy-start | bytes 3145732
  498.1 42.3 %collective-permute-start.10 = (bf16[4,256,128]{2,1,0:T(8,128)(2,1)S(1)}, bf16[4,256,128]{2,1,0:T(8,128)(2,1)S(1)}, u32[]{:S(2)}, u32[]{:S(2)}) collective-permute-start(bf16[4,256,128]{2,1,0:T(8,128)(2,1)S(1)} %dynamic-slice_bitcast_fusion.14), channel_id=1, source_target_pairs={{0,1},{1,0},{2,3},{3,2},{4,5},{5,4},{6,7},{7,6},{8,9},{9,8},{10,11... | collective-permute-start | bytes 786440 | tf_op jit(solution)/shard_map/ppermute | solution.py:755
  548.3 9.1 %slice-start = ((s8[6291456]{0:T(1024)(128)(4,1)}), s8[4194304]{0:T(1024)(128)(4,1)S(1)}, s32[]{:S(2)}) async-start(s8[6291456]{0:T(1024)(128)(4,1)} %bitcast.299), calls=%async_computation.3 | async-start | bytes 8388608
  548.6 14.9 %collective-permute-start.11 = (bf16[2,2,384,1024]{3,2,0,1:T(8,128)(2,1)S(1)}, bf16[2,2,384,1024]{3,2,0,1:T(8,128)(2,1)S(1)}, u32[]{:S(2)}, u32[]{:S(2)}) collective-permute-start(bf16[2,2,384,1024]{3,2,0,1:T(8,128)(2,1)S(1)} %bitcast.313), channel_id=1, source_target_pairs={{0,8},{8,0},{1,9},{9,1},{2,10},{10,2},{3,11},{11,3},{4,12},{12,4},... | collective-permute-start | bytes 9437192 | tf_op jit(solution)/shard_map/ppermute | solution.py:755
  550.4 7.0 %slice-start.1 = ((s8[6291456]{0:T(1024)(128)(4,1)}), s8[2097152]{0:T(1024)(128)(4,1)S(1)}, s32[]{:S(2)}) async-start(s8[6291456]{0:T(1024)(128)(4,1)} %bitcast.299), calls=%async_computation.4 | async-start | bytes 4194304
  551.7 5.7 copy-start.26
  551.7 5.7 copy-start.28
  551.7 5.7 copy-start.32
  551.7 5.7 copy-start.34
  552.6 17.8 %collective-permute-start.24 = (bf16[256,512]{0,1:T(8,128)(2,1)}, bf16[256,512]{0,1:T(8,128)(2,1)}, u32[]{:S(2)}, u32[]{:S(2)}) collective-permute-start(bf16[256,512]{0,1:T(8,128)(2,1)} %get-tuple-element.193), channel_id=1, source_target_pairs={{0,2},{2,4},{4,6},{6,0},{1,3},{3,5},{5,7},{7,1},{8,10},{10,12},{12... | collective-permute-start | bytes 786440 | tf_op jit(solution)/shard_map/ppermute | solution.py:755
  553.1 21.5 %collective-permute-start.25 = (bf16[256,512]{0,1:T(8,128)(2,1)}, bf16[256,512]{0,1:T(8,128)(2,1)}, u32[]{:S(2)}, u32[]{:S(2)}) collective-permute-start(bf16[256,512]{0,1:T(8,128)(2,1)} %get-tuple-element.195), channel_id=1, source_target_pairs={{0,4},{2,6},{4,0},{6,2},{1,5},{3,7},{5,1},{7,3},{8,12},{10,14},{12... | collective-permute-start | bytes 786440 | tf_op jit(solution)/shard_map/ppermute | solution.py:755
  553.1 21.5 %collective-permute-start.26 = (bf16[256,512]{0,1:T(8,128)(2,1)}, bf16[256,512]{0,1:T(8,128)(2,1)}, u32[]{:S(2)}, u32[]{:S(2)}) collective-permute-start(bf16[256,512]{0,1:T(8,128)(2,1)} %get-tuple-element.194), channel_id=1, source_target_pairs={{0,6},{2,0},{4,2},{6,4},{1,7},{3,1},{5,3},{7,5},{8,14},{10,8},{12,... | collective-permute-start | bytes 786440 | tf_op jit(solution)/shard_map/ppermute | solution.py:755
  568.4 36.1 %collective-permute-start.13 = (bf16[2,256,3,2,128]{4,1,2,3,0:T(8,128)(2,1)S(1)}, bf16[2,256,3,2,128]{4,1,2,3,0:T(8,128)(2,1)S(1)}, u32[]{:S(2)}, u32[]{:S(2)}) collective-permute-start(bf16[2,256,3,2,128]{4,1,2,3,0:T(8,128)(2,1)S(1)} %bitcast.327), channel_id=1, source_target_pairs={{0,16},{16,0},{1,17},{17,1},{2,18},{18,2},{3,19},{19,3},{4,20},{20... | collective-permute-start | bytes 2359304 | tf_op jit(solution)/shard_map/ppermute | solution.py:755
  570.3 57.6 %collective-permute-start.12 = (bf16[2,384,1024]{2,1,0:T(8,128)(2,1)}, bf16[2,384,1024]{2,1,0:T(8,128)(2,1)S(1)}, u32[]{:S(2)}, u32[]{:S(2)}) collective-permute-start(bf16[2,384,1024]{2,1,0:T(8,128)(2,1)} %dynamic-slice_bitcast_fusion), channel_id=1, source_target_pairs={{0,1},{1,0},{2,3},{3,2},{4,5},{5,4},{6,7},{7,6},{8,9},{9,8},{10,11... | collective-permute-start | bytes 4718600 | tf_op jit(solution)/shard_map/ppermute | solution.py:755
  570.4 12.1 %collective-permute-start.21 = (bf16[256,512]{1,0:T(8,128)(2,1)S(1)}, bf16[256,512]{1,0:T(8,128)(2,1)S(1)}, u32[]{:S(2)}, u32[]{:S(2)}) collective-permute-start(bf16[256,512]{1,0:T(8,128)(2,1)S(1)} %get-tuple-element.196), channel_id=1, source_target_pairs={{0,2},{2,4},{4,6},{6,0},{1,3},{3,5},{5,7},{7,1},{8,10},{10,12},{12... | collective-permute-start | bytes 786440 | tf_op jit(solution)/shard_map/ppermute | solution.py:755
  574.6 23.1 %collective-permute-start.22 = (bf16[256,512]{1,0:T(8,128)(2,1)S(1)}, bf16[256,512]{1,0:T(8,128)(2,1)S(1)}, u32[]{:S(2)}, u32[]{:S(2)}) collective-permute-start(bf16[256,512]{1,0:T(8,128)(2,1)S(1)} %get-tuple-element.198), channel_id=1, source_target_pairs={{0,4},{2,6},{4,0},{6,2},{1,5},{3,7},{5,1},{7,3},{8,12},{10,14},{12... | collective-permute-start | bytes 786440 | tf_op jit(solution)/shard_map/ppermute | solution.py:755
  574.6 29.0 %collective-permute-start.23 = (bf16[256,512]{1,0:T(8,128)(2,1)S(1)}, bf16[256,512]{1,0:T(8,128)(2,1)S(1)}, u32[]{:S(2)}, u32[]{:S(2)}) collective-permute-start(bf16[256,512]{1,0:T(8,128)(2,1)S(1)} %get-tuple-element.197), channel_id=1, source_target_pairs={{0,6},{2,0},{4,2},{6,4},{1,7},{3,1},{5,3},{7,5},{8,14},{10,8},{12,... | collective-permute-start | bytes 786440 | tf_op jit(solution)/shard_map/ppermute | solution.py:755
  582.5 24.5 %collective-permute-start.18 = (bf16[256,128]{1,0:T(8,128)(2,1)S(1)}, bf16[256,128]{1,0:T(8,128)(2,1)S(1)}, u32[]{:S(2)}, u32[]{:S(2)}) collective-permute-start(bf16[256,128]{1,0:T(8,128)(2,1)S(1)} %get-tuple-element.203), channel_id=1, source_target_pairs={{0,2},{2,4},{4,6},{6,0},{1,3},{3,5},{5,7},{7,1},{8,10},{10,12},{12... | collective-permute-start | bytes 196616 | tf_op jit(solution)/shard_map/ppermute | solution.py:755
  597.7 11.4 %collective-permute-start.19 = (bf16[256,128]{1,0:T(8,128)(2,1)S(1)}, bf16[256,128]{1,0:T(8,128)(2,1)S(1)}, u32[]{:S(2)}, u32[]{:S(2)}) collective-permute-start(bf16[256,128]{1,0:T(8,128)(2,1)S(1)} %get-tuple-element.205), channel_id=1, source_target_pairs={{0,4},{2,6},{4,0},{6,2},{1,5},{3,7},{5,1},{7,3},{8,12},{10,14},{12... | collective-permute-start | bytes 196616 | tf_op jit(solution)/shard_map/ppermute | solution.py:755
  603.6 7.7 %collective-permute-start.20 = (bf16[256,128]{1,0:T(8,128)(2,1)S(1)}, bf16[256,128]{1,0:T(8,128)(2,1)S(1)}, u32[]{:S(2)}, u32[]{:S(2)}) collective-permute-start(bf16[256,128]{1,0:T(8,128)(2,1)S(1)} %get-tuple-element.204), channel_id=1, source_target_pairs={{0,6},{2,0},{4,2},{6,4},{1,7},{3,1},{5,3},{7,5},{8,14},{10,8},{12,... | collective-permute-start | bytes 196616 | tf_op jit(solution)/shard_map/ppermute | solution.py:755
  604.5 23.5 %copy-start.24 = (f32[2,384]{1,0:T(2,128)S(1)}, f32[2,384]{1,0:T(2,128)}, u32[]{:S(2)}) copy-start(f32[2,384]{1,0:T(2,128)} %copy-done.23) | copy-start | bytes 9220
  605.4 8.0 %collective-permute-start.14 = (bf16[3,256,128]{2,1,0:T(8,128)(2,1)}, bf16[3,256,128]{2,1,0:T(8,128)(2,1)S(1)}, u32[]{:S(2)}, u32[]{:S(2)}) collective-permute-start(bf16[3,256,128]{2,1,0:T(8,128)(2,1)} %get-tuple-element.199), channel_id=1, source_target_pairs={{0,0},{2,2},{4,8},{6,10},{8,4},{10,6},{12,12},{14,14},{1,1},{3,3},... | collective-permute-start | bytes 589832 | tf_op jit(solution)/shard_map/ppermute | solution.py:918
  607.0 14.0 %collective-permute-start.15 = (bf16[3,256,128]{2,1,0:T(8,128)(2,1)S(1)}, bf16[3,256,128]{2,1,0:T(8,128)(2,1)S(1)}, u32[]{:S(2)}, u32[]{:S(2)}) collective-permute-start(bf16[3,256,128]{2,1,0:T(8,128)(2,1)S(1)} %get-tuple-element.202), channel_id=1, source_target_pairs={{0,2},{2,8},{4,10},{6,0},{8,6},{10,12},{12,14},{14,4},{1,3},{3,9},... | collective-permute-start | bytes 589832 | tf_op jit(solution)/shard_map/ppermute | solution.py:918
  609.1 18.1 %collective-permute-start.16 = (bf16[3,256,128]{2,1,0:T(8,128)(2,1)S(1)}, bf16[3,256,128]{2,1,0:T(8,128)(2,1)S(1)}, u32[]{:S(2)}, u32[]{:S(2)}) collective-permute-start(bf16[3,256,128]{2,1,0:T(8,128)(2,1)S(1)} %get-tuple-element.201), channel_id=1, source_target_pairs={{0,8},{2,10},{4,0},{6,2},{8,12},{10,14},{12,4},{14,6},{1,9},{3,11}... | collective-permute-start | bytes 589832 | tf_op jit(solution)/shard_map/ppermute | solution.py:918
  611.3 15.9 %collective-permute-start.17 = (bf16[3,256,128]{2,1,0:T(8,128)(2,1)S(1)}, bf16[3,256,128]{2,1,0:T(8,128)(2,1)S(1)}, u32[]{:S(2)}, u32[]{:S(2)}) collective-permute-start(bf16[3,256,128]{2,1,0:T(8,128)(2,1)S(1)} %get-tuple-element.200), channel_id=1, source_target_pairs={{0,10},{2,0},{4,2},{6,8},{8,14},{10,4},{12,6},{14,12},{1,11},{3,1}... | collective-permute-start | bytes 589832 | tf_op jit(solution)/shard_map/ppermute | solution.py:918
  628.0 5.1 copy-start.29
  (20 other events, 50.6 us)
Sparse Core Ops, SparseCore 0:
  10.9 200.5 all-gather.2

commit v2 on v1

--- a/solution.py
+++ b/solution.py
@@ -461,11 +461,19 @@
     )(tokens, qkv_weight, pack, ids)
 
 
-def exit_kernel(
-    outer_count, rest_count, sums_ref, own_ref, total_ref, out_ref,
-    dp_got, part, tensor_got, dp_send, dp_recv, tensor_send, tensor_recv,
-    move_send, move_recv, own_sem,
+def tail_kernel(
+    outer_count, rest_count, groups, sums_ref, gain_ref, x_ref, d_mid_ref, w_ref, h_ref, mlp_ref,
+    proj_ref, *refs,
 ):
+    d_refs, refs = refs[: 3 * groups], refs[3 * groups :]
+    total_ref, out_ref, shard_ref, fc1_ref, fc2_ref, proj_out_ref = refs[:6]
+    (
+        core_buf, core_got, rest_buf, rest_got, own_sum, grad_buf, grad_got, seq_buf, seq_got,
+        moved, lines, dp_got, part, tensor_got, proj_got,
+        core_send, core_recv, rest_send, rest_recv, grad_send, grad_recv, seq_send, seq_recv,
+        seq_own, dp_send, dp_recv, tensor_send, tensor_recv, move_send, move_recv, own_sem,
+        proj_send, proj_recv,
+    ) = refs[6:]
     o, c, a, r = (lax.axis_index(name) for name in everywhere)
     half, low = a // 2, a % 2
     counts = (outer_count, 2, 4, rest_count)
@@ -483,6 +491,11 @@
         pl.semaphore_signal(barrier, inc=1, device_id=partner, device_id_type=pl.DeviceIdType.MESH)
     pl.semaphore_wait(barrier, len(partners))
     peer = (o, 1 - c, a, r)
+    rows = x_ref.shape[1]
+    own_cols = 128 * groups
+    cols = own_cols // 2
+    dp_count = 2 * outer_count
+    shard_rows = w_ref.shape[0] // dp_count
 
     def remote(src, dst, send, recv, target):
         return pltpu.make_async_remote_copy(
@@ -490,17 +503,109 @@
             device_id=target, device_id_type=pl.DeviceIdType.MESH,
         )
 
+    def d_rows(i, spot):
+        return jnp.concatenate([d_refs[3 * g + i][spot, :] for g in range(groups)], axis=1)
+
+    def partial(core, turn, shift):
+        start = ((2 * core + turn) * rest_count + (r + shift) % rest_count) * rows
+        spot = pl.ds(pl.multiple_of(start, rows), rows)
+        total = 0.0
+        for i in range(3):
+            weight = w_ref[:, i * own_cols : (i + 1) * own_cols]
+            total = total + dot_f32(d_rows(i, spot), weight, contract_cols)
+        return total
+
+    def core_copy(slot):
+        return remote(
+            core_buf.at[slot], core_got.at[slot], core_send.at[slot], core_recv.at[slot], peer
+        )
+
+    def rest_copy(turn, shift):
+        return remote(
+            rest_buf.at[shift - 1, turn], rest_got.at[shift - 1, turn],
+            rest_send.at[shift - 1, turn], rest_recv.at[shift - 1, turn],
+            (o, c, a, (r + shift) % rest_count),
+        )
+
+    def proj_copy(shift):
+        target = (a + shift) % 4
+        return remote(
+            proj_ref.at[target], proj_got.at[shift - 1], proj_send.at[shift - 1],
+            proj_recv.at[shift - 1], (o, c, target, r),
+        )
+
+    order = [*range(1, rest_count), 0]
+    for shift in order:
+        for turn in range(2):
+            slot = 2 * shift + turn
+            core_buf[slot] = partial(1 - c, turn, shift).astype(jnp.bfloat16)
+            core_copy(slot).start()
+    for shift in order:
+        for turn in range(2):
+            slot = 2 * shift + turn
+            mine = partial(c, turn, shift)
+            core_copy(slot).wait_recv()
+            mine = mine + core_got[slot].astype(jnp.float32)
+            if shift:
+                rest_buf[shift - 1, turn] = mine.astype(jnp.bfloat16)
+                rest_copy(turn, shift).start()
+            else:
+                own_sum[turn] = mine
+
+    for shift in range(1, 4):
+        proj_copy(shift).start()
+
+    def grad_copy(shift):
+        target = (o + shift) % outer_count
+        return remote(
+            grad_buf.at[target], grad_got.at[shift - 1], grad_send.at[shift - 1],
+            grad_recv.at[shift - 1], (target, c, a, r),
+        )
+
+    for d in range(dp_count):
+        turned = h_ref[:, d * shard_rows : (d + 1) * shard_rows].T
+        for i in range(3):
+            grad = dot_f32(turned, d_rows(i, slice(None)))
+            grad_buf[d // 2, d % 2, :, i * own_cols : (i + 1) * own_cols] = grad.astype(
+                jnp.bfloat16
+            )
+    for shift in range(1, outer_count):
+        grad_copy(shift).start()
+
+    total = 0.0
+    for seq in range(4):
+        total = total + mlp_ref[seq, 0].astype(jnp.float32)
+    fc1_ref[...] = total
+    total = 0.0
+    for seq in range(4):
+        total = total + mlp_ref[seq, 1].astype(jnp.float32)
+    fc2_ref[...] = total.T
+    total = proj_ref[a].astype(jnp.float32)
+    for shift in range(1, 4):
+        proj_copy(shift).wait_recv()
+        total = total + proj_got[shift - 1].astype(jnp.float32)
+    proj_out_ref[...] = total.T
+
     def stays(turn):
         return jnp.logical_and(low == c, 2 * c + turn == a)
 
     def move_copy(turn):
         return remote(
-            own_ref.at[turn], out_ref.at[half], move_send.at[turn], move_recv.at[half],
+            moved.at[turn], out_ref.at[half], move_send.at[turn], move_recv.at[half],
             (o, low, 2 * c + turn, r),
         )
 
-    stay_copy = pltpu.make_async_copy(own_ref.at[low], out_ref.at[half], own_sem)
-    for turn in range(2):
+    stay_copy = pltpu.make_async_copy(moved.at[low], out_ref.at[half], own_sem)
+
+    def settle_rows(turn):
+        total = own_sum[turn]
+        for shift in range(1, rest_count):
+            rest_copy(turn, shift).wait_recv()
+            total = total + rest_got[shift - 1, turn].astype(jnp.float32)
+        normed, rate = norm_parts(x_ref[turn].astype(jnp.float32))
+        grad = d_mid_ref[turn] + norm_back(normed, rate, gain_ref[...], total)
+        moved[turn] = grad.astype(jnp.bfloat16)
+
         @pl.when(stays(turn))
         def _():
             stay_copy.start()
@@ -509,16 +614,59 @@
         def _():
             move_copy(turn).start()
 
+        gain = jnp.sum(total * normed, axis=0, keepdims=True)
+        return gain, jnp.sum(total, axis=0, keepdims=True)
+
+    def mine(block):
+        return jnp.logical_and(block // 2 == c, 2 * c + block % 2 == a)
+
+    def seq_copy(block):
+        return remote(
+            seq_buf.at[block], seq_got.at[a], seq_send.at[block], seq_recv.at[a],
+            (o, block // 2, 2 * c + block % 2, r),
+        )
+
+    def seq_keep(block):
+        return pltpu.make_async_copy(seq_buf.at[block], seq_got.at[a], seq_own)
+
+    first = settle_rows(0)
+    for shift in range(1, outer_count):
+        grad_copy(shift).wait_recv()
+    for core in range(2):
+        total = grad_buf[o, core].astype(jnp.float32)
+        for shift in range(1, outer_count):
+            total = total + grad_got[shift - 1, core].astype(jnp.float32)
+        for turn in range(2):
+            block = 2 * core + turn
+            for i in range(3):
+                start = i * own_cols + turn * cols
+                seq_buf[block, i] = total[:, start : start + cols].astype(jnp.bfloat16)
+
+            @pl.when(mine(block))
+            def _():
+                seq_keep(block).start()
+
+            @pl.when(jnp.logical_not(mine(block)))
+            def _():
+                seq_copy(block).start()
+    second = settle_rows(1)
+
+    lines[...] = sums_ref[...]
+    for i in range(2):
+        line = first[i] + second[i]
+        for d in range(dp_count):
+            lines[d, i : i + 1, :] = line[:, d * shard_rows : (d + 1) * shard_rows]
+
     def dp_copy(i):
         target = away(dp_shifts[i])
         return remote(
-            sums_ref.at[target[0] * 2 + target[1]], dp_got.at[i], dp_send.at[i], dp_recv.at[i],
+            lines.at[target[0] * 2 + target[1]], dp_got.at[i], dp_send.at[i], dp_recv.at[i],
             target,
         )
 
     for i in range(len(dp_shifts)):
         dp_copy(i).start()
-    total = sums_ref[o * 2 + c]
+    total = lines[o * 2 + c]
     for i in range(len(dp_shifts)):
         dp_copy(i).wait_recv()
         total = total + dp_got[i]
@@ -535,6 +683,22 @@
         tensor_copy(i).wait_recv()
         total = total + tensor_got[i]
     total_ref[...] = total
+
+    for block in range(4):
+        @pl.when(mine(block))
+        def _():
+            seq_keep(block).wait()
+    for seq in range(4):
+        here = jnp.logical_and(half == c, a == seq)
+
+        @pl.when(jnp.logical_not(here))
+        def _():
+            spot = seq_got.at[seq]
+            remote(spot, spot, seq_send.at[0], seq_recv.at[seq], peer).wait_recv()
+    total = 0.0
+    for seq in range(4):
+        total = total + seq_got[seq].astype(jnp.float32)
+    shard_ref[...] = total
 
     for batch in range(2):
         same = jnp.logical_and(half == c, 2 * batch + c == a)
@@ -551,46 +715,116 @@
         @pl.when(jnp.logical_not(stays(turn)))
         def _():
             move_copy(turn).wait_send()
+    for block in range(4):
+        @pl.when(jnp.logical_not(mine(block)))
+        def _():
+            seq_copy(block).wait_send()
+    for shift in order:
+        for turn in range(2):
+            core_copy(2 * shift + turn).wait_send()
+            if shift:
+                rest_copy(turn, shift).wait_send()
+    for shift in range(1, outer_count):
+        grad_copy(shift).wait_send()
+    for shift in range(1, 4):
+        proj_copy(shift).wait_send()
     for i in range(len(dp_shifts)):
         dp_copy(i).wait_send()
     for i in range(len(tensor_shifts)):
         tensor_copy(i).wait_send()
 
 
-def leave(sums, own):
-    outer_count, rest_count = lax.axis_size("o"), lax.axis_size("r")
+def tail(sums, gain, x, d_mid, w_qkv, h, mlp_parts, proj_parts, d_parts):
+    outer, rest = lax.axis_size("o"), lax.axis_size("r")
     dma = pltpu.SemaphoreType.DMA
-    few, many = 2 * outer_count - 1, 4 * rest_count - 1
+    few, many = 2 * outer - 1, 4 * rest - 1
+    wide, narrow = max(rest - 1, 1), max(outer - 1, 1)
     shape = sums.shape[1:]
+    _, rows, width = x.shape
+    groups = len(d_parts) // 3
+    own_cols, shard_rows = 128 * groups, width // (2 * outer)
+    low = jnp.bfloat16
+    space = pl.BlockSpec(memory_space=pltpu.VMEM)
     return pl.pallas_call(
-        lambda *refs: exit_kernel(outer_count, rest_count, *refs),
-        in_specs=[pl.BlockSpec(memory_space=pltpu.VMEM), pl.BlockSpec(memory_space=pl.ANY)],
-        out_specs=[pl.BlockSpec(memory_space=pltpu.VMEM), pl.BlockSpec(memory_space=pl.ANY)],
+        lambda *refs: tail_kernel(outer, rest, groups, *refs),
+        in_specs=[space] * (8 + 3 * groups),
+        out_specs=[space, pl.BlockSpec(memory_space=pl.ANY)] + [space] * 4,
         out_shape=[
             jax.ShapeDtypeStruct(shape, jnp.float32),
-            jax.ShapeDtypeStruct(own.shape, own.dtype),
+            jax.ShapeDtypeStruct(x.shape, low),
+            jax.ShapeDtypeStruct((3, shard_rows, own_cols // 2), jnp.float32),
+            jax.ShapeDtypeStruct(mlp_parts.shape[2:], jnp.float32),
+            jax.ShapeDtypeStruct(mlp_parts.shape[:1:-1], jnp.float32),
+            jax.ShapeDtypeStruct(proj_parts.shape[:0:-1], jnp.float32),
         ],
         scratch_shapes=[
+            pltpu.VMEM((2 * rest, rows, width), low), pltpu.VMEM((2 * rest, rows, width), low),
+            pltpu.VMEM((wide, 2, rows, width), low), pltpu.VMEM((wide, 2, rows, width), low),
+            pltpu.VMEM((2, rows, width), jnp.float32),
+            pltpu.VMEM((outer, 2, shard_rows, 3 * own_cols), low),
+            pltpu.VMEM((narrow, 2, shard_rows, 3 * own_cols), low),
+            pltpu.VMEM((4, 3, shard_rows, own_cols // 2), low),
+            pltpu.VMEM((4, 3, shard_rows, own_cols // 2), low),
+            pltpu.VMEM((2, rows, width), low),
+            pltpu.VMEM(sums.shape, jnp.float32),
             pltpu.VMEM((few, *shape), jnp.float32), pltpu.VMEM(shape, jnp.float32),
             pltpu.VMEM((many, *shape), jnp.float32),
+            pltpu.VMEM((3, *proj_parts.shape[1:]), low),
+            dma((2 * rest,)), dma((2 * rest,)), dma((wide, 2)), dma((wide, 2)),
+            dma((narrow,)), dma((narrow,)), dma((4,)), dma((4,)), dma(()),
             dma((few,)), dma((few,)), dma((many,)), dma((many,)), dma((2,)), dma((2,)), dma(()),
+            dma((3,)), dma((3,)),
         ],
-        compiler_params=pltpu.CompilerParams(collective_id=1, has_side_effects=True),
+        compiler_params=pltpu.CompilerParams(
+            collective_id=1, has_side_effects=True, vmem_limit_bytes=56 * 1024 * 1024
+        ),
         cost_estimate=pl.CostEstimate(
-            flops=0, bytes_accessed=120 * 1024 * 1024, transcendentals=0
+            flops=0, bytes_accessed=250 * 1024 * 1024, transcendentals=0
         ),
-    )(sums, own)
+    )(sums, gain, x, d_mid, w_qkv, h, mlp_parts, proj_parts, *d_parts)
 
 
 def mlp_kernel(
-    h_ref, dm_ref, w1_ref, w2_ref, bias_ref, m_ref, dh_ref, grad1_ref, grad2_ref, dbias_ref,
-    h_turned, dm_turned, kept, sent, got, send_sem, got_sem,
+    outer_count, rest_count,
+    h_ref, dm_ref, w1_ref, w2_ref, bias_ref, m_ref, dh_ref, kept1_ref, got1_ref, kept2_ref,
+    got2_ref, dbias_ref, h_turned, dm_turned, kept, sent, got, send_sem, got_sem,
+    own_sem, rest_send, rest_recv, outer_send, outer_recv,
 ):
     o, core, a, r = (lax.axis_index(name) for name in everywhere)
     block = pl.program_id(0)
     count = pl.num_programs(0) - 1
     slot, other = block % 2, (block + 1) % 2
     peer = (o, 1 - core, a, r)
+    partners = [peer]
+    partners += [(o, core, a, (r + i) % rest_count) for i in range(1, rest_count)]
+    partners += [((o + i) % outer_count, core, a, r) for i in range(1, outer_count)]
+
+    def to_rest(index):
+        target = index % rest_count
+        shift = (target - r + rest_count) % rest_count
+        return pltpu.make_async_remote_copy(
+            src_ref=got.at[index, 0], dst_ref=got1_ref.at[shift - 1, index // rest_count],
+            send_sem=rest_send.at[index], recv_sem=rest_recv.at[shift - 1, index // rest_count],
+            device_id=(o, core, a, target), device_id_type=pl.DeviceIdType.MESH,
+        )
+
+    def keep_rest(index):
+        return pltpu.make_async_copy(
+            got.at[index, 0], kept1_ref.at[index // rest_count], own_sem.at[0, index]
+        )
+
+    def to_outer(index, shift):
+        target = (o + shift) % outer_count
+        return pltpu.make_async_remote_copy(
+            src_ref=got.at[index, 1, target], dst_ref=got2_ref.at[shift - 1, index],
+            send_sem=outer_send.at[shift - 1, index], recv_sem=outer_recv.at[shift - 1, index],
+            device_id=(target, core, a, r), device_id_type=pl.DeviceIdType.MESH,
+        )
+
+    def keep_outer(index):
+        return pltpu.make_async_copy(
+            got.at[index, 1, o], kept2_ref.at[index], own_sem.at[1, index]
+        )
 
     def to_peer(index, turn):
         return pltpu.make_async_remote_copy(
@@ -602,8 +836,11 @@
     @pl.when(block == 0)
     def _():
         barrier = pltpu.get_barrier_semaphore()
-        pl.semaphore_signal(barrier, inc=1, device_id=peer, device_id_type=pl.DeviceIdType.MESH)
-        pl.semaphore_wait(barrier, 1)
+        for partner in partners:
+            pl.semaphore_signal(
+                barrier, inc=1, device_id=partner, device_id_type=pl.DeviceIdType.MESH
+            )
+        pl.semaphore_wait(barrier, len(partners))
         h_turned[...] = h_ref[...].T
         dm_turned[...] = dm_ref[...].T
         m_ref[...] = jnp.zeros_like(m_ref)
@@ -652,13 +889,51 @@
     @pl.when(block >= 1)
     def _():
         to_peer(block - 1, other).wait_recv()
-        for turn, out_ref in enumerate((grad1_ref, grad2_ref)):
+        done = block - 1
+        for turn in range(2):
             mine = kept[other, turn].astype(jnp.float32)
-            out_ref[0] = (mine + got[block - 1, turn].astype(jnp.float32)).astype(jnp.bfloat16)
+            both = mine + got[done, turn].astype(jnp.float32)
+            got[done, turn] = both.astype(jnp.bfloat16)
+
+        @pl.when(done % rest_count == r)
+        def _():
+            keep_rest(done).start()
+
+        @pl.when(done % rest_count != r)
+        def _():
+            to_rest(done).start()
+
+        keep_outer(done).start()
+        for shift in range(1, outer_count):
+            to_outer(done, shift).start()
 
     @pl.when(block == count)
     def _():
         to_peer(block - 1, other).wait_send()
+
+        def settle(index, carry):
+            @pl.when(index % rest_count == r)
+            def _():
+                keep_rest(index).wait()
+
+            @pl.when(index % rest_count != r)
+            def _():
+                to_rest(index).wait_send()
+
+            keep_outer(index).wait()
+            for shift in range(1, outer_count):
+                to_outer(index, shift).wait()
+            return carry
+
+        lax.fori_loop(0, 4 * rest_count, settle, 0)
+        for seq in range(4):
+            for shift in range(1, rest_count):
+                spot = got1_ref.at[shift - 1, seq]
+                pltpu.make_async_remote_copy(
+                    src_ref=spot, dst_ref=spot, send_sem=rest_send.at[0],
+                    recv_sem=rest_recv.at[shift - 1, seq],
+                    device_id=peer, device_id_type=pl.DeviceIdType.MESH,
+                ).wait_recv()
 
 
 def mlp(rows_low, d_branch, weights, hid, bias):
@@ -666,20 +941,27 @@
     dp_count, tensor_count, _, rows = weights.shape
     outer = dp_count // 2
     whole = pl.BlockSpec((tokens_here, width), lambda t: (0, 0))
-    grad_spec = pl.BlockSpec((1, outer, rows, hid), lambda t: (jnp.maximum(t - 1, 0), 0, 0, 0))
-    grad = jax.ShapeDtypeStruct((tensor_count, outer, rows, hid), jnp.bfloat16)
+    rest = tensor_count // 4
+    far = pl.BlockSpec(memory_space=pl.ANY)
+    wide, narrow = max(rest - 1, 1), max(outer - 1, 1)
+    low = jnp.bfloat16
+    dma = pltpu.SemaphoreType.DMA
     out = jax.ShapeDtypeStruct((tokens_here, width), jnp.float32)
     last = tensor_count - 1
     line = pl.BlockSpec((1, hid), lambda t: (0, jnp.minimum(t, last)))
     w1_spec = pl.BlockSpec((dp_count, 1, hid, rows), lambda t: (0, jnp.minimum(t, last), 0, 0))
     w2_spec = pl.BlockSpec((dp_count, 1, hid, rows), lambda t: (0, jnp.minimum(t, last), 1, 0))
     return pl.pallas_call(
-        mlp_kernel,
+        lambda *refs: mlp_kernel(outer, rest, *refs),
         grid=(tensor_count + 1,),
         in_specs=[whole, whole, w1_spec, w2_spec, line],
-        out_specs=[whole, whole, grad_spec, grad_spec, line],
+        out_specs=[whole, whole, far, far, far, far, line],
         out_shape=[
-            out, out, grad, grad,
+            out, out,
+            jax.ShapeDtypeStruct((4, outer, rows, hid), low),
+            jax.ShapeDtypeStruct((wide, 4, outer, rows, hid), low),
+            jax.ShapeDtypeStruct((tensor_count, rows, hid), low),
+            jax.ShapeDtypeStruct((narrow, tensor_count, rows, hid), low),
             jax.ShapeDtypeStruct((1, tensor_count * hid), jnp.float32),
         ],
         scratch_shapes=[
@@ -688,8 +970,9 @@
             pltpu.VMEM((2, 2, outer, rows, hid), jnp.bfloat16),
             pltpu.VMEM((2, 2, outer, rows, hid), jnp.bfloat16),
             pltpu.VMEM((tensor_count, 2, outer, rows, hid), jnp.bfloat16),
-            pltpu.SemaphoreType.DMA((2,)),
-            pltpu.SemaphoreType.DMA((tensor_count,)),
+            dma((2,)), dma((tensor_count,)), dma((2, tensor_count)),
+            dma((tensor_count,)), dma((wide, 4)),
+            dma((narrow, tensor_count)), dma((narrow, tensor_count)),
         ],
         compiler_params=pltpu.CompilerParams(
             vmem_limit_bytes=60 * 1024 * 1024, collective_id=2, has_side_effects=True
@@ -702,6 +985,153 @@
     )(rows_low, d_branch, weights, weights, bias)
 
 
+def proj_groups(weights_ref, rest_count):
+    for group in range(weights_ref.shape[1] // 2):
+        first = 2 * (group // rest_count) * rest_count + group % rest_count
+        yield group, first, first + rest_count
+
+
+def before_kernel(
+    rest_count, att_ref, x_ref, dy_ref, weights_ref, vec_ref, mid_ref, branch_ref, h_ref, dm_ref
+):
+    dp_count, _, depth, rows = weights_ref.shape
+    branch = []
+    for d in range(dp_count):
+        total = vec_ref[2:3, d * rows : (d + 1) * rows]
+        for group, one, two in proj_groups(weights_ref, rest_count):
+            weight = jnp.concatenate([weights_ref[d, one], weights_ref[d, two]], axis=0)
+            total = total + dot_f32(att_ref[group], weight)
+        branch.append(total)
+    branch = jnp.concatenate(branch, axis=1)
+    branch_ref[...] = branch
+    middle = x_ref[...].astype(jnp.float32) + vec_ref[3:4] * branch
+    mid_ref[...] = middle
+    normed, _ = norm_parts(middle)
+    h_ref[...] = (normed * vec_ref[4:5] + vec_ref[5:6]).astype(jnp.bfloat16)
+    dm_ref[...] = (vec_ref[7:8] * dy_ref[...].astype(jnp.float32)).astype(jnp.bfloat16)
+
+
+def after_kernel(
+    rest_count, m_ref, dh_ref, mid_ref, branch_ref, dy_ref, att_ref, weights_ref, vec_ref,
+    out_ref, d_mid_ref, d_att_ref, sums_ref, kept_ref, sent_ref, grad,
+):
+    step, core = pl.program_id(0), lax.axis_index("c")
+    dp_count, _, depth, rows = weights_ref.shape
+
+    @pl.when(step == 0)
+    def _():
+        sums_ref[...] = jnp.zeros_like(sums_ref)
+        grad[...] = jnp.zeros_like(grad)
+
+    middle, dy = mid_ref[...], dy_ref[...].astype(jnp.float32)
+    two = m_ref[...] + vec_ref[6:7]
+    out_ref[...] = (middle + vec_ref[7:8] * two).astype(jnp.bfloat16)
+    dm = (vec_ref[7:8] * dy).astype(jnp.bfloat16).astype(jnp.float32)
+    normed, rate = norm_parts(middle)
+    d_normed = dh_ref[...]
+    d_mid = dy + norm_back(normed, rate, vec_ref[4:5], d_normed)
+    d_mid_ref[...] = d_mid
+    d_branch = (vec_ref[3:4] * d_mid).astype(jnp.bfloat16)
+    lines = [
+        d_branch.astype(jnp.float32), d_mid * branch_ref[...], d_normed * normed, d_normed, dm,
+        dy * two,
+    ]
+    for i, line in enumerate(lines):
+        sums_ref[i : i + 1] += jnp.sum(line, axis=0, keepdims=True)
+    turned = d_branch.T
+    for group, one, two in proj_groups(weights_ref, rest_count):
+        total = 0.0
+        for d in range(dp_count):
+            part = slice(d * rows, (d + 1) * rows)
+            weight = jnp.concatenate([weights_ref[d, one], weights_ref[d, two]], axis=0)
+            total = total + dot_f32(d_branch[:, part], weight, contract_cols)
+        d_att_ref[group] = total.astype(jnp.bfloat16)
+        both = dot_f32(turned, att_ref[group])
+        grad[one] += both[:, :depth]
+        grad[two] += both[:, depth:]
+
+    @pl.when(step == pl.num_programs(0) - 1)
+    def _():
+        for d in range(dp_count):
+            part = grad[:, d * rows : (d + 1) * rows].astype(jnp.bfloat16)
+
+            @pl.when(core == d % 2)
+            def _():
+                kept_ref[:, d // 2] = part
+
+            @pl.when(core != d % 2)
+            def _():
+                sent_ref[:, d // 2] = part
+
+
+def side_specs(weights, own_cols, steps, own_rows, width):
+    dp_count, tensor_count, total, rows = weights.shape
+    depth = own_cols // 2
+    tile = own_rows // steps
+    groups = tensor_count // 2
+    row_spec = pl.BlockSpec((tile, width), lambda i: (i, 0))
+    att_spec = pl.BlockSpec((groups, tile, own_cols), lambda i: (0, i, 0))
+    w_spec = pl.BlockSpec(
+        (dp_count, tensor_count, depth, rows), lambda i: (0, 0, total // depth - 1, 0)
+    )
+    vec_spec = pl.BlockSpec((8, width), lambda i: (0, 0))
+    return row_spec, att_spec, w_spec, vec_spec
+
+
+side_steps = 2
+
+
+def before(att, x, dy, weights, vecs):
+    own_rows, width = x.shape
+    rest = lax.axis_size("r")
+    row_spec, att_spec, w_spec, vec_spec = side_specs(
+        weights, att.shape[2], side_steps, own_rows, width
+    )
+    wide = jax.ShapeDtypeStruct((own_rows, width), jnp.float32)
+    slim = jax.ShapeDtypeStruct((own_rows, width), jnp.bfloat16)
+    return pl.pallas_call(
+        lambda *refs: before_kernel(rest, *refs),
+        grid=(side_steps,),
+        in_specs=[att_spec, row_spec, row_spec, w_spec, vec_spec],
+        out_specs=[row_spec] * 4,
+        out_shape=[wide, wide, slim, slim],
+        compiler_params=pltpu.CompilerParams(vmem_limit_bytes=48 * 1024 * 1024),
+        cost_estimate=pl.CostEstimate(
+            flops=4 * own_rows * width * width, bytes_accessed=16 * 1024 * 1024, transcendentals=0
+        ),
+    )(att, x, dy, weights, vecs)
+
+
+def after(m, dh, middle, branch, dy, att, weights, vecs):
+    own_rows, width = m.shape
+    rest, outer = lax.axis_size("r"), lax.axis_size("o")
+    tensor_count, rows = weights.shape[1], weights.shape[3]
+    depth = att.shape[2] // 2
+    row_spec, att_spec, w_spec, vec_spec = side_specs(
+        weights, att.shape[2], side_steps, own_rows, width
+    )
+    grad_spec = pl.BlockSpec((tensor_count, outer, rows, depth), lambda i: (0, 0, 0, 0))
+    grad = jax.ShapeDtypeStruct((tensor_count, outer, rows, depth), jnp.bfloat16)
+    return pl.pallas_call(
+        lambda *refs: after_kernel(rest, *refs),
+        grid=(side_steps,),
+        in_specs=[row_spec] * 5 + [att_spec, w_spec, vec_spec],
+        out_specs=[row_spec, row_spec, att_spec, vec_spec, grad_spec, grad_spec],
+        out_shape=[
+            jax.ShapeDtypeStruct((own_rows, width), jnp.bfloat16),
+            jax.ShapeDtypeStruct((own_rows, width), jnp.float32),
+            jax.ShapeDtypeStruct(att.shape, jnp.bfloat16),
+            jax.ShapeDtypeStruct((8, width), jnp.float32),
+            grad, grad,
+        ],
+        scratch_shapes=[pltpu.VMEM((tensor_count, width, depth), jnp.float32)],
+        compiler_params=pltpu.CompilerParams(vmem_limit_bytes=56 * 1024 * 1024),
+        cost_estimate=pl.CostEstimate(
+            flops=8 * own_rows * width * width, bytes_accessed=24 * 1024 * 1024, transcendentals=0
+        ),
+    )(m, dh, middle, branch, dy, att, weights, vecs)
+
+
 def gather_parts(shard):
     parts = lax.all_gather(shard, everywhere, axis=0, tiled=False)
     return parts.reshape(lax.axis_size("o") * 2, -1, *shard.shape)
@@ -759,6 +1189,21 @@
     for values in got:
         total = total + values.astype(jnp.float32)
     return total.astype(dtype)
+
+
+def seq_parts(blocks):
+    me = lax.axis_index("a")
+    parts = [pick(blocks, me)]
+    for step in range(1, 4):
+        parts.append(lax.ppermute(pick(blocks, (me + step) % 4), "a", place_shift(step, 4)))
+    return parts
+
+
+def pair_sum(kept, got, count):
+    total = kept.astype(jnp.float32)
+    for i in range(count):
+        total = total + got[i].astype(jnp.float32)
+    return total.astype(jnp.bfloat16)
 
 
 def core_sum(own, sent):
@@ -811,8 +1256,6 @@
     ids_row, ids_col = run_ids[None, :], run_ids[:, None]
 
     weights = gather_parts(jnp.concatenate([fc1_weight.T, fc2_weight, proj_weight]))
-    w_proj = weights[:, :, 2 * fc2_weight.shape[0] :]
-    w_proj = jnp.transpose(w_proj, (1, 2, 0, 3)).reshape(width, width)
     w_qkv = jnp.moveaxis(w_parts, 0, 2).swapaxes(0, 1).reshape(width, 3 * own_cols)
 
     def own_of(values):
@@ -827,57 +1270,34 @@
     grad_moved = move_in(out_grad)
     att_heads, lse = attention(qkv, bounds, ids_row, ids_col)
 
-    rows_in = own_of(seq_rows).astype(jnp.float32)
-    normed_one, rate_one = norm_parts(rows_in)
+    rows_own = own_of(seq_rows)
+    grad_top = grad_moved.reshape(own_rows, width)
     sent = att_heads.reshape(2, 2, rest, rows_here, own_cols)
     sent = jnp.swapaxes(sent, 1, 2).reshape(2 * rest, own_rows, own_cols)
     attended = lax.all_to_all(sent, ("c", "r"), split_axis=0, concat_axis=0, tiled=True)
-    attended = attended.reshape(2, rest, own_rows, 2, cols_here)
-    attended = jnp.transpose(attended, (2, 0, 3, 1, 4)).reshape(own_rows, width)
-    branch_one = dot_f32(attended, w_proj) + vecs[2]
-    middle = rows_in + vecs[3] * branch_one
-    normed_two, rate_two = norm_parts(middle)
-    mlp_in = (normed_two * vecs[4] + vecs[5]).astype(jnp.bfloat16)
-    grad_top = grad_moved.reshape(own_rows, width).astype(jnp.float32)
-    d_branch2 = (vecs[7] * grad_top).astype(jnp.bfloat16)
-    d_fc2_bias = jnp.sum(d_branch2.astype(jnp.float32), axis=0)
-    branch_two, d_normed_two, grad_fc1, grad_fc2, d_fc1_bias = mlp(
+    middle, branch_one, mlp_in, d_branch2 = before(attended, rows_own, grad_top, weights, vecs)
+    branch_two, d_normed_two, kept1, got1, kept2, got2, d_fc1_bias = mlp(
         mlp_in, d_branch2, weights, fc2_weight.shape[0], bias_fc1[None]
     )
-    branch_two = branch_two + vecs[6]
-    block_out = (middle + vecs[7] * branch_two).astype(jnp.bfloat16)
-    d_scale2 = jnp.sum(grad_top * branch_two, axis=0)
-    d_gain2 = jnp.sum(d_normed_two * normed_two, axis=0)
-    d_bias2 = jnp.sum(d_normed_two, axis=0)
-    d_middle = grad_top + norm_back(normed_two, rate_two, vecs[4], d_normed_two)
-    d_scale1 = jnp.sum(d_middle * branch_one, axis=0)
-    d_branch1 = (vecs[3] * d_middle).astype(jnp.bfloat16)
-    d_proj_bias = jnp.sum(d_branch1.astype(jnp.float32), axis=0)
-    grad_fc1 = sum_shards(grad_fc1.reshape(4, rest, *grad_fc1.shape[1:]), "r", 1, jnp.bfloat16)
-    grad_fc2 = sum_shards(grad_fc2.reshape(4, rest, *grad_fc2.shape[1:]), "o", 2, jnp.bfloat16)
-    block_out = move_out(block_out.reshape(2, rows_here, width))
-    d_attended = dot_f32(d_branch1, w_proj, contract_cols).astype(jnp.bfloat16)
-    sent = d_attended.reshape(own_rows, 2, 2, rest, cols_here)
-    sent = jnp.transpose(sent, (1, 3, 0, 2, 4)).reshape(2 * rest, own_rows, own_cols)
+    grad_fc1 = pair_sum(kept1, got1, rest - 1)
+    grad_fc2 = pair_sum(kept2, got2, outer - 1).reshape(4, rest, *kept2.shape[1:])
+    branch_two, grad_fc1, grad_fc2 = lax.optimization_barrier((branch_two, grad_fc1, grad_fc2))
+    grad_fc1 = sum_shards(grad_fc1, "o", 1, jnp.bfloat16)
+    grad_fc2 = sum_shards(grad_fc2, "r", 1, jnp.bfloat16)
+    block_out, d_middle, sent, line_sums, proj_kept, proj_sent = after(
+        branch_two, d_normed_two, middle, branch_one, grad_top, attended, weights, vecs
+    )
     d_heads = lax.all_to_all(sent, ("c", "r"), split_axis=0, concat_axis=0, tiled=True)
     d_heads = jnp.swapaxes(d_heads.reshape(2, rest, 2, rows_here, own_cols), 1, 2)
     d_heads = d_heads.reshape(tok_count, own_cols)
-
-    split = d_branch1.reshape(own_rows, outer, 2, shard_rows)
-
-    def proj_grad(which):
-        mine = lax.dynamic_index_in_dim(split, which, 2, keepdims=False)
-        grad = dot_f32(mine.reshape(own_rows, width // 2), attended, contract_rows)
-        grad = grad.astype(jnp.bfloat16).reshape(outer, shard_rows, tensor_count, cols_here)
-        return jnp.transpose(grad, (2, 0, 1, 3))
-
-    grad_proj = core_sum(proj_grad(c), proj_grad(1 - c))
-    d_heads, grad_fc1, grad_fc2, grad_proj = lax.optimization_barrier(
-        (d_heads, grad_fc1, grad_fc2, grad_proj)
-    )
-
-    grad_fc1 = sum_shards(grad_fc1, "o", 1, jnp.bfloat16)
-    grad_fc2 = sum_shards(grad_fc2, "r", 1, jnp.bfloat16)
+    grad_proj = core_sum(proj_kept, proj_sent)
+    d_heads, grad_fc1, grad_fc2, grad_proj, block_out = lax.optimization_barrier(
+        (d_heads, grad_fc1, grad_fc2, grad_proj, block_out)
+    )
+
+    block_out = move_out(block_out.reshape(2, rows_here, width))
+    mlp_parts = jnp.stack([grad_fc1, grad_fc2], axis=1)
+    mlp_parts = lax.all_to_all(mlp_parts, "a", split_axis=0, concat_axis=0, tiled=True)
     grad_proj = sum_shards(grad_proj, "o", 2, jnp.bfloat16)
     groups = own_cols // 128
     d_parts = []
@@ -886,54 +1306,32 @@
             attention_back(qkv, bounds, ids_row, ids_col, att_heads, d_heads, lse, group)
         )
         if group == 0:
-            d_parts, d_heads, grad_fc1, grad_fc2, grad_proj = lax.optimization_barrier(
-                (d_parts, d_heads, grad_fc1, grad_fc2, grad_proj)
-            )
-            shard_fc1 = sum_shards(grad_fc1, "a", 0, jnp.float32)
-            shard_fc2 = sum_shards(grad_fc2, "a", 0, jnp.float32)
+            d_parts, d_heads, grad_proj = lax.optimization_barrier((d_parts, d_heads, grad_proj))
             grad_proj = sum_shards(grad_proj, "r", 1, jnp.bfloat16)
-    d_parts, grad_proj = lax.optimization_barrier((d_parts, grad_proj))
-
-    shard_proj = sum_shards(grad_proj, "a", 0, jnp.float32)
-    d_qkv = jnp.concatenate([part[i] for i in range(3) for part in d_parts], axis=1)
-    d_rows = dot_f32(d_qkv, w_qkv, contract_cols).astype(jnp.bfloat16)
-    d_rows = sum_shards(d_rows.reshape(2, 2, rest, rows_here, width), "c", 0, jnp.bfloat16)
-    d_w_qkv = dot_f32(normed_all_low, d_qkv, contract_rows).astype(jnp.bfloat16)
-    d_bias_qkv = jnp.sum(d_qkv.astype(jnp.float32), axis=0).reshape(3, 2, cols_here)
-    d_bias_qv = jnp.stack([d_bias_qkv[0], d_bias_qkv[2]])
-    d_rows, d_w_qkv, d_bias_qv = lax.optimization_barrier((d_rows, d_w_qkv, d_bias_qv))
-
-    d_w_qkv = sum_shards(
-        d_w_qkv.reshape(outer, 2, shard_rows, 3, 2, cols_here), "o", 0, jnp.bfloat16
-    )
-    d_normed_one = sum_shards(d_rows, "r", 1, jnp.float32).reshape(own_rows, width)
-    d_w_qkv = jnp.transpose(d_w_qkv, (0, 3, 2, 1, 4)).reshape(4, 3, shard_rows, cols_here)
-    shard_qkv = 0.0
-    for step in range(4):
-        pairs = []
-        for core in range(2):
-            for seq in range(4):
-                k = (seq + step) % 4
-                pairs.append((core * 4 + seq, (k // 2) * 4 + 2 * core + k % 2))
-        got = lax.ppermute(pick(d_w_qkv, (a + step) % 4), ("c", "a"), pairs)
-        shard_qkv = shard_qkv + got.astype(jnp.float32)
-    d_gain1 = jnp.sum(d_normed_one * normed_one, axis=0)
-    d_bias1 = jnp.sum(d_normed_one, axis=0)
-    input_grad = d_middle + norm_back(normed_one, rate_one, vecs[0], d_normed_one)
+    d_parts, grad_proj, block_out, mlp_parts = lax.optimization_barrier(
+        (d_parts, grad_proj, block_out, mlp_parts)
+    )
+    d_bias_qv = jnp.stack(
+        [
+            jnp.concatenate([jnp.sum(part[i].astype(jnp.float32), axis=0) for part in d_parts])
+            for i in (0, 2)
+        ]
+    ).reshape(2, 2, cols_here)
     spread_qv = jnp.zeros((2, 2, 2, rest, cols_here), jnp.float32)
     spread_qv = lax.dynamic_update_slice(
         spread_qv, d_bias_qv[:, None, :, None], (0, c, 0, r, 0)
     )
-    lines = [d_gain1, d_bias1, d_proj_bias, d_scale1, d_gain2, d_bias2, d_fc2_bias, d_scale2]
-    lines = jnp.stack(lines).reshape(8, dp_count, shard_rows)
+    lines = jnp.concatenate([line_sums[6:], line_sums[:6]]).reshape(8, dp_count, shard_rows)
     fc1_lines = d_fc1_bias.reshape(tensor_count, dp_count, fc1_short)
     fc1_lines = jnp.swapaxes(fc1_lines, 0, 1).reshape(dp_count, -1, shard_rows)
     qv_lines = spread_qv.reshape(2, tensor_count, dp_count, short)
     qv_lines = jnp.moveaxis(qv_lines, 2, 0).reshape(dp_count, -1, shard_rows)
     sums = jnp.concatenate([jnp.swapaxes(lines, 0, 1), fc1_lines, qv_lines], axis=1)
     sums = jnp.pad(sums, ((0, 0), (0, -sums.shape[1] % 8), (0, 0)))
-    vec_sums, input_grad = leave(
-        sums, input_grad.astype(jnp.bfloat16).reshape(2, rows_here, width)
+    vec_sums, input_grad, shard_qkv, shard_fc1, shard_fc2, shard_proj = tail(
+        sums, vecs[:1], rows_own.reshape(2, rows_here, width),
+        d_middle.reshape(2, rows_here, width), w_qkv, normed_all_low, mlp_parts, grad_proj,
+        [values for part in d_parts for values in part],
     )
     place = a * rest + r
     fc1_rows = fc1_lines.shape[1]
@@ -950,14 +1348,14 @@
         vec_sums[1],
         shard_qkv,
         grad_qv_bias,
-        shard_proj.T,
+        shard_proj,
         vec_sums[2],
         vec_sums[3],
         vec_sums[4],
         vec_sums[5],
         shard_fc1,
         grad_fc1_bias,
-        shard_fc2.T,
+        shard_fc2,
         vec_sums[6],
         vec_sums[7],
     )

time: 704 us -> 613 us (0.87)
  Pallas kernels: 350 us -> 427 us
  local copies, waits for them, and re-layouts: 112 us -> 41.7 us
  matrix products: 31.2 us -> 5.35 us
  other arithmetic: 63.3 us -> 38 us
  starting transfers between devices: 71.3 us -> 46.1 us
  waiting for transfers between devices: 53.5 us -> 30.2 us
    pallas_call x2 -> x4, Pallas kernels: 104 us -> 193 us  [the longest x1 96.2 us: tail(): pl.pallas_call(lambda *refs: tail_kernel(outer, rest, groups, *refs), in_...]
    dot_general x7 -> x1, matrix products: 31.2 us -> 5.35 us  [dot_f32(): lax.dot_general(left, right, dims, preferred_element_type=jnp.float32)]
    ppermute x18 -> x4, starting transfers between devices: 27.9 us -> 4.9 us  [sum_shards(): lax.ppermute(block((me + step) % count), axis, place_shift(step, count))]
    dynamic_slice x9 -> x1, local copies, waits for them, and re-layouts: 23.2 us -> 2.72 us  [own_of(): split = lax.dynamic_index_in_dim(split, r, 1, keepdims=False)]
    reshape x7 -> x2, local copies, waits for them, and re-layouts: 22.6 us -> 2.92 us  [the longest x1 1.64 us: body(): jnp.moveaxis(w_parts, 0, 2).swapaxes(0, 1).reshape(width, 3 * own_cols)]
    reduce_sum x6 -> x4, other arithmetic: 18.8 us -> 1.68 us  [body(): jnp.sum(part[i].astype(jnp.float32), axis=0)]
    ppermute x4 -> x0, waiting for transfers between devices: 13.7 us -> none  [body(): got = lax.ppermute(pick(d_w_qkv, (a + step) % 4), ('c', 'a'), pairs)]
    unnamed x90 -> x99, local copies, waits for them, and re-layouts: 26.6 us -> 13.9 us
  transfers between devices with their start and end apart: 30 -> 13, of which waited for: 7 -> 4; matrix products, arithmetic and copies ran while one was open for 19% -> 9% of each run, Pallas kernels for 35% -> 41%
where the time goes in v2:
time: 613 us; the launch traced here: 604 us
  Pallas kernels  427 us (70%)
  starting transfers between devices  46.1 us (8%)
  local copies, waits for them, and re-layouts  41.7 us (7%)
  other arithmetic  38 us (6%)
  waiting for transfers between devices  30.2 us (5%)
  between operations  15.1 us (2%)
    pallas_call x1, Pallas kernels, entry(): pl.pallas_call(lambda *refs: entry_kernel(outer_count, rest_count, *refs)...  102 us
    pallas_call x1, Pallas kernels, tail(): pl.pallas_call(lambda *refs: tail_kernel(outer, rest, groups, *refs), in_...  96.2 us
    pallas_call x2, Pallas kernels, attention_back(): pl.pallas_call(backward_kernel, grid_spec=pltpu.PrefetchScalarGridSpec(nu...  74.6 us
    pallas_call x1, Pallas kernels, mlp(): pl.pallas_call(lambda *refs: mlp_kernel(outer, rest, *refs), grid=(tensor...  74.1 us
    pallas_call x1, Pallas kernels, attention(): pl.pallas_call(forward_kernel, grid_spec=pltpu.PrefetchScalarGridSpec(num...  58.2 us
    all_to_all x2, starting transfers between devices, body(): lax.all_to_all(sent, ('c', 'r'), split_axis=0, concat_axis=0, tiled=True)  21.6 us
    all_to_all x2, waiting for transfers between devices, body(): lax.all_to_all(sent, ('c', 'r'), split_axis=0, concat_axis=0, tiled=True)  20.9 us
    pallas_call x1, Pallas kernels, after(): pl.pallas_call(lambda *refs: after_kernel(rest, *refs), grid=(side_steps,...  15 us
  transfers between devices with their start and end apart: 13, of which 4 were waited for; matrix products, arithmetic and copies ran while one was open for 9% of the time, Pallas kernels for 41%

profile of v2, /device:TPU:0, one launch (start us, length us, event | category | flops | bytes accessed | tf_op | source)
XLA Modules:
  0.0 603.8 jit_solution(8518529627083184000)
XLA Ops:
  7.3 1.2 copy.78
  8.5 1.9 pad_maximum_fusion.3
  10.8 1.2 concatenate.26.refs_2_
  12.1 101.8 %shard_map.288 = (bf16[3072,1024]{1,0:T(8,128)(2,1)}, bf16[2,3,1024,128]{3,2,1,0:T(8,128)(2,1)}, bf16[8,4,16,256]{3,2,1,0:T(8,128)(2,1)}, s32[2,2,1,3072]{3,2,1,0:T(1,128)}) custom-call(bf16[2,384,1024]{2,1,0:T(8,128)(2,1)} %refs_0_.1, bf16[3,256,128]{2,1,0:T(8,128)(2,1)} %refs_1_.1, bf16[16,256]{1,0:T(8,128)(2,1)} %concatenate.26.refs_2_, s32[2,1,3072]{2,1,0:T(1,128)} %refs_3_.1), custom_call_target="tpu_custom_call" | custom-call | bytes 209715200 | tf_op jit(solution)/shard_map/pallas_call | solution.py:436
  113.9 1.3 dynamic-slice_bitcast_fusion.5
  115.2 7.5 %collective-permute-start = (bf16[384,1024]{1,0:T(8,128)(2,1)}, bf16[384,1024]{1,0:T(8,128)(2,1)}, u32[]{:S(2)}, u32[]{:S(2)}) collective-permute-start(bf16[384,1024]{1,0:T(8,128)(2,1)} %get-tuple-element.148), channel_id=1, source_target_pairs={{0,0},{2,4},{4,8},{6,12},{8,2},{10,6},{12,10},{14,14},{1,1},{3,5},... | collective-permute-start | bytes 2359304 | tf_op jit(solution)/shard_map/ppermute | solution.py:1161
  123.2 1.4 fusion.14
  126.4 3.6 copy.74
  130.0 1.6 reshape.153.refs_4_
  132.1 3.7 convert_reduce_fusion
  135.8 4.6 fusion.2
  141.2 5.0 fusion.5.refs_5_
  146.3 5.3 multiply_convert_fusion.q_ref.k_ref.v_ref
  151.6 58.2 %shard_map.289 = (bf16[3072,256]{1,0:T(8,128)(2,1)S(1)}, f32[2,6,2,512]{3,2,1,0:T(2,128)S(1)}) custom-call(s32[6]{0:T(128)S(1)} %get-tuple-element.163.low_ref, s32[6]{0:T(128)S(1)} %get-tuple-element.162.high_ref, bf16[3072,768]{1,0:T(8,128)(2,1)S(1)} %multiply_convert_fusion.q_ref.k_ref.v_ref, ...), custom_call_target="tpu_custom_call" | custom-call | flops 38654705664 | bytes 4718592 | tf_op jit(solution)/shard_map/pallas_call | solution.py:154
  209.8 1.2 copy.76
  211.1 1.2 copy-done.7
  212.2 18.0 %all-to-all-start = ((bf16[4,768,256]{2,1,0:T(8,128)(2,1)}), bf16[4,768,256]{2,1,0:T(8,128)(2,1)S(1)}, u32[]{:S(2)}, u32[]{:S(2)}) async-start(bf16[4,768,256]{2,1,0:T(8,128)(2,1)} %bitcast.136), calls=%async_computation | async-start | bytes 3145728 | tf_op jit(solution)/shard_map/all_to_all | solution.py:1277
  231.0 2.7 constant_dynamic-slice_fusion.3
  233.7 1.5 select_bitcast_fusion.3
  235.2 1.3 pad_maximum_fusion.1
  236.5 13.8 %all-to-all-done.refs_0_.refs_5_ = bf16[4,768,256]{2,1,0:T(8,128)(2,1)S(1)} async-done(((bf16[4,768,256]{2,1,0:T(8,128)(2,1)}), bf16[4,768,256]{2,1,0:T(8,128)(2,1)S(1)}, u32[]{:S(2)}, u32[]{:S(2)}) %all-to-all-start) | async-done | bytes 1572896 | tf_op jit(solution)/shard_map/all_to_all | solution.py:1277
  250.3 7.5 %shard_map.290 = (f32[768,1024]{1,0:T(8,128)}, f32[768,1024]{1,0:T(8,128)}, bf16[768,1024]{1,0:T(8,128)(2,1)S(1)}, bf16[768,1024]{1,0:T(8,128)(2,1)S(1)}) custom-call(bf16[4,768,256]{2,1,0:T(8,128)(2,1)S(1)} %all-to-all-done.refs_0_.refs_5_, bf16[768,1024]{1,0:T(8,128)(2,1)} %bitcast.138, bf16[768,1024]{1,0:T(8,128)(2,1)} %bitcast.132, ...), custom_call_target="tpu_custom_call" | custom-call | flops 3221225472 | bytes 16777216 | tf_op jit(solution)/shard_map/pallas_call | solution.py:1092
  260.1 74.1 %shard_map.291 = (f32[768,1024]{1,0:T(8,128)}, f32[768,1024]{1,0:T(8,128)}, bf16[4,2,256,512]{3,2,1,0:T(8,128)(2,1)}, bf16[1,4,2,256,512]{4,3,2,1,0:T(8,128)(2,1...) custom-call(bf16[768,1024]{1,0:T(8,128)(2,1)} %copy-done.12, ...), custom_call_target="tpu_custom_call" | custom-call | flops 38654705664 | bytes 67108864 | tf_op jit(solution)/shard_map/pallas_call | solution.py:954
  334.3 3.0 fusion.7
  338.4 1.2 dynamic-slice_bitcast_fusion
  339.6 2.6 collective-permute-start.3
  344.1 15.0 %shard_map.292 = (bf16[768,1024]{1,0:T(8,128)(2,1)}, f32[768,1024]{1,0:T(8,128)}, bf16[4,768,256]{2,1,0:T(8,128)(2,1)}, f32[8,1024]{1,0:T(8,128)}, bf16[8,2,256,...) custom-call(f32[768,1024]{1,0:T(8,128)} %get-tuple-element.89.refs_0_, f32[768,1024]{1,0:T(8,128)} %get-tuple-element.90.refs_1_, ...), custom_call_target="tpu_custom_call" | custom-call | flops 6442450944 | bytes 25165824 | tf_op jit(solution)/shard_map/pallas_call | solution.py:1115
  359.2 3.6 all-to-all-start.1
  362.9 2.7 fusion.19.refs_2_
  365.7 2.2 collective-permute-done.2
  367.9 2.8 fusion.9
  370.7 2.6 fusion.8
  373.2 2.5 add_convert_fusion
  375.8 7.1 %all-to-all-done.1 = bf16[4,768,256]{2,1,0:T(8,128)(2,1)S(1)} async-done(((bf16[4,768,256]{2,1,0:T(8,128)(2,1)}), bf16[4,768,256]{2,1,0:T(8,128)(2,1)S(1)}, u32[]{:S(2)}, u32[]{:S(2)}) %all-to-all-start.1) | async-done | bytes 1572896 | tf_op jit(solution)/shard_map/all_to_all | solution.py:1290
  382.9 1.3 copy.81
  385.0 1.5 pad_maximum_fusion
  386.5 6.8 %all-to-all-start.2 = ((bf16[4,2,256,512]{3,2,1,0:T(8,128)(2,1)}), bf16[4,2,256,512]{3,2,1,0:T(8,128)(2,1)}, u32[]{:S(2)}, u32[]{:S(2)}) async-start(bf16[4,2,256,512]{3,2,1,0:T(8,128)(2,1)} %pad_maximum_fusion), calls=%async_computation.2 | async-start | bytes 4194304 | tf_op jit(solution)/shard_map/all_to_all | solution.py:1300
  393.3 1.2 collective-permute-start.5
  394.5 1.5 dynamic-slice_bitcast_fusion.3
  396.8 4.5 collective-permute-start.8
  401.2 37.3 %shard_map.293 = (bf16[3072,128]{1,0:T(8,128)(2,1)S(1)}, bf16[3072,128]{1,0:T(8,128)(2,1)S(1)}, bf16[3072,128]{1,0:T(8,128)(2,1)S(1)}) custom-call(s32[6]{0:T(128)S(1)} %get-tuple-element.163.low_ref, s32[6]{0:T(128)S(1)} %get-tuple-element.162.high_ref, bf16[3072,768]{1,0:T(8,128)(2,1)} %copy-done.14, bf16[3072,768]{1,0:T(8,128)(2,1)} %copy-done.14, ...), custom_call_target="tpu_custom_call" | custom-call | flops 24159191040 | bytes 9437184 | tf_op jit(solution)/shard_map/pallas_call | solution.py:182
  438.8 2.1 copy-done.6
  440.8 37.3 %shard_map.294 = (bf16[3072,128]{1,0:T(8,128)(2,1)S(1)}, bf16[3072,128]{1,0:T(8,128)(2,1)S(1)}, bf16[3072,128]{1,0:T(8,128)(2,1)S(1)}) custom-call(s32[6]{0:T(128)S(1)} %get-tuple-element.163.low_ref, s32[6]{0:T(128)S(1)} %get-tuple-element.162.high_ref, bf16[3072,768]{1,0:T(8,128)(2,1)} %copy-done.14, bf16[3072,768]{1,0:T(8,128)(2,1)} %copy-done.14, ...), custom_call_target="tpu_custom_call" | custom-call | flops 24159191040 | bytes 9437184 | tf_op jit(solution)/shard_map/pallas_call | solution.py:182
  478.5 1.5 pad_maximum_fusion.2
  480.0 7.0 %collective-permute-done.6 = bf16[4,256,128]{2,1,0:T(8,128)(2,1)S(1)} collective-permute-done((bf16[4,256,128]{2,1,0:T(8,128)(2,1)S(1)}, bf16[4,256,128]{2,1,0:T(8,128)(2,1)S(1)}, u32[]{:S(2)}, u32[]{:S(2)}) %collective-permute-start.6) | collective-permute-done | bytes 262176 | tf_op jit(solution)/shard_map/ppermute | solution.py:1185
  490.6 96.2 %shard_map.295 = (f32[16,256]{1,0:T(8,128)}, bf16[2,384,1024]{2,1,0:T(8,128)(2,1)}, f32[3,256,128]{2,1,0:T(8,128)}, f32[256,512]{1,0:T(8,128)}, f32[512,256]{1,0:T(8,128)}, /*index=5*/f32[128,256]{1,0:T(8,128)}) custom-call(f32[4,16,256]{2,1,0:T(8,128)} %select_maximum_fusion.refs_0_, f32[1,1024]{1,0:T(1,128)} %bitcast.156, ...), custom_call_target="tpu_custom_call" | custom-call | bytes 262144000 | tf_op jit(solution)/shard_map/pallas_call | solution.py:748
  588.3 1.6 fusion.16
  591.0 2.8 copy.110
  (173 shorter events, 21.2 us)
Async XLA Ops:
  7.2 3.3 copy-start.35
  7.2 3.4 copy-start.36
  7.2 3.5 copy-start.37
  7.2 3.5 copy-start.38
  7.2 3.5 copy-start.39
  7.2 3.5 copy-start.40
  7.2 3.5 copy-start.41
  7.3 3.5 copy-start.42
  7.3 3.5 copy-start.43
  7.3 3.5 copy-start.44
  7.3 106.6 %copy-start.26 = (bf16[2,384,1024]{2,1,0:T(8,128)(2,1)S(1)}, bf16[2,384,1024]{2,1,0:T(8,128)(2,1)}, u32[]{:S(2)}) copy-start(bf16[2,384,1024]{2,1,0:T(8,128)(2,1)} %param.19) | copy-start | bytes 4718596
  7.3 243.1 %all-gather.3.cloned.1.call-start = ((), (), s32[]{:S(2)}) async-start(), calls=%async_computation.3 | async-start | bytes 19464192 | tf_op jit(solution)/shard_map/all_gather | solution.py:1136
  115.2 118.5 %collective-permute-start = (bf16[384,1024]{1,0:T(8,128)(2,1)}, bf16[384,1024]{1,0:T(8,128)(2,1)}, u32[]{:S(2)}, u32[]{:S(2)}) collective-permute-start(bf16[384,1024]{1,0:T(8,128)(2,1)} %get-tuple-element.148), channel_id=1, source_target_pairs={{0,0},{2,4},{4,8},{6,12},{8,2},{10,6},{12,10},{14,14},{1,1},{3,5},... | collective-permute-start | bytes 2359304 | tf_op jit(solution)/shard_map/ppermute | solution.py:1161
  122.7 111.0 %collective-permute-start.1 = (bf16[384,1024]{1,0:T(8,128)(2,1)}, bf16[384,1024]{1,0:T(8,128)(2,1)}, u32[]{:S(2)}, u32[]{:S(2)}) collective-permute-start(bf16[384,1024]{1,0:T(8,128)(2,1)} %get-tuple-element.149), channel_id=1, source_target_pairs={{0,4},{2,0},{4,12},{6,8},{8,6},{10,2},{12,14},{14,10},{1,5},{3,1},... | collective-permute-start | bytes 2359304 | tf_op jit(solution)/shard_map/ppermute | solution.py:1161
  126.4 274.8 %copy-start.5 = (s32[3072,1]{1,0:T(8,128)}, s32[3072,1]{1,0:T(8,128)S(1)}, u32[]{:S(2)}) copy-start(s32[3072,1]{1,0:T(8,128)S(1)} %copy.83.idk_ref) | copy-start | bytes 36868
  141.2 109.2 %copy-start.11 = (f32[4,8,256]{2,1,0:T(8,128)}, f32[4,8,256]{2,1,0:T(8,128)S(1)}, u32[]{:S(2)}) copy-start(f32[4,8,256]{2,1,0:T(8,128)S(1)} %get-tuple-element.150) | copy-start | bytes 98308
  141.2 5.1 copy-start.33
  141.2 5.1 copy-start.19
  141.2 5.1 copy-start.45
  146.3 5.4 copy-start.15
  151.6 58.2 %copy-start.14 = (bf16[3072,768]{1,0:T(8,128)(2,1)}, bf16[3072,768]{1,0:T(8,128)(2,1)S(1)}, u32[]{:S(2)}) copy-start(bf16[3072,768]{1,0:T(8,128)(2,1)S(1)} %multiply_convert_fusion.q_ref.k_ref.v_ref) | copy-start | bytes 14155780
  212.2 38.1 %all-to-all-start = ((bf16[4,768,256]{2,1,0:T(8,128)(2,1)}), bf16[4,768,256]{2,1,0:T(8,128)(2,1)S(1)}, u32[]{:S(2)}, u32[]{:S(2)}) async-start(bf16[4,768,256]{2,1,0:T(8,128)(2,1)} %bitcast.136), calls=%async_computation | async-start | bytes 3145728 | tf_op jit(solution)/shard_map/all_to_all | solution.py:1277
  250.3 7.5 %copy-start = (bf16[4,768,256]{2,1,0:T(8,128)(2,1)}, bf16[4,768,256]{2,1,0:T(8,128)(2,1)S(1)}, u32[]{:S(2)}) copy-start(bf16[4,768,256]{2,1,0:T(8,128)(2,1)S(1)} %all-to-all-done.refs_0_.refs_5_) | copy-start | bytes 4718596
  334.2 3.5 copy-start.25
  337.3 4.9 copy-start.18
  338.4 4.8 copy-start.16
  339.6 31.0 %collective-permute-start.3 = (bf16[4,256,512]{2,1,0:T(8,128)(2,1)}, bf16[4,256,512]{2,1,0:T(8,128)(2,1)}, u32[]{:S(2)}, u32[]{:S(2)}) collective-permute-start(bf16[4,256,512]{2,1,0:T(8,128)(2,1)} %dynamic-slice_bitcast_fusion), channel_id=1, source_target_pairs={{0,1},{1,0},{2,3},{3,2},{4,5},{5,4},{6,7},{7,6},{8,9},{9,8},{10,11... | collective-permute-start | bytes 3145736 | tf_op jit(solution)/shard_map/ppermute | solution.py:1185
  343.3 24.6 %collective-permute-start.2 = (bf16[4,256,512]{2,1,0:T(8,128)(2,1)}, bf16[4,256,512]{2,1,0:T(8,128)(2,1)}, u32[]{:S(2)}, u32[]{:S(2)}) collective-permute-start(bf16[4,256,512]{2,1,0:T(8,128)(2,1)} %dynamic-slice_bitcast_fusion.1), channel_id=1, source_target_pairs={{0,16},{16,0},{1,17},{17,1},{2,18},{18,2},{3,19},{19,3},{4,20},{20... | collective-permute-start | bytes 3145736 | tf_op jit(solution)/shard_map/ppermute | solution.py:1185
  359.2 14.1 %collective-permute-start.4 = (bf16[8,2,256,128]{3,2,1,0:T(8,128)(2,1)}, bf16[8,2,256,128]{3,2,1,0:T(8,128)(2,1)}, u32[]{:S(2)}, u32[]{:S(2)}) collective-permute-start(bf16[8,2,256,128]{3,2,1,0:T(8,128)(2,1)} %get-tuple-element.97), channel_id=1, source_target_pairs={{0,8},{8,0},{1,9},{9,1},{2,10},{10,2},{3,11},{11,3},{4,12},{12,4},... | collective-permute-start | bytes 3145736 | tf_op jit(solution)/shard_map/ppermute | solution.py:1210
  359.2 23.6 %all-to-all-start.1 = ((bf16[4,768,256]{2,1,0:T(8,128)(2,1)}), bf16[4,768,256]{2,1,0:T(8,128)(2,1)S(1)}, u32[]{:S(2)}, u32[]{:S(2)}) async-start(bf16[4,768,256]{2,1,0:T(8,128)(2,1)} %get-tuple-element.93), calls=%async_computation.1 | async-start | bytes 3145728 | tf_op jit(solution)/shard_map/all_to_all | solution.py:1290
  365.6 5.1 copy-start.17
  386.5 6.8 %copy-start.20 = (bf16[8,2,256,128]{3,2,1,0:T(8,128)(2,1)S(1)}, bf16[8,2,256,128]{3,2,1,0:T(8,128)(2,1)}, u32[]{:S(2)}) copy-start(bf16[8,2,256,128]{3,2,1,0:T(8,128)(2,1)} %add_convert_fusion) | copy-start | bytes 3145732
  386.5 101.3 %all-to-all-start.2 = ((bf16[4,2,256,512]{3,2,1,0:T(8,128)(2,1)}), bf16[4,2,256,512]{3,2,1,0:T(8,128)(2,1)}, u32[]{:S(2)}, u32[]{:S(2)}) async-start(bf16[4,2,256,512]{3,2,1,0:T(8,128)(2,1)} %pad_maximum_fusion), calls=%async_computation.2 | async-start | bytes 4194304 | tf_op jit(solution)/shard_map/all_to_all | solution.py:1300
  393.3 8.0 %copy-start.8 = (bf16[3072,256]{1,0:T(8,128)(2,1)S(1)}, bf16[3072,256]{1,0:T(8,128)(2,1)}, u32[]{:S(2)}) copy-start(bf16[3072,256]{1,0:T(8,128)(2,1)} %copy-done.7) | copy-start | bytes 4718596
  393.3 45.3 %collective-permute-start.5 = (bf16[4,2,256,128]{3,2,0,1:T(8,128)(2,1)S(1)}, bf16[4,2,256,128]{3,2,0,1:T(8,128)(2,1)S(1)}, u32[]{:S(2)}, u32[]{:S(2)}) collective-permute-start(bf16[4,2,256,128]{3,2,0,1:T(8,128)(2,1)S(1)} %copy_bitcast_fusion), channel_id=1, source_target_pairs={{0,16},{16,0},{1,17},{17,1},{2,18},{18,2},{3,19},{19,3},{4,20},{20... | collective-permute-start | bytes 1572872 | tf_op jit(solution)/shard_map/ppermute | solution.py:1185
  396.0 82.4 %collective-permute-start.7 = (bf16[384,1024]{1,0:T(8,128)(2,1)S(1)}, bf16[384,1024]{1,0:T(8,128)(2,1)S(1)}, u32[]{:S(2)}, u32[]{:S(2)}) collective-permute-start(bf16[384,1024]{1,0:T(8,128)(2,1)S(1)} %get-tuple-element.144), channel_id=1, source_target_pairs={{0,0},{4,2},{8,4},{12,6},{2,8},{6,10},{10,12},{14,14},{1,1},{5,3},... | collective-permute-start | bytes 2359304 | tf_op jit(solution)/shard_map/ppermute | solution.py:1170
  396.8 81.6 %collective-permute-start.8 = (bf16[384,1024]{1,0:T(8,128)(2,1)S(1)}, bf16[384,1024]{1,0:T(8,128)(2,1)S(1)}, u32[]{:S(2)}, u32[]{:S(2)}) collective-permute-start(bf16[384,1024]{1,0:T(8,128)(2,1)S(1)} %get-tuple-element.145), channel_id=1, source_target_pairs={{4,0},{0,2},{12,4},{8,6},{6,8},{2,10},{14,12},{10,14},{5,1},{1,3},... | collective-permute-start | bytes 2359304 | tf_op jit(solution)/shard_map/ppermute | solution.py:1170
  401.2 37.4 %copy-start.21 = (bf16[8,2,256,128]{3,2,1,0:T(8,128)(2,1)S(1)}, bf16[8,2,256,128]{3,2,1,0:T(8,128)(2,1)}, u32[]{:S(2)}) copy-start(bf16[8,2,256,128]{3,2,1,0:T(8,128)(2,1)} %add_convert_fusion) | copy-start | bytes 3145732
  438.6 39.5 %copy-start.9 = (bf16[3072,128]{1,0:T(8,128)(2,1)}, bf16[3072,128]{1,0:T(8,128)(2,1)S(1)}, u32[]{:S(2)}) copy-start(bf16[3072,128]{1,0:T(8,128)(2,1)S(1)} %get-tuple-element.126.refs_9_) | copy-start | bytes 2359300
  438.6 49.2 %copy-start.1 = (bf16[3072,128]{1,0:T(8,128)(2,1)}, bf16[3072,128]{1,0:T(8,128)(2,1)S(1)}, u32[]{:S(2)}) copy-start(bf16[3072,128]{1,0:T(8,128)(2,1)S(1)} %get-tuple-element.119.refs_8_) | copy-start | bytes 2359300
  438.6 50.1 %copy-start.2 = (bf16[3072,128]{1,0:T(8,128)(2,1)}, bf16[3072,128]{1,0:T(8,128)(2,1)S(1)}, u32[]{:S(2)}) copy-start(bf16[3072,128]{1,0:T(8,128)(2,1)S(1)} %get-tuple-element.121.refs_10_) | copy-start | bytes 2359300
  478.1 10.1 %copy-start.3 = (bf16[3072,128]{1,0:T(8,128)(2,1)}, bf16[3072,128]{1,0:T(8,128)(2,1)S(1)}, u32[]{:S(2)}) copy-start(bf16[3072,128]{1,0:T(8,128)(2,1)S(1)} %get-tuple-element.120.refs_11_) | copy-start | bytes 2359300
  478.1 11.0 %copy-start.4 = (bf16[3072,128]{1,0:T(8,128)(2,1)}, bf16[3072,128]{1,0:T(8,128)(2,1)S(1)}, u32[]{:S(2)}) copy-start(bf16[3072,128]{1,0:T(8,128)(2,1)S(1)} %get-tuple-element.122.refs_13_) | copy-start | bytes 2359300
  478.2 8.9 %collective-permute-start.6 = (bf16[4,256,128]{2,1,0:T(8,128)(2,1)S(1)}, bf16[4,256,128]{2,1,0:T(8,128)(2,1)S(1)}, u32[]{:S(2)}, u32[]{:S(2)}) collective-permute-start(bf16[4,256,128]{2,1,0:T(8,128)(2,1)S(1)} %dynamic-slice_bitcast_fusion.6), channel_id=1, source_target_pairs={{0,1},{1,0},{2,3},{3,2},{4,5},{5,4},{6,7},{7,6},{8,9},{9,8},{10,11... | collective-permute-start | bytes 786440 | tf_op jit(solution)/shard_map/ppermute | solution.py:1185
  586.8 7.0 %copy-start.30 = (f32[3,256,128]{2,1,0:T(8,128)S(1)}, f32[3,256,128]{2,1,0:T(8,128)}, u32[]{:S(2)}) copy-start(f32[3,256,128]{2,1,0:T(8,128)} %get-tuple-element.184) | copy-start | bytes 1179652
  586.8 7.7 %copy-start.31 = (f32[128,256]{1,0:T(8,128)S(1)}, f32[128,256]{1,0:T(8,128)}, u32[]{:S(2)}) copy-start(f32[128,256]{1,0:T(8,128)} %get-tuple-element.186) | copy-start | bytes 393220
  591.0 4.2 copy-start.29
  591.0 5.0 copy-start.28
  (11 other events, 22.4 us)
Sparse Core Ops, SparseCore 0:
  11.0 194.8 all-gather.2

commit v3 on v2

--- a/solution.py
+++ b/solution.py
@@ -10,6 +10,7 @@
 norm_eps = 1e-06
 mask_fill = -1e30
 query_rows = 512
+back_rows = 256
 key_rows = 512
 contract_rows = (((0,), (0,)), ((), ()))
 contract_cols = (((1,), (1,)), ((), ()))
@@ -133,14 +134,14 @@
         dv_ref[...] = dv_sum[...].astype(dv_ref.dtype)
 
 
-def column_specs(tok_count, col_blocks, group=0):
-    q_spec = pl.BlockSpec((query_rows, 128), lambda g, i, *_: (i, group + g))
+def column_specs(tok_count, col_blocks, rows, group=0):
+    q_spec = pl.BlockSpec((rows, 128), lambda g, i, *_: (i, group + g))
     k_spec = pl.BlockSpec((tok_count, 128), lambda g, i, *_: (0, col_blocks + group + g))
     v_spec = pl.BlockSpec((tok_count, 128), lambda g, i, *_: (0, 2 * col_blocks + group + g))
-    idq_spec = pl.BlockSpec((1, query_rows), lambda g, i, *_: (0, i))
+    idq_spec = pl.BlockSpec((1, rows), lambda g, i, *_: (0, i))
     idk_spec = pl.BlockSpec((tok_count, 1), lambda g, i, *_: (0, 0))
     lse_spec = pl.BlockSpec(
-        (1, 1, 128 // HEAD_DIM, query_rows), lambda g, i, *_: (group + g, i, 0, 0)
+        (1, 1, 128 // HEAD_DIM, rows), lambda g, i, *_: (group + g, i, 0, 0)
     )
     return q_spec, k_spec, v_spec, idq_spec, idk_spec, lse_spec
 
@@ -149,7 +150,7 @@
     tok_count, cols3 = qkv.shape
     cols = cols3 // 3
     blocks, groups = tok_count // query_rows, cols // 128
-    q_spec, k_spec, v_spec, idq_spec, idk_spec, lse_spec = column_specs(tok_count, groups)
+    q_spec, k_spec, v_spec, idq_spec, idk_spec, lse_spec = column_specs(tok_count, groups, query_rows)
     pairs = tok_count * tok_count // 2
     return pl.pallas_call(
         forward_kernel,
@@ -173,10 +174,12 @@
 def attention_back(qkv, bounds, ids_row, ids_col, att, d_att, lse, group):
     tok_count, cols3 = qkv.shape
     cols = cols3 // 3
-    blocks, groups = tok_count // query_rows, cols // 128
-    q_spec, k_spec, v_spec, idq_spec, idk_spec, lse_spec = column_specs(tok_count, groups, group)
+    blocks, groups = tok_count // back_rows, cols // 128
+    q_spec, k_spec, v_spec, idq_spec, idk_spec, lse_spec = column_specs(
+        tok_count, groups, back_rows, group
+    )
     pairs = tok_count * tok_count // 2
-    out_spec = pl.BlockSpec((query_rows, 128), lambda g, i, *_: (i, 0))
+    out_spec = pl.BlockSpec((back_rows, 128), lambda g, i, *_: (i, 0))
     out_whole = pl.BlockSpec((tok_count, 128), lambda g, i, *_: (0, 0))
     one = jax.ShapeDtypeStruct((tok_count, 128), jnp.bfloat16)
     return pl.pallas_call(
@@ -1247,12 +1250,14 @@
     scale_qkv = jnp.concatenate([jnp.full((own_cols,), 0.125), jnp.ones((2 * own_cols,))])
 
     run_ids = pick(pick(ids, a % 2), a // 2)[0]
-    blocks = tok_count // query_rows
-    first = run_ids.reshape(blocks, query_rows)[:, :1]
-    last = run_ids.reshape(blocks, query_rows)[:, -1:]
-    low = jnp.sum((run_ids[None] < first).astype(jnp.int32), axis=-1) // key_rows
-    reach = jnp.sum((run_ids[None] <= last).astype(jnp.int32), axis=-1)
-    bounds = (low, (reach + key_rows - 1) // key_rows)
+
+    def key_bounds(rows):
+        split = run_ids.reshape(tok_count // rows, rows)
+        low = jnp.sum((run_ids[None] < split[:, :1]).astype(jnp.int32), axis=-1) // key_rows
+        reach = jnp.sum((run_ids[None] <= split[:, -1:]).astype(jnp.int32), axis=-1)
+        return low, (reach + key_rows - 1) // key_rows
+
+    bounds, back_bounds = key_bounds(query_rows), key_bounds(back_rows)
     ids_row, ids_col = run_ids[None, :], run_ids[:, None]
 
     weights = gather_parts(jnp.concatenate([fc1_weight.T, fc2_weight, proj_weight]))
@@ -1269,6 +1274,8 @@
     qkv = ((dot_f32(normed_all_low, w_qkv) + bias_qkv) * scale_qkv).astype(jnp.bfloat16)
     grad_moved = move_in(out_grad)
     att_heads, lse = attention(qkv, bounds, ids_row, ids_col)
+    lse = lse.reshape(*lse.shape[:3], query_rows // back_rows, back_rows)
+    lse = jnp.swapaxes(lse, 2, 3).reshape(lse.shape[0], -1, lse.shape[2], back_rows)
 
     rows_own = own_of(seq_rows)
     grad_top = grad_moved.reshape(own_rows, width)
@@ -1303,7 +1310,7 @@
     d_parts = []
     for group in range(groups):
         d_parts.append(
-            attention_back(qkv, bounds, ids_row, ids_col, att_heads, d_heads, lse, group)
+            attention_back(qkv, back_bounds, ids_row, ids_col, att_heads, d_heads, lse, group)
         )
         if group == 0:
             d_parts, d_heads, grad_proj = lax.optimization_barrier((d_parts, d_heads, grad_proj))

time: 613 us -> 617 us (level)
  Pallas kernels: 427 us -> 436 us
    pallas_call x2, Pallas kernels: 74.6 us -> 82.3 us  [attention_back(): pl.pallas_call(backward_kernel, grid_spec=pltpu.PrefetchScalarGridSpec(nu...]
  transfers between devices with their start and end apart: 13 -> 13, of which waited for: 4 -> 4; matrix products, arithmetic and copies ran while one was open for 9% -> 9% of each run, Pallas kernels for 41% -> 43%
where the time goes in v3:
time: 617 us; the launch traced here: 609 us
  Pallas kernels  436 us (71%)
  starting transfers between devices  42.5 us (7%)
  local copies, waits for them, and re-layouts  41.9 us (7%)
  other arithmetic  38.4 us (6%)
  waiting for transfers between devices  29.1 us (5%)
  between operations  15.2 us (2%)
    pallas_call x1, Pallas kernels, entry(): pl.pallas_call(lambda *refs: entry_kernel(outer_count, rest_count, *refs)...  102 us
    pallas_call x1, Pallas kernels, tail(): pl.pallas_call(lambda *refs: tail_kernel(outer, rest, groups, *refs), in_...  92.4 us
    pallas_call x2, Pallas kernels, attention_back(): pl.pallas_call(backward_kernel, grid_spec=pltpu.PrefetchScalarGridSpec(nu...  82.3 us
    pallas_call x1, Pallas kernels, mlp(): pl.pallas_call(lambda *refs: mlp_kernel(outer, rest, *refs), grid=(tensor...  74.1 us
    pallas_call x1, Pallas kernels, attention(): pl.pallas_call(forward_kernel, grid_spec=pltpu.PrefetchScalarGridSpec(num...  63.1 us
    all_to_all x2, starting transfers between devices, body(): lax.all_to_all(sent, ('c', 'r'), split_axis=0, concat_axis=0, tiled=True)  21.6 us
    all_to_all x2, waiting for transfers between devices, body(): lax.all_to_all(sent, ('c', 'r'), split_axis=0, concat_axis=0, tiled=True)  20.4 us
    pallas_call x1, Pallas kernels, after(): pl.pallas_call(lambda *refs: after_kernel(rest, *refs), grid=(side_steps,...  15 us
  transfers between devices with their start and end apart: 13, of which 4 were waited for; matrix products, arithmetic and copies ran while one was open for 9% of the time, Pallas kernels for 43%

profile of v3, /device:TPU:0, one launch (start us, length us, event | category | flops | bytes accessed | tf_op | source)
XLA Modules:
  0.0 608.7 jit_solution(7715656553265813947)
XLA Ops:
  7.3 1.2 copy.78
  8.5 1.9 pad_maximum_fusion.3
  10.8 1.2 concatenate.29.refs_2_
  12.1 101.8 %shard_map.288 = (bf16[3072,1024]{1,0:T(8,128)(2,1)}, bf16[2,3,1024,128]{3,2,1,0:T(8,128)(2,1)}, bf16[8,4,16,256]{3,2,1,0:T(8,128)(2,1)}, s32[2,2,1,3072]{3,2,1,0:T(1,128)}) custom-call(bf16[2,384,1024]{2,1,0:T(8,128)(2,1)} %refs_0_.1, bf16[3,256,128]{2,1,0:T(8,128)(2,1)} %refs_1_.1, bf16[16,256]{1,0:T(8,128)(2,1)} %concatenate.29.refs_2_, s32[2,1,3072]{2,1,0:T(1,128)} %refs_3_.1), custom_call_target="tpu_custom_call" | custom-call | bytes 209715200 | tf_op jit(solution)/shard_map/pallas_call | solution.py:439
  113.9 1.3 dynamic-slice_bitcast_fusion.5
  115.2 7.5 %collective-permute-start = (bf16[384,1024]{1,0:T(8,128)(2,1)}, bf16[384,1024]{1,0:T(8,128)(2,1)}, u32[]{:S(2)}, u32[]{:S(2)}) collective-permute-start(bf16[384,1024]{1,0:T(8,128)(2,1)} %get-tuple-element.152), channel_id=1, source_target_pairs={{0,0},{2,4},{4,8},{6,12},{8,2},{10,6},{12,10},{14,14},{1,1},{3,5},... | collective-permute-start | bytes 2359304 | tf_op jit(solution)/shard_map/ppermute | solution.py:1164
  123.2 1.4 fusion.14
  126.4 3.6 copy.74
  130.0 1.6 reshape.158.refs_4_
  132.1 3.7 convert_reduce_fusion
  135.8 4.6 fusion.2
  141.2 5.0 fusion.5.refs_5_
  146.2 5.3 multiply_convert_fusion.q_ref.k_ref.v_ref
  151.6 63.1 %shard_map.289 = (bf16[3072,256]{1,0:T(8,128)(2,1)S(1)}, f32[2,6,2,512]{3,2,1,0:T(2,128)S(1)}) custom-call(s32[6]{0:T(128)S(1)} %get-tuple-element.169.low_ref, s32[6]{0:T(128)S(1)} %get-tuple-element.168.high_ref, bf16[3072,768]{1,0:T(8,128)(2,1)S(1)} %multiply_convert_fusion.q_ref.k_ref.v_ref, ...), custom_call_target="tpu_custom_call" | custom-call | flops 38654705664 | bytes 4718592 | tf_op jit(solution)/shard_map/pallas_call | solution.py:155
  214.7 1.2 copy.76
  217.1 18.0 %all-to-all-start = ((bf16[4,768,256]{2,1,0:T(8,128)(2,1)}), bf16[4,768,256]{2,1,0:T(8,128)(2,1)S(1)}, u32[]{:S(2)}, u32[]{:S(2)}) async-start(bf16[4,768,256]{2,1,0:T(8,128)(2,1)} %bitcast.139), calls=%async_computation | async-start | bytes 3145728 | tf_op jit(solution)/shard_map/all_to_all | solution.py:1284
  236.3 2.7 constant_dynamic-slice_fusion.3
  239.0 1.5 select_bitcast_fusion.3
  240.5 1.3 pad_maximum_fusion.1
  241.8 13.4 %all-to-all-done.refs_0_.refs_5_ = bf16[4,768,256]{2,1,0:T(8,128)(2,1)S(1)} async-done(((bf16[4,768,256]{2,1,0:T(8,128)(2,1)}), bf16[4,768,256]{2,1,0:T(8,128)(2,1)S(1)}, u32[]{:S(2)}, u32[]{:S(2)}) %all-to-all-start) | async-done | bytes 1572896 | tf_op jit(solution)/shard_map/all_to_all | solution.py:1284
  255.2 7.5 %shard_map.290 = (f32[768,1024]{1,0:T(8,128)}, f32[768,1024]{1,0:T(8,128)}, bf16[768,1024]{1,0:T(8,128)(2,1)S(1)}, bf16[768,1024]{1,0:T(8,128)(2,1)S(1)}) custom-call(bf16[4,768,256]{2,1,0:T(8,128)(2,1)S(1)} %all-to-all-done.refs_0_.refs_5_, bf16[768,1024]{1,0:T(8,128)(2,1)} %bitcast.141, bf16[768,1024]{1,0:T(8,128)(2,1)} %bitcast.135, ...), custom_call_target="tpu_custom_call" | custom-call | flops 3221225472 | bytes 16777216 | tf_op jit(solution)/shard_map/pallas_call | solution.py:1095
  263.8 1.2 copy-done.13
  265.0 74.1 %shard_map.291 = (f32[768,1024]{1,0:T(8,128)}, f32[768,1024]{1,0:T(8,128)}, bf16[4,2,256,512]{3,2,1,0:T(8,128)(2,1)}, bf16[1,4,2,256,512]{4,3,2,1,0:T(8,128)(2,1...) custom-call(bf16[768,1024]{1,0:T(8,128)(2,1)} %copy-done.12, ...), custom_call_target="tpu_custom_call" | custom-call | flops 38654705664 | bytes 67108864 | tf_op jit(solution)/shard_map/pallas_call | solution.py:957
  339.1 3.0 fusion.7
  343.3 1.2 dynamic-slice_bitcast_fusion
  344.5 2.6 collective-permute-start.3
  349.0 15.0 %shard_map.292 = (bf16[768,1024]{1,0:T(8,128)(2,1)}, f32[768,1024]{1,0:T(8,128)}, bf16[4,768,256]{2,1,0:T(8,128)(2,1)}, f32[8,1024]{1,0:T(8,128)}, bf16[8,2,256,...) custom-call(f32[768,1024]{1,0:T(8,128)} %get-tuple-element.89.refs_0_, f32[768,1024]{1,0:T(8,128)} %get-tuple-element.90.refs_1_, ...), custom_call_target="tpu_custom_call" | custom-call | flops 6442450944 | bytes 25165824 | tf_op jit(solution)/shard_map/pallas_call | solution.py:1118
  364.0 3.6 all-to-all-start.1
  367.8 2.7 fusion.20.refs_2_
  370.6 2.2 collective-permute-done.2
  372.7 2.8 fusion.9
  375.6 2.5 fusion.8
  378.1 2.6 add_convert_fusion
  380.7 7.0 %all-to-all-done.1 = bf16[4,768,256]{2,1,0:T(8,128)(2,1)S(1)} async-done(((bf16[4,768,256]{2,1,0:T(8,128)(2,1)}), bf16[4,768,256]{2,1,0:T(8,128)(2,1)S(1)}, u32[]{:S(2)}, u32[]{:S(2)}) %all-to-all-start.1) | async-done | bytes 1572896 | tf_op jit(solution)/shard_map/all_to_all | solution.py:1297
  387.7 1.3 copy.81
  389.8 1.5 pad_maximum_fusion
  391.3 4.6 all-to-all-start.2
  395.9 1.2 collective-permute-start.5
  397.2 1.5 dynamic-slice_bitcast_fusion.3
  399.4 3.2 collective-permute-start.8
  402.6 41.2 %shard_map.293 = (bf16[3072,128]{1,0:T(8,128)(2,1)S(1)}, bf16[3072,128]{1,0:T(8,128)(2,1)S(1)}, bf16[3072,128]{1,0:T(8,128)(2,1)S(1)}) custom-call(s32[12]{0:T(128)S(1)} %get-tuple-element.171.low_ref, s32[12]{0:T(128)S(1)} %get-tuple-element.170.high_ref, bf16[3072,768]{1,0:T(8,128)(2,1)} %copy-done.14, bf16[3072,768]{1,0:T(8,128)(2,1)} %copy-done.14, ...), custom_call_target="tpu_custom_call" | custom-call | flops 24159191040 | bytes 9437184 | tf_op jit(solution)/shard_map/pallas_call | solution.py:185
  444.0 2.1 copy-done.6
  446.0 41.2 %shard_map.294 = (bf16[3072,128]{1,0:T(8,128)(2,1)S(1)}, bf16[3072,128]{1,0:T(8,128)(2,1)S(1)}, bf16[3072,128]{1,0:T(8,128)(2,1)S(1)}) custom-call(s32[12]{0:T(128)S(1)} %get-tuple-element.171.low_ref, s32[12]{0:T(128)S(1)} %get-tuple-element.170.high_ref, bf16[3072,768]{1,0:T(8,128)(2,1)} %copy-done.14, bf16[3072,768]{1,0:T(8,128)(2,1)} %copy-done.14, ...), custom_call_target="tpu_custom_call" | custom-call | flops 24159191040 | bytes 9437184 | tf_op jit(solution)/shard_map/pallas_call | solution.py:185
  487.6 1.6 pad_maximum_fusion.2
  489.2 6.5 %collective-permute-done.6 = bf16[4,256,128]{2,1,0:T(8,128)(2,1)S(1)} collective-permute-done((bf16[4,256,128]{2,1,0:T(8,128)(2,1)S(1)}, bf16[4,256,128]{2,1,0:T(8,128)(2,1)S(1)}, u32[]{:S(2)}, u32[]{:S(2)}) %collective-permute-start.6) | collective-permute-done | bytes 262176 | tf_op jit(solution)/shard_map/ppermute | solution.py:1188
  499.2 92.4 %shard_map.295 = (f32[16,256]{1,0:T(8,128)}, bf16[2,384,1024]{2,1,0:T(8,128)(2,1)}, f32[3,256,128]{2,1,0:T(8,128)}, f32[256,512]{1,0:T(8,128)}, f32[512,256]{1,0:T(8,128)}, /*index=5*/f32[128,256]{1,0:T(8,128)}) custom-call(f32[4,16,256]{2,1,0:T(8,128)} %select_maximum_fusion.refs_0_, f32[1,1024]{1,0:T(1,128)} %bitcast.159, ...), custom_call_target="tpu_custom_call" | custom-call | bytes 262144000 | tf_op jit(solution)/shard_map/pallas_call | solution.py:751
  593.1 1.6 fusion.17
  595.9 2.8 copy.110
  (180 shorter events, 21.7 us)
Async XLA Ops:
  7.2 3.3 copy-start.35
  7.2 3.4 copy-start.36
  7.2 3.5 copy-start.37
  7.2 3.5 copy-start.38
  7.2 3.5 copy-start.39
  7.2 3.5 copy-start.40
  7.2 3.5 copy-start.41
  7.3 3.5 copy-start.42
  7.3 3.5 copy-start.43
  7.3 3.5 copy-start.44
  7.3 106.6 %copy-start.26 = (bf16[2,384,1024]{2,1,0:T(8,128)(2,1)S(1)}, bf16[2,384,1024]{2,1,0:T(8,128)(2,1)}, u32[]{:S(2)}) copy-start(bf16[2,384,1024]{2,1,0:T(8,128)(2,1)} %param.19) | copy-start | bytes 4718596
  7.3 247.9 %all-gather.3.cloned.1.call-start = ((), (), s32[]{:S(2)}) async-start(), calls=%async_computation.3 | async-start | bytes 19464192 | tf_op jit(solution)/shard_map/all_gather | solution.py:1139
  115.2 123.8 %collective-permute-start = (bf16[384,1024]{1,0:T(8,128)(2,1)}, bf16[384,1024]{1,0:T(8,128)(2,1)}, u32[]{:S(2)}, u32[]{:S(2)}) collective-permute-start(bf16[384,1024]{1,0:T(8,128)(2,1)} %get-tuple-element.152), channel_id=1, source_target_pairs={{0,0},{2,4},{4,8},{6,12},{8,2},{10,6},{12,10},{14,14},{1,1},{3,5},... | collective-permute-start | bytes 2359304 | tf_op jit(solution)/shard_map/ppermute | solution.py:1164
  122.7 116.3 %collective-permute-start.1 = (bf16[384,1024]{1,0:T(8,128)(2,1)}, bf16[384,1024]{1,0:T(8,128)(2,1)}, u32[]{:S(2)}, u32[]{:S(2)}) collective-permute-start(bf16[384,1024]{1,0:T(8,128)(2,1)} %get-tuple-element.153), channel_id=1, source_target_pairs={{0,4},{2,0},{4,12},{6,8},{8,6},{10,2},{12,14},{14,10},{1,5},{3,1},... | collective-permute-start | bytes 2359304 | tf_op jit(solution)/shard_map/ppermute | solution.py:1164
  126.4 276.2 %copy-start.5 = (s32[3072,1]{1,0:T(8,128)}, s32[3072,1]{1,0:T(8,128)S(1)}, u32[]{:S(2)}) copy-start(s32[3072,1]{1,0:T(8,128)S(1)} %copy.83.idk_ref) | copy-start | bytes 36868
  141.1 114.1 %copy-start.11 = (f32[4,8,256]{2,1,0:T(8,128)}, f32[4,8,256]{2,1,0:T(8,128)S(1)}, u32[]{:S(2)}) copy-start(f32[4,8,256]{2,1,0:T(8,128)S(1)} %get-tuple-element.154) | copy-start | bytes 98308
  141.1 5.1 copy-start.33
  141.1 5.1 copy-start.19
  141.2 5.1 copy-start.45
  146.2 5.4 copy-start.15
  151.6 63.1 %copy-start.14 = (bf16[3072,768]{1,0:T(8,128)(2,1)}, bf16[3072,768]{1,0:T(8,128)(2,1)S(1)}, u32[]{:S(2)}) copy-start(bf16[3072,768]{1,0:T(8,128)(2,1)S(1)} %multiply_convert_fusion.q_ref.k_ref.v_ref) | copy-start | bytes 14155780
  217.1 38.1 %all-to-all-start = ((bf16[4,768,256]{2,1,0:T(8,128)(2,1)}), bf16[4,768,256]{2,1,0:T(8,128)(2,1)S(1)}, u32[]{:S(2)}, u32[]{:S(2)}) async-start(bf16[4,768,256]{2,1,0:T(8,128)(2,1)} %bitcast.139), calls=%async_computation | async-start | bytes 3145728 | tf_op jit(solution)/shard_map/all_to_all | solution.py:1284
  255.2 7.5 %copy-start = (bf16[4,768,256]{2,1,0:T(8,128)(2,1)}, bf16[4,768,256]{2,1,0:T(8,128)(2,1)S(1)}, u32[]{:S(2)}) copy-start(bf16[4,768,256]{2,1,0:T(8,128)(2,1)S(1)} %all-to-all-done.refs_0_.refs_5_) | copy-start | bytes 4718596
  339.1 3.5 copy-start.25
  342.2 4.9 copy-start.18
  343.3 4.8 copy-start.16
  344.5 31.0 %collective-permute-start.3 = (bf16[4,256,512]{2,1,0:T(8,128)(2,1)}, bf16[4,256,512]{2,1,0:T(8,128)(2,1)}, u32[]{:S(2)}, u32[]{:S(2)}) collective-permute-start(bf16[4,256,512]{2,1,0:T(8,128)(2,1)} %dynamic-slice_bitcast_fusion), channel_id=1, source_target_pairs={{0,1},{1,0},{2,3},{3,2},{4,5},{5,4},{6,7},{7,6},{8,9},{9,8},{10,11... | collective-permute-start | bytes 3145736 | tf_op jit(solution)/shard_map/ppermute | solution.py:1188
  348.1 24.6 %collective-permute-start.2 = (bf16[4,256,512]{2,1,0:T(8,128)(2,1)}, bf16[4,256,512]{2,1,0:T(8,128)(2,1)}, u32[]{:S(2)}, u32[]{:S(2)}) collective-permute-start(bf16[4,256,512]{2,1,0:T(8,128)(2,1)} %dynamic-slice_bitcast_fusion.1), channel_id=1, source_target_pairs={{0,16},{16,0},{1,17},{17,1},{2,18},{18,2},{3,19},{19,3},{4,20},{20... | collective-permute-start | bytes 3145736 | tf_op jit(solution)/shard_map/ppermute | solution.py:1188
  363.9 14.1 %collective-permute-start.4 = (bf16[8,2,256,128]{3,2,1,0:T(8,128)(2,1)}, bf16[8,2,256,128]{3,2,1,0:T(8,128)(2,1)}, u32[]{:S(2)}, u32[]{:S(2)}) collective-permute-start(bf16[8,2,256,128]{3,2,1,0:T(8,128)(2,1)} %get-tuple-element.97), channel_id=1, source_target_pairs={{0,8},{8,0},{1,9},{9,1},{2,10},{10,2},{3,11},{11,3},{4,12},{12,4},... | collective-permute-start | bytes 3145736 | tf_op jit(solution)/shard_map/ppermute | solution.py:1213
  364.0 23.6 %all-to-all-start.1 = ((bf16[4,768,256]{2,1,0:T(8,128)(2,1)}), bf16[4,768,256]{2,1,0:T(8,128)(2,1)S(1)}, u32[]{:S(2)}, u32[]{:S(2)}) async-start(bf16[4,768,256]{2,1,0:T(8,128)(2,1)} %get-tuple-element.93), calls=%async_computation.1 | async-start | bytes 3145728 | tf_op jit(solution)/shard_map/all_to_all | solution.py:1297
  370.5 5.1 copy-start.17
  391.3 4.6 copy-start.20
  391.3 105.2 %all-to-all-start.2 = ((bf16[4,2,256,512]{3,2,1,0:T(8,128)(2,1)}), bf16[4,2,256,512]{3,2,1,0:T(8,128)(2,1)}, u32[]{:S(2)}, u32[]{:S(2)}) async-start(bf16[4,2,256,512]{3,2,1,0:T(8,128)(2,1)} %pad_maximum_fusion), calls=%async_computation.2 | async-start | bytes 4194304 | tf_op jit(solution)/shard_map/all_to_all | solution.py:1307
  395.9 6.7 %copy-start.8 = (bf16[3072,256]{1,0:T(8,128)(2,1)S(1)}, bf16[3072,256]{1,0:T(8,128)(2,1)}, u32[]{:S(2)}) copy-start(bf16[3072,256]{1,0:T(8,128)(2,1)} %copy-done.7) | copy-start | bytes 4718596
  395.9 47.9 %collective-permute-start.5 = (bf16[4,2,256,128]{3,2,0,1:T(8,128)(2,1)S(1)}, bf16[4,2,256,128]{3,2,0,1:T(8,128)(2,1)S(1)}, u32[]{:S(2)}, u32[]{:S(2)}) collective-permute-start(bf16[4,2,256,128]{3,2,0,1:T(8,128)(2,1)S(1)} %copy_bitcast_fusion), channel_id=1, source_target_pairs={{0,16},{16,0},{1,17},{17,1},{2,18},{18,2},{3,19},{19,3},{4,20},{20... | collective-permute-start | bytes 1572872 | tf_op jit(solution)/shard_map/ppermute | solution.py:1188
  398.7 88.8 %collective-permute-start.7 = (bf16[384,1024]{1,0:T(8,128)(2,1)S(1)}, bf16[384,1024]{1,0:T(8,128)(2,1)S(1)}, u32[]{:S(2)}, u32[]{:S(2)}) collective-permute-start(bf16[384,1024]{1,0:T(8,128)(2,1)S(1)} %get-tuple-element.148), channel_id=1, source_target_pairs={{0,0},{4,2},{8,4},{12,6},{2,8},{6,10},{10,12},{14,14},{1,1},{5,3},... | collective-permute-start | bytes 2359304 | tf_op jit(solution)/shard_map/ppermute | solution.py:1173
  399.4 88.1 %collective-permute-start.8 = (bf16[384,1024]{1,0:T(8,128)(2,1)S(1)}, bf16[384,1024]{1,0:T(8,128)(2,1)S(1)}, u32[]{:S(2)}, u32[]{:S(2)}) collective-permute-start(bf16[384,1024]{1,0:T(8,128)(2,1)S(1)} %get-tuple-element.149), channel_id=1, source_target_pairs={{4,0},{0,2},{12,4},{8,6},{6,8},{2,10},{14,12},{10,14},{5,1},{1,3},... | collective-permute-start | bytes 2359304 | tf_op jit(solution)/shard_map/ppermute | solution.py:1173
  402.6 41.2 %copy-start.21 = (bf16[8,2,256,128]{3,2,1,0:T(8,128)(2,1)S(1)}, bf16[8,2,256,128]{3,2,1,0:T(8,128)(2,1)}, u32[]{:S(2)}) copy-start(bf16[8,2,256,128]{3,2,1,0:T(8,128)(2,1)} %add_convert_fusion) | copy-start | bytes 3145732
  443.8 43.5 %copy-start.9 = (bf16[3072,128]{1,0:T(8,128)(2,1)}, bf16[3072,128]{1,0:T(8,128)(2,1)S(1)}, u32[]{:S(2)}) copy-start(bf16[3072,128]{1,0:T(8,128)(2,1)S(1)} %get-tuple-element.126.refs_9_) | copy-start | bytes 2359300
  443.8 52.7 %copy-start.1 = (bf16[3072,128]{1,0:T(8,128)(2,1)}, bf16[3072,128]{1,0:T(8,128)(2,1)S(1)}, u32[]{:S(2)}) copy-start(bf16[3072,128]{1,0:T(8,128)(2,1)S(1)} %get-tuple-element.119.refs_8_) | copy-start | bytes 2359300
  443.8 53.5 %copy-start.2 = (bf16[3072,128]{1,0:T(8,128)(2,1)}, bf16[3072,128]{1,0:T(8,128)(2,1)S(1)}, u32[]{:S(2)}) copy-start(bf16[3072,128]{1,0:T(8,128)(2,1)S(1)} %get-tuple-element.121.refs_10_) | copy-start | bytes 2359300
  487.2 9.6 %copy-start.3 = (bf16[3072,128]{1,0:T(8,128)(2,1)}, bf16[3072,128]{1,0:T(8,128)(2,1)S(1)}, u32[]{:S(2)}) copy-start(bf16[3072,128]{1,0:T(8,128)(2,1)S(1)} %get-tuple-element.120.refs_11_) | copy-start | bytes 2359300
  487.3 10.5 %copy-start.4 = (bf16[3072,128]{1,0:T(8,128)(2,1)}, bf16[3072,128]{1,0:T(8,128)(2,1)S(1)}, u32[]{:S(2)}) copy-start(bf16[3072,128]{1,0:T(8,128)(2,1)S(1)} %get-tuple-element.122.refs_13_) | copy-start | bytes 2359300
  487.3 8.4 %collective-permute-start.6 = (bf16[4,256,128]{2,1,0:T(8,128)(2,1)S(1)}, bf16[4,256,128]{2,1,0:T(8,128)(2,1)S(1)}, u32[]{:S(2)}, u32[]{:S(2)}) collective-permute-start(bf16[4,256,128]{2,1,0:T(8,128)(2,1)S(1)} %dynamic-slice_bitcast_fusion.6), channel_id=1, source_target_pairs={{0,1},{1,0},{2,3},{3,2},{4,5},{5,4},{6,7},{7,6},{8,9},{9,8},{10,11... | collective-permute-start | bytes 786440 | tf_op jit(solution)/shard_map/ppermute | solution.py:1188
  591.7 7.0 %copy-start.30 = (f32[3,256,128]{2,1,0:T(8,128)S(1)}, f32[3,256,128]{2,1,0:T(8,128)}, u32[]{:S(2)}) copy-start(f32[3,256,128]{2,1,0:T(8,128)} %get-tuple-element.192) | copy-start | bytes 1179652
  591.7 7.7 %copy-start.31 = (f32[128,256]{1,0:T(8,128)S(1)}, f32[128,256]{1,0:T(8,128)}, u32[]{:S(2)}) copy-start(f32[128,256]{1,0:T(8,128)} %get-tuple-element.194) | copy-start | bytes 393220
  595.9 4.2 copy-start.29
  595.9 5.0 copy-start.28
  (11 other events, 22.6 us)
Sparse Core Ops, SparseCore 0:
  11.0 194.8 all-gather.2
